TPU v7x, 256 devices: a whole 4x4x8 slice. The times are simulated.
256 devices in a mesh: grp: 32 (over z_hi, y, x), tp: 8 (over z_lo, core).
Axes of the slice: x: 4, y: 4, z: 8 (z_hi: 2, z_lo: 4; z = z_hi * 4 + z_lo), core: 2. Of those that a mesh axis runs over, the one named last changes fastest.
Arguments:
- tokens: bfloat16 [512, 16384], P('grp', 'tp'), may hold values from -54 to 54
- queries: bfloat16 [512, 8192], P('grp', 'tp'), may hold values from -5 to 5
- new_key: bfloat16 [512, 1024], P('grp', 'tp'), may hold values from -5 to 5
- new_value: bfloat16 [512, 1024], P('grp', 'tp'), may hold values from -4 to 4
- key_cache: bfloat16 [512, 48, 1024], P('grp', None, 'tp'), may hold values from -5 to 5
- value_cache: bfloat16 [512, 48, 1024], P('grp', None, 'tp'), may hold values from -4 to 4
- lengths: int32 [512], P('grp'), may hold values from 1 to 48
- group_of: int32 [512], replicated, may hold values from 0 to 31, as said below
- out_weight: bfloat16 [8192, 16384], P('tp', 'grp'), may hold values from -0.0625 to 0.0625
- norm_gain: bfloat16 [16384], P('tp'), may hold values from 0.5 to 1.5
- gate_weight: bfloat16 [16384, 26624], P('tp', 'grp'), may hold values from -0.046875 to 0.046875
- up_weight: bfloat16 [16384, 26624], P('tp', 'grp'), may hold values from -0.046875 to 0.046875
- down_weight: bfloat16 [26624, 16384], P('grp', 'tp'), may hold values from -0.0390625 to 0.0390625
Outputs:
- layer_out: bfloat16 [512, 16384], P('grp', 'tp')
Inputs may be any that keep to these rules, and one draw needn't show every extreme that they name: `group_of`: the 16 rows of one device name any group at most 2 times and some group exactly 2 times; every group is named by exactly 16 rows.
All inputs are finite; a program needn't handle non-finite values.
Results may differ from a plain program's by a relative error of at most 0.012.
Values may be sent and summed in bfloat16 or wider, within the bound.
No kernel may reach another device: no remote copies, remote signals or barrier semaphores. Data moves between devices by JAX's collectives and lax.ppermute only.
A program may use at most 64 MiB of HBM per device.

v0:
```python
import math

import jax
import jax.numpy as jnp
from jax import lax
from jax.sharding import PartitionSpec as P

D = 16384
HD = 128


def row_layout(group_of, groups, rows_dev):
    blocks = group_of.reshape(groups, rows_dev)
    group_ids = jnp.arange(groups, dtype=jnp.int32)
    matches = (blocks[:, :, None] == group_ids[None, None, :]).astype(jnp.int32)
    counts = jnp.sum(matches, axis=1)
    before = jnp.cumsum(counts, axis=0) - counts
    inner_rank = jnp.cumsum(matches, axis=1) - matches
    row_rank = jnp.sum(inner_rank * matches, axis=2)
    offsets = jnp.sum(before[:, None, :] * matches, axis=2)
    position = blocks * rows_dev + offsets + row_rank
    return (blocks, row_rank, counts, before, position)


def shards(
    tokens,
    queries,
    new_key,
    new_value,
    key_cache,
    value_cache,
    lengths,
    group_of,
    out_weight,
    norm_gain,
    gate_weight,
    up_weight,
    down_weight,
):
    groups = lax.axis_size("grp")
    rows_dev = tokens.shape[0]
    total_rows = group_of.shape[0]
    q_cols = queries.shape[1]
    kv_cols = new_key.shape[1]
    kv_local = kv_cols // HD
    per_kv = q_cols // kv_cols
    capacity = max(2, -(-rows_dev // groups))
    own_group = lax.axis_index("grp")
    blocks, row_rank, counts, before, position = row_layout(group_of, groups, rows_dev)
    group_ids = jnp.arange(groups, dtype=jnp.int32)
    slot_ids = jnp.arange(capacity, dtype=jnp.int32)
    my_targets = lax.dynamic_index_in_dim(blocks, own_group, 0, keepdims=False)
    my_ranks = lax.dynamic_index_in_dim(row_rank, own_group, 0, keepdims=False)
    selector = (
        (my_targets[None, None, :] == group_ids[:, None, None])
        & (my_ranks[None, None, :] == slot_ids[None, :, None])
    ).astype(jnp.bfloat16)
    packed = jnp.concatenate([queries, new_key, new_value], axis=1)
    bucket = jnp.einsum("dcj,jf->dcf", selector, packed, preferred_element_type=jnp.float32).astype(
        jnp.bfloat16
    )
    received = lax.all_to_all(bucket, "grp", split_axis=0, concat_axis=0, tiled=True)
    from_counts = lax.dynamic_index_in_dim(counts, own_group, 1, keepdims=False)
    from_before = lax.dynamic_index_in_dim(before, own_group, 1, keepdims=False)
    slot_place = from_before[:, None] + slot_ids[None, :]
    filled = slot_ids[None, :] < from_counts[:, None]
    row_ids = jnp.arange(rows_dev, dtype=jnp.int32)
    compact = ((slot_place[None, :, :] == row_ids[:, None, None]) & filled[None, :, :]).astype(
        jnp.bfloat16
    )
    arrived = jnp.einsum(
        "psc,scf->pf", compact, received, preferred_element_type=jnp.float32
    ).astype(jnp.bfloat16)
    query_view = arrived[:, :q_cols].reshape(rows_dev, kv_local, per_kv, HD)
    key_new = arrived[:, q_cols : q_cols + kv_cols].reshape(rows_dev, kv_local, HD)
    value_new = arrived[:, q_cols + kv_cols :].reshape(rows_dev, kv_local, HD)
    cache_len = key_cache.shape[1]
    key_view = key_cache.reshape(rows_dev, cache_len, kv_local, HD)
    value_view = value_cache.reshape(rows_dev, cache_len, kv_local, HD)
    qk_scale = 1.0 / math.sqrt(HD)
    scores = (
        jnp.einsum("rkjd,rlkd->rkjl", query_view, key_view, preferred_element_type=jnp.float32)
        * qk_scale
    )
    own_score = (
        jnp.einsum("rkjd,rkd->rkj", query_view, key_new, preferred_element_type=jnp.float32)
        * qk_scale
    )
    live_mask = (jnp.arange(cache_len, dtype=jnp.int32)[None, :] < lengths[:, None])[
        :, None, None, :
    ]
    masked = jnp.where(live_mask, scores, -1e30)
    row_top = jnp.maximum(jnp.max(masked, axis=3), own_score)
    exp_live = jnp.exp(masked - row_top[..., None])
    exp_own = jnp.exp(own_score - row_top)
    totals = jnp.sum(exp_live, axis=3) + exp_own
    weights = (exp_live / totals[..., None]).astype(jnp.bfloat16)
    own_weight = (exp_own / totals).astype(jnp.bfloat16).astype(jnp.float32)
    head_out = jnp.einsum(
        "rkjl,rlkd->rkjd", weights, value_view, preferred_element_type=jnp.float32
    )
    head_out = head_out + own_weight[..., None] * value_new.astype(jnp.float32)[:, :, None, :]
    head_out = head_out.astype(jnp.bfloat16).reshape(rows_dev, q_cols)
    projected = jnp.dot(
        lax.all_gather(head_out, "grp", axis=0, tiled=True),
        out_weight,
        preferred_element_type=jnp.float32,
    )
    batch_rows = jnp.take(projected, position.reshape(total_rows), axis=0)
    exchanged = lax.all_to_all(batch_rows, "grp", split_axis=0, concat_axis=1, tiled=True)
    attn_out = lax.psum_scatter(exchanged, "tp", scatter_dimension=1, tiled=True).astype(
        jnp.bfloat16
    )
    residual = (tokens.astype(jnp.float32) + attn_out.astype(jnp.float32)).astype(jnp.bfloat16)
    wide = residual.astype(jnp.float32)
    squares = lax.psum(jnp.sum(wide * wide, axis=1), "tp")
    normed = wide * lax.rsqrt(squares / D + 1e-05)[:, None] * norm_gain.astype(jnp.float32)[None, :]
    normed = normed.astype(jnp.bfloat16)
    part_rows = lax.all_gather(normed, "grp", axis=0, tiled=True)
    gate_part = jnp.dot(part_rows, gate_weight, preferred_element_type=jnp.float32)
    up_part = jnp.dot(part_rows, up_weight, preferred_element_type=jnp.float32)
    gate_up = jnp.stack([gate_part, up_part], axis=1)
    summed = lax.psum(gate_up, "tp")
    hidden = (jax.nn.silu(summed[:, 0]) * summed[:, 1]).astype(jnp.bfloat16)
    ffn_out = lax.psum_scatter(
        jnp.dot(hidden, down_weight, preferred_element_type=jnp.float32).astype(jnp.bfloat16),
        "grp",
        scatter_dimension=0,
        tiled=True,
    ).astype(jnp.float32)
    return (wide + ffn_out).astype(jnp.bfloat16)


def solution(mesh):
    in_specs = (
        P("grp", "tp"),
        P("grp", "tp"),
        P("grp", "tp"),
        P("grp", "tp"),
        P("grp", None, "tp"),
        P("grp", None, "tp"),
        P("grp"),
        P(),
        P("tp", "grp"),
        P("tp"),
        P("tp", "grp"),
        P("tp", "grp"),
        P("grp", "tp"),
    )
    out_specs = P("grp", "tp")
    return jax.shard_map(shards, mesh=mesh, in_specs=in_specs, out_specs=out_specs, check_vma=False)
```

profile of v0, /device:TPU:32, one launch (start us, length us, event | category | flops | bytes accessed | tf_op | source)
XLA Modules:
  0.0 642.2 jit_solution(12824562580208945989)
XLA Ops:
  6.5 0.0 copy-start
  6.5 0.0 copy-start.2
  6.5 0.9 eq.66
  7.5 0.1 copy.25
  7.5 0.1 iota_compare_fusion.3
  7.6 0.6 fusion.36
  8.2 0.2 dynamic-slice_reduce_fusion.2
  8.4 1.1 convolution_convert_fusion.1
  9.5 0.8 copy.28
  10.3 13.2 %all-to-all-start = ((bf16[32,2,1280]{2,1,0:T(2,128)(2,1)}), bf16[32,2,1280]{2,1,0:T(2,128)(2,1)}, u32[]{:S(2)}, u32[]{:S(2)}) async-start(bf16[32,2,1280]{2,1,0:T(2,128)(2,1)} %copy.28), calls=%async_computation | async-start | bytes 327680 | tf_op jit(solution)/shard_map/all_to_all | solution.py:62
  23.5 0.0 all-gather.3.cloned.1.call-start
  23.5 0.1 convert_reduce_fusion
  23.7 0.1 reduce_window_sum.22
  23.7 0.2 dynamic-slice_reduce_fusion
  24.0 0.7 iota_compare_fusion.4
  24.7 11.8 %all-to-all-done = bf16[32,2,1280]{2,1,0:T(2,128)(2,1)} async-done(((bf16[32,2,1280]{2,1,0:T(2,128)(2,1)}), bf16[32,2,1280]{2,1,0:T(2,128)(2,1)}, u32[]{:S(2)}, u32[]{:S(2)}) %all-to-all-start) | async-done | bytes 163872 | tf_op jit(solution)/shard_map/all_to_all | solution.py:62
  36.4 1.1 fusion
  37.6 0.1 fusion.26
  37.7 1.2 fusion.37
  39.0 0.2 fusion.15
  39.2 1.2 fusion.5
  40.3 0.6 copy.41
  41.0 0.0 all-gather.3.cloned.1.call-update
  41.0 0.0 reduce-scatter.3.cloned.1.call-start
  41.0 0.1 copy.27
  41.1 0.1 reduce_sum.53
  41.2 0.5 select_reduce_fusion
  41.7 0.1 copy.26
  41.7 0.1 reduce_sum.51
  41.8 0.0 copy-done.2
  41.8 0.1 broadcast_in_dim.19
  41.9 74.5 %all-gather.3.cloned.1.call-done = bf16[512,1024]{1,0:T(8,128)(2,1)} async-done(((bf16[16,1024]{1,0:T(8,128)(2,1)}), bf16[512,1024]{1,0:T(8,128)(2,1)}) %all-gather.3.cloned.1.call-update) | async-done | bytes 1048592 | tf_op jit(solution)/shard_map/all_gather | solution.py:105
  116.4 3.2 fusion.38
  119.7 4.0 gather_fusion
  123.6 1.4 broadcast_select_fusion
  125.0 34.8 %all_to_all.21 = f32[32,16,512]{2,1,0:T(8,128)S(1)} all-to-all(f32[32,16,512]{2,1,0:T(8,128)S(1)} %broadcast_select_fusion), channel_id=1, replica_groups=mesh['grp'=32,'tp'=8] {'grp'}, dimensions={0} | all-to-all | bytes 2097152 | tf_op jit(solution)/shard_map/all_to_all | solution.py:110
  159.8 0.0 copy-start.3
  159.8 0.0 copy-start.1
  159.8 1.1 copy.33
  160.9 0.0 reduce-scatter.3.cloned.1.call-update
  160.9 0.0 all-gather.5.cloned.1.call-start
  160.9 0.0 copy-done.3
  161.0 29.7 %reduce-scatter.3.cloned.1.call-done = f32[16,2048]{1,0:T(8,128)} async-done(((f32[16,16384]{1,0:T(8,128)}), f32[16,2048]{1,0:T(8,128)}) %reduce-scatter.3.cloned.1.call-update) | async-done | bytes 131088 | tf_op jit(solution)/shard_map/reduce_scatter | solution.py:111
  190.6 0.0 copy-done.1
  190.6 1.0 fusion.10
  191.7 14.6 %psum.14 = f32[16]{0:T(128)S(1)} all-reduce(f32[16]{0:T(128)S(1)} %get-tuple-element.5), channel_id=1, replica_groups=mesh['grp'=32,'tp'=8] {'tp'}, use_global_device_ids=true, to_apply=%region_9.10 | all-reduce | flops 16 | bytes 128 | tf_op jit(solution)/shard_map/psum | solution.py:116
  206.3 0.7 fusion.12
  207.0 0.0 all-gather.5.cloned.1.call-update
  207.0 0.0 all-reduce.2.cloned.1.call-start
  207.1 95.6 %all-gather.5.cloned.1.call-done = bf16[512,2048]{1,0:T(8,128)(2,1)} async-done(((bf16[16,2048]{1,0:T(8,128)(2,1)}), bf16[512,2048]{1,0:T(8,128)(2,1)}) %all-gather.5.cloned.1.call-update) | async-done | bytes 2097168 | tf_op jit(solution)/shard_map/all_gather | solution.py:119
  302.7 0.0 copy-start.4
  302.7 4.7 convolution_bitcast_fusion.1
  307.4 0.0 copy-done.4
  307.4 0.0 copy-done.5
  307.4 2.0 convolution_bitcast_fusion.2
  309.4 2.1 pad_maximum_fusion
  311.5 0.0 all-reduce.2.cloned.1.call-update
  311.5 0.0 reduce-scatter.5.cloned.1.call-start
  311.5 85.7 %all-reduce.2.cloned.1.call-done = f32[512,2,832]{0,2,1:T(8,128)} async-done(((f32[512,2,832]{0,2,1:T(8,128)}), f32[512,2,832]{0,2,1:T(8,128)}) %all-reduce.2.cloned.1.call-update) | async-done | bytes 3407888 | tf_op jit(solution)/shard_map/psum | solution.py:123
  397.3 0.0 copy-done
  397.3 5.8 convolution_convert_fusion
  403.1 0.0 reduce-scatter.5.cloned.1.call-update
  403.1 231.1 %reduce-scatter.5.cloned.1.call-done = bf16[16,2048]{1,0:T(8,128)(2,1)} async-done(((bf16[512,2048]{1,0:T(8,128)(2,1)}), bf16[16,2048]{1,0:T(8,128)(2,1)}) %reduce-scatter.5.cloned.1.call-update) | async-done | bytes 65552 | tf_op jit(solution)/shard_map/reduce_scatter | solution.py:125
  634.2 1.5 fusion.13
  (15 shorter events, 0.1 us)
Async XLA Ops:
  6.5 390.7 %copy-start = (bf16[832,2048]{1,0:T(8,128)(2,1)S(1)}, bf16[832,2048]{1,0:T(8,128)(2,1)}, u32[]{:S(2)}) copy-start(bf16[832,2048]{1,0:T(8,128)(2,1)} %param.25) | copy-start | bytes 10223620
  6.5 35.3 %copy-start.2 = (s32[512]{0:T(512)S(1)}, s32[512]{0:T(512)}, u32[]{:S(2)}) copy-start(s32[512]{0:T(512)} %param.20) | copy-start | bytes 6148
  10.3 26.1 %all-to-all-start = ((bf16[32,2,1280]{2,1,0:T(2,128)(2,1)}), bf16[32,2,1280]{2,1,0:T(2,128)(2,1)}, u32[]{:S(2)}, u32[]{:S(2)}) async-start(bf16[32,2,1280]{2,1,0:T(2,128)(2,1)} %copy.28), calls=%async_computation | async-start | bytes 327680 | tf_op jit(solution)/shard_map/all_to_all | solution.py:62
  23.5 92.9 %all-gather.3.cloned.1.call-start = ((), (), s32[]{:S(2)}) async-start(), calls=%async_computation.4 | async-start | bytes 1081344 | tf_op jit(solution)/shard_map/all_gather | solution.py:105
  41.0 149.7 %reduce-scatter.3.cloned.1.call-start = ((), (), s32[]{:S(2)}) async-start(), calls=%async_computation.5 | async-start | bytes 1179648 | tf_op jit(solution)/shard_map/reduce_scatter | solution.py:111
  159.8 1.2 copy-start.3
  159.8 30.9 %copy-start.1 = (bf16[16,2048]{1,0:T(8,128)(2,1)S(1)}, bf16[16,2048]{1,0:T(8,128)(2,1)}, u32[]{:S(2)}) copy-start(bf16[16,2048]{1,0:T(8,128)(2,1)} %param.13) | copy-start | bytes 196612
  160.9 141.8 %all-gather.5.cloned.1.call-start = ((), (), s32[]{:S(2)}) async-start(), calls=%async_computation.6 | async-start | bytes 2162688 | tf_op jit(solution)/shard_map/all_gather | solution.py:119
  207.0 190.2 %all-reduce.2.cloned.1.call-start = ((), (), s32[]{:S(2)}) async-start(), calls=%async_computation.7 | async-start | bytes 6815744 | tf_op jit(solution)/shard_map/psum | solution.py:123
  302.7 4.7 copy-start.4
  302.7 4.7 copy-start.5
  311.5 322.7 %reduce-scatter.5.cloned.1.call-start = ((), (), s32[]{:S(2)}) async-start(), calls=%async_computation.8 | async-start | bytes 2162688 | tf_op jit(solution)/shard_map/reduce_scatter | solution.py:125
Sparse Core Ops, SparseCore 0:
  41.1 75.2 all-gather.2
  161.0 29.5 reduce-scatter.2
  207.2 95.4 all-gather.4
  311.6 85.6 all-reduce.1
  403.2 230.9 reduce-scatter.4
where the time goes:
time: 643 us; the launch traced here: 642 us
  waiting for transfers between devices  528 us (82%)
  blocking collectives  49.4 us (8%)
  matrix products  20.4 us (3%)
  starting transfers between devices  13.4 us (2%)
  between operations  13.3 us (2%)
  other arithmetic  9.01 us (1%)
  local copies, waits for them, and re-layouts  8.29 us (1%)
    reduce_scatter x1, waiting for transfers between devices, shards(): lax.psum_scatter(jnp.dot(hidden, down_weight, preferred_element_type=jnp....  231 us
    all_gather x1, waiting for transfers between devices, shards(): part_rows = lax.all_gather(normed, 'grp', axis=0, tiled=True)  95.6 us
    psum x1, waiting for transfers between devices, shards(): summed = lax.psum(gate_up, 'tp')  85.7 us
    all_gather x1, waiting for transfers between devices, shards(): lax.all_gather(head_out, 'grp', axis=0, tiled=True)  74.5 us
    all_to_all x1, blocking collectives, shards(): lax.all_to_all(batch_rows, 'grp', split_axis=0, concat_axis=1, tiled=True)  34.8 us
    reduce_scatter x1, waiting for transfers between devices, shards(): lax.psum_scatter(exchanged, 'tp', scatter_dimension=1, tiled=True)  29.7 us
    psum x1, blocking collectives, shards(): squares = lax.psum(jnp.sum(wide * wide, axis=1), 'tp')  14.6 us
    all_to_all x1, starting transfers between devices, shards(): lax.all_to_all(bucket, 'grp', split_axis=0, concat_axis=0, tiled=True)  13.2 us
  transfers between devices with their start and end apart: 6, of which 6 were waited for; matrix products, arithmetic and copies ran while one was open for 0% of the time, Pallas kernels for 0%

commit v1 on v0

v1 whole, which is shorter than its diff:
```python
import functools
import math

import jax
import jax.numpy as jnp
import numpy as np
from jax import lax
from jax.experimental import pallas as pl
from jax.experimental.pallas import tpu as pltpu
from jax.sharding import Mesh
from jax.sharding import PartitionSpec as P

D = 16384
HD = 128
AXES = ("z_hi", "y", "x", "z_lo", "core")
SIZES = (2, 4, 4, 4, 2)
GRP = ("z_hi", "y", "x")
TP = ("z_lo", "core")
YX = ("y", "x")
BF = jnp.bfloat16
F32 = jnp.float32
MIB = 1 << 20
PAD = 896


def flat(z_hi, y, x, z_lo, core):
    return (((z_hi * 4 + y) * 4 + x) * 4 + z_lo) * 2 + core


def spread_pairs(flip):
    pairs = []
    for z_hi in range(2):
        for y in range(4):
            for x in range(4):
                for z_lo in range(4):
                    for core in range(2):
                        src = flat(z_hi, y, x, z_lo, core)
                        dst = flat(core ^ flip, z_lo, x, 2 * z_hi + y // 2, y % 2)
                        pairs.append((src, dst))
    return pairs


def swap(v, axis):
    return lax.ppermute(v, axis, [(0, 1), (1, 0)])


def pick(v, index):
    return lax.dynamic_index_in_dim(v, index, 0, keepdims=False)


def spread(v, axes, count):
    copies = jnp.broadcast_to(v[None], (count,) + v.shape)
    return lax.all_to_all(copies, axes, split_axis=0, concat_axis=0, tiled=True)


def call(body, out_shape, *operands, scalars=(), scratch=(), limit=24, flops=0, moved=0):
    whole = pl.BlockSpec(memory_space=pltpu.VMEM)
    single = not isinstance(out_shape, (list, tuple))
    specs = [pl.BlockSpec(memory_space=pltpu.SMEM)] * len(scalars) + [whole] * len(operands)
    return pl.pallas_call(
        body,
        out_shape=out_shape,
        in_specs=specs,
        out_specs=whole if single else [whole] * len(out_shape),
        scratch_shapes=list(scratch),
        compiler_params=pltpu.CompilerParams(vmem_limit_bytes=limit * MIB),
        cost_estimate=pl.CostEstimate(flops=flops, bytes_accessed=moved, transcendentals=0),
    )(*[jnp.reshape(s, (1,)).astype(jnp.int32) for s in scalars], *operands)


def shape(dims, dtype):
    return jax.ShapeDtypeStruct(dims, dtype)


def dot(a, b):
    return jnp.dot(a, b, preferred_element_type=F32)


def attend_body(rows, cache_len, heads, slot_ref, got_ref, key_ref, value_ref, len_ref, out_ref):
    slots = lax.broadcasted_iota(jnp.int32, (rows, got_ref.shape[0]), 1)
    compact = (slot_ref[...] == slots).astype(F32).astype(BF)
    arrived = dot(compact, got_ref[...])
    q_cols = heads * HD
    rounded = arrived[:, :q_cols].astype(BF)
    tall = jnp.concatenate([rounded[:, j * HD : (j + 1) * HD] for j in range(heads)], axis=0)
    key_new = jnp.concatenate([arrived[:, q_cols : q_cols + HD]] * heads, axis=0)
    value_new = jnp.concatenate([arrived[:, q_cols + HD :]] * heads, axis=0)
    scale = 1.0 / math.sqrt(HD)
    scores = lax.dot_general(tall, key_ref[...], (((1,), (1,)), ((), ())), preferred_element_type=F32) * scale
    own = jnp.sum(tall.astype(F32) * key_new, axis=1, keepdims=True) * scale
    spot = lax.broadcasted_iota(jnp.int32, scores.shape, 1)
    row = lax.rem(lax.broadcasted_iota(jnp.int32, scores.shape, 0), rows)
    start = row * cache_len
    lens = jnp.concatenate([len_ref[...]] * heads, axis=0)
    live = (spot >= start) & (spot < start + lens)
    masked = jnp.where(live, scores, -1e30)
    top = jnp.maximum(jnp.max(masked, axis=1, keepdims=True), own)
    exp_live = jnp.where(live, jnp.exp(masked - top), 0.0)
    exp_own = jnp.exp(own - top)
    total = jnp.sum(exp_live, axis=1, keepdims=True) + exp_own
    weights = (exp_live / total).astype(BF)
    own_weight = (exp_own / total).astype(BF).astype(F32)
    out = (dot(weights, value_ref[...]) + own_weight * value_new).astype(BF)
    for j in range(heads):
        out_ref[:, j * HD : (j + 1) * HD] = out[j * rows : (j + 1) * rows]


def project_body(send_pos, keep_pos, heads_ref, weight_ref, send_ref, keep_ref):
    product = dot(heads_ref[...], weight_ref[...]).astype(BF)
    for pos, out in ((send_pos, send_ref), (keep_pos, keep_ref)):
        spot = lax.broadcasted_iota(jnp.int32, (pos.shape[0], product.shape[0]), 1)
        unsort = (pos[...] == spot).astype(F32).astype(BF)
        out[...] = dot(unsort, product).astype(BF)


def split_body(z_lo, keep_ref, got_ref, own_ref, one_ref, two_ref, three_ref):
    rows = own_ref.shape[0]
    for step, out in enumerate((own_ref, one_ref, two_ref, three_ref)):
        at = pl.ds(pl.multiple_of((z_lo[0] ^ step) * rows, rows), rows)
        out[...] = (keep_ref[at, :].astype(F32) + got_ref[at, :].astype(F32)).astype(out.dtype)


def line_reduce(keep, got, z_lo):
    rows, cols = keep.shape[0] // 4, keep.shape[1]
    outs = [shape((rows, cols), F32)] + [shape((rows, cols), BF)] * 3
    own, *pieces = call(split_body, outs, keep, got, scalars=(z_lo,))
    return [own] + [
        lax.ppermute(piece, "z_lo", [(i, i ^ step) for i in range(4)])
        for step, piece in zip((1, 2, 3), pieces)
    ]


def gate_up_body(core, rows_ref, gain_ref, gate_ref, up_ref, send_ref, keep_ref, total):
    planes, blocks, count, cols = rows_ref.shape
    hid = gate_ref.shape[1]
    rows = planes * count
    squares = jnp.zeros((rows, 1), F32)
    parts = []
    for b in range(blocks):
        wide = rows_ref[:, b].reshape(rows, cols).astype(F32)
        squares += jnp.sum(wide * wide, axis=1, keepdims=True)
        parts.append((wide * gain_ref[:, b * cols : (b + 1) * cols].astype(F32)).astype(BF))
    scaled = jnp.concatenate(parts, axis=1)
    total[:, :hid] = dot(scaled, gate_ref[...])
    total[:, PAD : PAD + hid] = dot(scaled, up_ref[...])
    high = squares.astype(BF).astype(F32)
    lane = lax.broadcasted_iota(jnp.int32, (rows, PAD - hid), 1)
    total[:, hid:PAD] = jnp.where(lane == 0, high, jnp.where(lane == 1, squares - high, 0.0))
    half = rows // 2
    send_ref[...] = total[pl.ds(pl.multiple_of((1 - core[0]) * half, half), half), :].astype(BF)
    keep_ref[...] = total[pl.ds(pl.multiple_of(core[0] * half, half), half), :]


def hidden_body(own_ref, one_ref, two_ref, three_ref, out_ref):
    hid = out_ref.shape[1]
    sums = own_ref[...] + one_ref[...].astype(F32) + two_ref[...].astype(F32) + three_ref[...].astype(F32)
    mean_square = (sums[:, hid : hid + 1] + sums[:, hid + 1 : hid + 2]) / D
    inv = lax.rsqrt(mean_square + 1e-05)
    gate = sums[:, :hid] * inv
    up = sums[:, PAD : PAD + hid] * inv
    out_ref[...] = (gate / (1.0 + jnp.exp(-gate)) * up).astype(BF)


def join_body(z_lo, own_ref, one_ref, two_ref, three_ref, out_ref):
    rows = own_ref.shape[0]
    for step, piece in enumerate((own_ref, one_ref, two_ref, three_ref)):
        out_ref[pl.ds(pl.multiple_of((z_lo[0] ^ step) * rows, rows), rows), :] = piece[...]


def down_body(core, own_ref, other_ref, weight_ref, out_ref):
    half = own_ref.shape[0]
    out_ref[pl.ds(pl.multiple_of(core[0] * half, half), half), :] = dot(own_ref[...], weight_ref[...]).astype(BF)
    out_ref[pl.ds(pl.multiple_of((1 - core[0]) * half, half), half), :] = dot(
        other_ref[...], weight_ref[...]
    ).astype(BF)


def feed_forward(gathered, gain, gate_weight, up_weight, down_weight, core, z_lo):
    rows = gathered.shape[0] * gathered.shape[2]
    hid, width = down_weight.shape
    cols = PAD + hid
    outs = [shape((rows // 2, cols), BF), shape((rows // 2, cols), F32)]
    send, keep = call(
        gate_up_body, outs, gathered, gain, gate_weight, up_weight,
        scalars=(core,), scratch=[pltpu.VMEM((rows, cols), F32)], limit=32, flops=4 * rows * width * hid,
    )
    pieces = line_reduce(keep, swap(send, "core"), z_lo)
    hidden = call(hidden_body, shape((rows // 8, hid), BF), *pieces)
    others = [lax.ppermute(hidden, "z_lo", [(i, i ^ step) for i in range(4)]) for step in (1, 2, 3)]
    half = call(join_body, shape((rows // 2, hid), BF), hidden, *others, scalars=(z_lo,))
    down = call(
        down_body, shape((rows, width), BF), half, swap(half, "core"), down_weight,
        scalars=(core,), flops=2 * rows * width * hid,
    )
    return lax.all_to_all(down.reshape(16, rows // 16, width), YX, split_axis=0, concat_axis=0, tiled=True)


def shards(
    tokens,
    queries,
    new_key,
    new_value,
    key_cache,
    value_cache,
    lengths,
    group_of,
    out_weight,
    norm_gain,
    gate_weight,
    up_weight,
    down_weight,
):
    groups = 32
    rows_dev, width = tokens.shape
    rows = group_of.shape[0]
    q_cols = queries.shape[1]
    cache_len = key_cache.shape[1]
    capacity = 2
    quarter = width // 4
    own_group = lax.axis_index(GRP)
    z_lo = lax.axis_index("z_lo")
    core = lax.axis_index("core")
    place_y = lax.axis_index("y")
    place_x = lax.axis_index("x")

    blocks = group_of.reshape(groups, rows_dev)
    mine = pick(blocks, own_group)
    earlier = jnp.arange(rows_dev)[:, None] > jnp.arange(rows_dev)[None, :]
    my_ranks = jnp.sum((mine[:, None] == mine[None, :]) & earlier, axis=1, dtype=jnp.int32)
    my_slots = mine * capacity + my_ranks
    selector = (jnp.arange(groups * capacity, dtype=jnp.int32)[:, None] == my_slots[None, :]).astype(BF)
    packed = jnp.concatenate([queries, new_key, new_value], axis=1)
    bucket = dot(selector, packed).astype(BF).reshape(groups, capacity, packed.shape[1])
    bucket, tokens_in = lax.optimization_barrier((bucket, tokens))
    received = lax.all_to_all(bucket, GRP, split_axis=0, concat_axis=0, tiled=True)

    flat_groups = group_of.reshape(rows)
    same = flat_groups[:, None] == flat_groups[None, :]
    index = jnp.arange(rows, dtype=jnp.int32)
    ahead = jnp.sum(same & (index[:, None] > index[None, :]), axis=1, dtype=jnp.int32)
    position = flat_groups * rows_dev + ahead
    halves = position.reshape(2, rows // 2, 1)
    in_block = index // rows_dev
    block_rank = jnp.sum(
        same & (index[:, None] > index[None, :]) & (in_block[:, None] == in_block[None, :]), axis=1, dtype=jnp.int32
    )
    slot_of = in_block * capacity + block_rank
    wanted = own_group * rows_dev + jnp.arange(rows_dev, dtype=jnp.int32)
    arrival = jnp.sum(
        jnp.where(position[None, :] == wanted[:, None], slot_of[None, :], 0), axis=1, keepdims=True, dtype=jnp.int32
    )

    tok = tokens_in.reshape(rows_dev, 4, quarter).transpose(1, 0, 2)
    tok = lax.all_to_all(tok, "x", split_axis=0, concat_axis=0, tiled=True)
    tok = lax.ppermute(tok.reshape(4 * rows_dev, quarter), AXES, [(b, a) for a, b in spread_pairs(0)])
    received, tok, arrival, halves = lax.optimization_barrier((received, tok, arrival, halves))

    heads = call(
        functools.partial(attend_body, rows_dev, cache_len, q_cols // HD),
        shape((rows_dev, q_cols), BF),
        arrival,
        received.reshape(groups * capacity, packed.shape[1]),
        key_cache.reshape(rows_dev * cache_len, HD),
        value_cache.reshape(rows_dev * cache_len, HD),
        lengths.reshape(rows_dev, 1),
    )
    heads = spread(heads, GRP, groups).reshape(rows, q_cols)
    outs = [shape((rows // 2, out_weight.shape[1]), BF)] * 2
    send, keep = call(
        project_body, outs, pick(halves, 1 - core), pick(halves, core), heads, out_weight,
        flops=4 * rows * q_cols * out_weight.shape[1],
    )
    own, one, two, three = line_reduce(keep, swap(send, "core"), z_lo)
    attn_out = (own + one.astype(F32) + two.astype(F32) + three.astype(F32)).astype(BF)
    residual = (tok.astype(F32) + attn_out.astype(F32)).astype(BF)
    near = lax.ppermute(residual, AXES, spread_pairs(0)).reshape(4, rows_dev, quarter)
    far = lax.ppermute(residual, AXES, spread_pairs(1)).reshape(4, rows_dev, quarter)

    gathered = spread(jnp.stack([near, far], axis=1).reshape(rows // 4, quarter), YX, 16)
    gathered = gathered.reshape(4, 4, rows // 4, quarter)
    parts = feed_forward(gathered, norm_gain.reshape(1, width), gate_weight, up_weight, down_weight, core, z_lo)
    sums = jnp.sum(parts.astype(F32), axis=0)
    ffn_out = sums[:rows_dev] + swap(sums[rows_dev:].astype(BF), "z_hi").astype(F32)
    kept = pick(gathered, place_y)
    kept = lax.dynamic_slice_in_dim(kept, place_x * 2 * rows_dev, rows_dev, axis=1)
    kept = kept.transpose(1, 0, 2).reshape(rows_dev, width)
    return (kept.astype(F32) + ffn_out).astype(BF)


def solution(mesh):
    fine = Mesh(np.asarray(mesh.devices).reshape(SIZES), AXES)
    in_specs = (
        P(GRP, TP),
        P(GRP, TP),
        P(GRP, TP),
        P(GRP, TP),
        P(GRP, None, TP),
        P(GRP, None, TP),
        P(GRP),
        P(),
        P(TP, GRP),
        P(TP),
        P(TP, GRP),
        P(TP, GRP),
        P(GRP, TP),
    )
    return jax.shard_map(shards, mesh=fine, in_specs=in_specs, out_specs=P(GRP, TP), check_vma=False)
```

time: 643 us -> 249 us (0.39)
  waiting for transfers between devices: 528 us -> 133 us
  starting transfers between devices: 13.4 us -> 67.4 us
  blocking collectives: 49.4 us -> 0 us
  local copies, waits for them, and re-layouts: 8.29 us -> 31.6 us
  matrix products: 20.4 us -> 0.96 us
  between operations: 13.3 us -> 0.29 us
  Pallas kernels: 0 us -> 9.44 us
    reduce_scatter x2 -> x0, waiting for transfers between devices: 261 us -> none  [the longest x1 231 us: shards(): lax.psum_scatter(jnp.dot(hidden, down_weight, preferred_element_type=jnp....]
    all_gather x2 -> x0, waiting for transfers between devices: 170 us -> none  [the longest x1 95.6 us: shards(): part_rows = lax.all_gather(normed, 'grp', axis=0, tiled=True)]
    psum x1 -> x0, waiting for transfers between devices: 85.7 us -> none  [shards(): summed = lax.psum(gate_up, 'tp')]
    all_to_all x1 -> x5, waiting for transfers between devices: 11.8 us -> 86.2 us  [the longest x2 44 us: spread(): return lax.all_to_all(copies, axes, split_axis=0, concat_axis=0, tiled=True)]
    ppermute x0 -> x16, waiting for transfers between devices: none -> 47.2 us  [the longest x6 22.3 us: line_reduce(): lax.ppermute(piece, 'z_lo', [(i, i ^ step) for i in range(4)])]
    all_to_all x1 -> x0, blocking collectives: 34.8 us -> none  [shards(): lax.all_to_all(batch_rows, 'grp', split_axis=0, concat_axis=1, tiled=True)]
    ppermute x0 -> x16, starting transfers between devices: none -> 32.2 us  [the longest x6 10.6 us: line_reduce(): lax.ppermute(piece, 'z_lo', [(i, i ^ step) for i in range(4)])]
    all_to_all x1 -> x5, starting transfers between devices: 13.2 us -> 35.2 us  [the longest x2 15.3 us: spread(): return lax.all_to_all(copies, axes, split_axis=0, concat_axis=0, tiled=True)]
  transfers between devices with their start and end apart: 6 -> 21, of which waited for: 6 -> 21; matrix products, arithmetic and copies ran while one was open for 0% -> 6% of each run, Pallas kernels for 0% -> 0%
where the time goes in v1:
time: 249 us; the launch traced here: 248 us
  waiting for transfers between devices  133 us (53%)
  starting transfers between devices  67.4 us (27%)
  local copies, waits for them, and re-layouts  31.6 us (13%)
  Pallas kernels  9.44 us (4%)
  other arithmetic  4.99 us (2%)
    all_to_all x2, waiting for transfers between devices, spread(): return lax.all_to_all(copies, axes, split_axis=0, concat_axis=0, tiled=True)  44 us
    all_to_all x1, waiting for transfers between devices, feed_forward(): lax.all_to_all(down.reshape(16, rows // 16, width), YX, split_axis=0, con...  33.9 us
    ppermute x6, waiting for transfers between devices, line_reduce(): lax.ppermute(piece, 'z_lo', [(i, i ^ step) for i in range(4)])  22.3 us
    unnamed x22, local copies, waits for them, and re-layouts  22 us
    all_to_all x2, starting transfers between devices, spread(): return lax.all_to_all(copies, axes, split_axis=0, concat_axis=0, tiled=True)  15.3 us
    all_to_all x1, starting transfers between devices, shards(): lax.all_to_all(bucket, GRP, split_axis=0, concat_axis=0, tiled=True)  11.2 us
    ppermute x6, starting transfers between devices, line_reduce(): lax.ppermute(piece, 'z_lo', [(i, i ^ step) for i in range(4)])  10.6 us
    ppermute x3, waiting for transfers between devices, feed_forward(): lax.ppermute(hidden, 'z_lo', [(i, i ^ step) for i in range(4)])  9.93 us
  transfers between devices with their start and end apart: 21, of which 21 were waited for; matrix products, arithmetic and copies ran while one was open for 6% of the time, Pallas kernels for 0%

profile of v1, /device:TPU:32, one launch (start us, length us, event | category | flops | bytes accessed | tf_op | source)
XLA Modules:
  0.0 248.1 jit_solution(2712146964395675876)
XLA Ops:
  0.0 0.8 reshape.98
  0.8 0.2 convert_reduce_fusion.3
  1.0 1.0 convolution_convert_fusion
  1.9 0.7 reshape.99
  2.7 1.5 copy.64
  4.1 4.3 %all-to-all-start.1 = ((bf16[4,16,512]{2,1,0:T(8,128)(2,1)}), bf16[4,16,512]{2,1,0:T(8,128)(2,1)S(1)}, u32[]{:S(2)}, u32[]{:S(2)}) async-start(bf16[4,16,512]{2,1,0:T(8,128)(2,1)} %bitcast.42), calls=%async_computation.1 | async-start | bytes 131072 | tf_op jit(solution)/shard_map/all_to_all | solution.py:254
  8.4 1.2 convert_reduce_fusion.2
  9.6 0.7 multiply_add_fusion.1
  10.3 0.7 copy.51.len_ref
  11.1 3.0 %all-to-all-done.1 = bf16[4,16,512]{2,1,0:T(8,128)(2,1)S(1)} async-done(((bf16[4,16,512]{2,1,0:T(8,128)(2,1)}), bf16[4,16,512]{2,1,0:T(8,128)(2,1)S(1)}, u32[]{:S(2)}, u32[]{:S(2)}) %all-to-all-start.1) | async-done | bytes 65568 | tf_op jit(solution)/shard_map/all_to_all | solution.py:254
  14.1 11.2 %all-to-all-start = ((bf16[32,2,1280]{2,1,0:T(2,128)(2,1)}), bf16[32,2,1280]{2,1,0:T(2,128)(2,1)S(1)}, u32[]{:S(2)}, u32[]{:S(2)}) async-start(bf16[32,2,1280]{2,1,0:T(2,128)(2,1)} %reshape.99), calls=%async_computation | async-start | bytes 327680 | tf_op jit(solution)/shard_map/all_to_all | solution.py:235
  25.3 5.7 %collective-permute-start = (bf16[64,512]{1,0:T(8,128)(2,1)S(1)}, bf16[64,512]{1,0:T(8,128)(2,1)S(1)}, u32[]{:S(2)}, u32[]{:S(2)}) collective-permute-start(bf16[64,512]{1,0:T(8,128)(2,1)S(1)} %bitcast.52), channel_id=1, source_target_pairs={{0,0},{128,1},{32,2},{160,3},{64,4},{192,5},{96,6},{224,7},{8,8},{... | collective-permute-start | bytes 196616 | tf_op jit(solution)/shard_map/ppermute | solution.py:255
  30.9 0.2 select_reduce_fusion
  31.1 1.7 collective-permute-done
  32.8 5.3 %all-to-all-done = bf16[32,2,1280]{2,1,0:T(2,128)(2,1)S(1)} async-done(((bf16[32,2,1280]{2,1,0:T(2,128)(2,1)}), bf16[32,2,1280]{2,1,0:T(2,128)(2,1)S(1)}, u32[]{:S(2)}, u32[]{:S(2)}) %all-to-all-start) | async-done | bytes 163872 | tf_op jit(solution)/shard_map/all_to_all | solution.py:235
  38.3 0.9 copy-done.5
  39.2 0.9 copy-done.6
  40.1 0.9 shard_map.127
  41.0 1.1 broadcast_in_dim.19
  42.2 10.7 %all-to-all-start.2 = ((bf16[32,16,1024]{2,1,0:T(8,128)(2,1)}), bf16[32,16,1024]{2,1,0:T(8,128)(2,1)S(1)}, u32[]{:S(2)}, u32[]{:S(2)}) async-start(bf16[32,16,1024]{2,1,0:T(8,128)(2,1)} %broadcast_in_dim.19), calls=%async_computation.2 | async-start | bytes 2097152 | tf_op jit(solution)/shard_map/all_to_all | solution.py:53
  53.1 26.6 %all-to-all-done.2 = bf16[32,16,1024]{2,1,0:T(8,128)(2,1)S(1)} async-done(((bf16[32,16,1024]{2,1,0:T(8,128)(2,1)}), bf16[32,16,1024]{2,1,0:T(8,128)(2,1)S(1)}, u32[]{:S(2)}, u32[]{:S(2)}) %all-to-all-start.2) | async-done | bytes 1048608 | tf_op jit(solution)/shard_map/all_to_all | solution.py:53
  79.7 1.1 shard_map.128
  80.9 1.5 collective-permute-done.1.got_ref
  82.7 3.4 %collective-permute-start.4 = (bf16[64,512]{1,0:T(8,128)(2,1)S(1)}, bf16[64,512]{1,0:T(8,128)(2,1)S(1)}, u32[]{:S(2)}, u32[]{:S(2)}) collective-permute-start(bf16[64,512]{1,0:T(8,128)(2,1)S(1)} %get-tuple-element.34), channel_id=1, source_target_pairs={{0,6},{2,4},{4,2},{6,0},{1,7},{3,5},{5,3},{7,1},{8,14},{10,12},{12... | collective-permute-start | bytes 196616 | tf_op jit(solution)/shard_map/ppermute | solution.py:128
  86.0 1.3 collective-permute-done.2
  87.4 0.9 collective-permute-done.3
  88.3 3.6 %collective-permute-done.4 = bf16[64,512]{1,0:T(8,128)(2,1)S(1)} collective-permute-done((bf16[64,512]{1,0:T(8,128)(2,1)S(1)}, bf16[64,512]{1,0:T(8,128)(2,1)S(1)}, u32[]{:S(2)}, u32[]{:S(2)}) %collective-permute-start.4) | collective-permute-done | bytes 65568 | tf_op jit(solution)/shard_map/ppermute | solution.py:128
  91.9 2.0 collective-permute-start.5
  93.9 3.8 %collective-permute-start.6 = (bf16[64,512]{1,0:T(8,128)(2,1)S(1)}, bf16[64,512]{1,0:T(8,128)(2,1)S(1)}, u32[]{:S(2)}, u32[]{:S(2)}) collective-permute-start(bf16[64,512]{1,0:T(8,128)(2,1)S(1)} %add_convert_fusion), channel_id=1, source_target_pairs={{0,128},{1,0},{2,160},{3,32},{4,192},{5,64},{6,224},{7,96},{8,136}... | collective-permute-start | bytes 196616 | tf_op jit(solution)/shard_map/ppermute | solution.py:277
  97.7 4.1 %collective-permute-done.5 = bf16[64,512]{1,0:T(8,128)(2,1)S(1)} collective-permute-done((bf16[64,512]{1,0:T(8,128)(2,1)S(1)}, bf16[64,512]{1,0:T(8,128)(2,1)S(1)}, u32[]{:S(2)}, u32[]{:S(2)}) %collective-permute-start.5) | collective-permute-done | bytes 65568 | tf_op jit(solution)/shard_map/ppermute | solution.py:276
  101.9 1.6 broadcast_in_dim.25
  103.5 4.6 %all-to-all-start.3 = ((bf16[16,128,512]{2,1,0:T(8,128)(2,1)}), bf16[16,128,512]{2,1,0:T(8,128)(2,1)S(1)}, u32[]{:S(2)}, u32[]{:S(2)}) async-start(bf16[16,128,512]{2,1,0:T(8,128)(2,1)} %broadcast_in_dim.25), calls=%async_computation.3 | async-start | bytes 4194304 | tf_op jit(solution)/shard_map/all_to_all | solution.py:53
  108.1 6.0 %copy.57.gate_ref = bf16[2048,832]{1,0:T(8,128)(2,1)} copy(bf16[2048,832]{0,1:T(8,128)(2,1)} %param.23) | data formatting | bytes 6815744 | tf_op args[10]
  114.1 6.0 %copy.58.up_ref = bf16[2048,832]{1,0:T(8,128)(2,1)} copy(bf16[2048,832]{0,1:T(8,128)(2,1)} %param.24) | data formatting | bytes 6815744 | tf_op args[11]
  120.2 17.4 %all-to-all-done.3 = bf16[16,128,512]{2,1,0:T(8,128)(2,1)S(1)} async-done(((bf16[16,128,512]{2,1,0:T(8,128)(2,1)}), bf16[16,128,512]{2,1,0:T(8,128)(2,1)S(1)}, u32[]{:S(2)}, u32[]{:S(2)}) %all-to-all-start.3) | async-done | bytes 2097184 | tf_op jit(solution)/shard_map/all_to_all | solution.py:53
  137.6 2.0 copy-done
  139.6 2.0 copy-done.1
  141.7 4.7 %shard_map.130 = (bf16[256,1728]{1,0:T(8,128)(2,1)S(1)}, f32[256,1728]{1,0:T(8,128)S(1)}) custom-call(s32[1]{0:T(128)} %bitcast.21.core, bf16[4,4,128,512]{3,2,1,0:T(8,128)(2,1)S(1)} %bitcast.43, bf16[1,2048]{1,0:T(2,128)(2,1)S(1)} %reshape.111.gain_ref, bf16[2048,832]{1,0:T(8,128)(2,1)S(1)} %copy-done, bf16[2048,832]{1,0:T(8,128)(2,1)S(1)} %copy-done.1), custom_call_target="tpu_custom_call" | custom-call | flops 3489660928 | tf_op jit(solution)/shard_map/pallas_call | solution.py:60
  146.4 1.2 copy-done.3
  147.6 1.3 copy.59
  148.9 2.8 %collective-permute-done.7 = bf16[256,1728]{0,1:T(8,128)(2,1)} collective-permute-done((bf16[256,1728]{0,1:T(8,128)(2,1)}, bf16[256,1728]{0,1:T(8,128)(2,1)}, u32[]{:S(2)}, u32[]{:S(2)}) %collective-permute-start.7) | collective-permute-done | bytes 884768 | tf_op jit(solution)/shard_map/ppermute | solution.py:44
  151.7 1.4 copy.60.got_ref
  153.1 1.5 copy-done.4
  154.8 3.6 %collective-permute-start.10 = (bf16[64,1728]{1,0:T(8,128)(2,1)S(1)}, bf16[64,1728]{1,0:T(8,128)(2,1)S(1)}, u32[]{:S(2)}, u32[]{:S(2)}) collective-permute-start(bf16[64,1728]{1,0:T(8,128)(2,1)S(1)} %get-tuple-element.40), channel_id=1, source_target_pairs={{0,6},{2,4},{4,2},{6,0},{1,7},{3,5},{5,3},{7,1},{8,14},{10,12},{12... | collective-permute-start | bytes 663560 | tf_op jit(solution)/shard_map/ppermute | solution.py:128
  158.4 3.5 %collective-permute-start.8 = (bf16[64,1728]{1,0:T(8,128)(2,1)S(1)}, bf16[64,1728]{1,0:T(8,128)(2,1)S(1)}, u32[]{:S(2)}, u32[]{:S(2)}) collective-permute-start(bf16[64,1728]{1,0:T(8,128)(2,1)S(1)} %get-tuple-element.38), channel_id=1, source_target_pairs={{0,2},{2,0},{4,6},{6,4},{1,3},{3,1},{5,7},{7,5},{8,10},{10,8},{12,... | collective-permute-start | bytes 663560 | tf_op jit(solution)/shard_map/ppermute | solution.py:128
  161.8 7.8 %collective-permute-done.10.three_ref = bf16[64,1728]{1,0:T(8,128)(2,1)S(1)} collective-permute-done((bf16[64,1728]{1,0:T(8,128)(2,1)S(1)}, bf16[64,1728]{1,0:T(8,128)(2,1)S(1)}, u32[]{:S(2)}, u32[]{:S(2)}) %collective-permute-start.10) | collective-permute-done | bytes 221216 | tf_op jit(solution)/shard_map/ppermute | solution.py:128
  169.7 4.5 %collective-permute-done.8.one_ref = bf16[64,1728]{1,0:T(8,128)(2,1)S(1)} collective-permute-done((bf16[64,1728]{1,0:T(8,128)(2,1)S(1)}, bf16[64,1728]{1,0:T(8,128)(2,1)S(1)}, u32[]{:S(2)}, u32[]{:S(2)}) %collective-permute-start.8) | collective-permute-done | bytes 221216 | tf_op jit(solution)/shard_map/ppermute | solution.py:128
  174.1 4.1 %collective-permute-done.9.two_ref = bf16[64,1728]{1,0:T(8,128)(2,1)S(1)} collective-permute-done((bf16[64,1728]{1,0:T(8,128)(2,1)S(1)}, bf16[64,1728]{1,0:T(8,128)(2,1)S(1)}, u32[]{:S(2)}, u32[]{:S(2)}) %collective-permute-start.9) | collective-permute-done | bytes 221216 | tf_op jit(solution)/shard_map/ppermute | solution.py:128
  178.3 0.2 shard_map.132.own_ref
  178.5 2.3 collective-permute-start.11
  180.8 1.2 collective-permute-start.12
  182.1 0.5 collective-permute-start.13
  182.5 2.1 collective-permute-done.11.one_ref
  184.6 5.5 %collective-permute-done.12.two_ref = bf16[64,832]{1,0:T(8,128)(2,1)S(1)} collective-permute-done((bf16[64,832]{1,0:T(8,128)(2,1)S(1)}, bf16[64,832]{1,0:T(8,128)(2,1)S(1)}, u32[]{:S(2)}, u32[]{:S(2)}) %collective-permute-start.12) | collective-permute-done | bytes 106528 | tf_op jit(solution)/shard_map/ppermute | solution.py:189
  190.1 2.3 collective-permute-done.13.three_ref
  192.6 1.8 collective-permute-done.14.other_ref
  194.4 2.3 shard_map.134
  196.8 1.3 copy-done.2
  198.1 4.4 %all-to-all-start.4 = ((bf16[16,32,2048]{2,1,0:T(8,128)(2,1)}), bf16[16,32,2048]{2,1,0:T(8,128)(2,1)}, u32[]{:S(2)}, u32[]{:S(2)}) async-start(bf16[16,32,2048]{2,1,0:T(8,128)(2,1)} %bitcast.45), calls=%async_computation.4 | async-start | bytes 4194304 | tf_op jit(solution)/shard_map/all_to_all | solution.py:195
  202.5 33.9 %all-to-all-done.4 = bf16[16,32,2048]{2,1,0:T(8,128)(2,1)} async-done(((bf16[16,32,2048]{2,1,0:T(8,128)(2,1)}), bf16[16,32,2048]{2,1,0:T(8,128)(2,1)}, u32[]{:S(2)}, u32[]{:S(2)}) %all-to-all-start.4) | async-done | bytes 2097184 | tf_op jit(solution)/shard_map/all_to_all | solution.py:195
  236.4 2.0 convert_reduce_fusion
  238.5 6.0 %collective-permute-start.15 = (bf16[16,2048]{1,0:T(8,128)(2,1)S(1)}, bf16[16,2048]{1,0:T(8,128)(2,1)S(1)}, u32[]{:S(2)}, u32[]{:S(2)}) collective-permute-start(bf16[16,2048]{1,0:T(8,128)(2,1)S(1)} %slice.17), channel_id=1, source_target_pairs={{0,128},{128,0},{1,129},{129,1},{2,130},{130,2},{3,131},{131,3},{4... | collective-permute-start | bytes 196616 | tf_op jit(solution)/shard_map/ppermute | solution.py:44
  244.5 2.9 %collective-permute-done.15 = bf16[16,2048]{1,0:T(8,128)(2,1)S(1)} collective-permute-done((bf16[16,2048]{1,0:T(8,128)(2,1)S(1)}, bf16[16,2048]{1,0:T(8,128)(2,1)S(1)}, u32[]{:S(2)}, u32[]{:S(2)}) %collective-permute-start.15) | collective-permute-done | bytes 65568 | tf_op jit(solution)/shard_map/ppermute | solution.py:44
  247.4 0.7 fusion.2
  (40 shorter events, 1.3 us)
Async XLA Ops:
  4.1 9.9 %all-to-all-start.1 = ((bf16[4,16,512]{2,1,0:T(8,128)(2,1)}), bf16[4,16,512]{2,1,0:T(8,128)(2,1)S(1)}, u32[]{:S(2)}, u32[]{:S(2)}) async-start(bf16[4,16,512]{2,1,0:T(8,128)(2,1)} %bitcast.42), calls=%async_computation.1 | async-start | bytes 131072 | tf_op jit(solution)/shard_map/all_to_all | solution.py:254
  14.1 24.1 %all-to-all-start = ((bf16[32,2,1280]{2,1,0:T(2,128)(2,1)}), bf16[32,2,1280]{2,1,0:T(2,128)(2,1)S(1)}, u32[]{:S(2)}, u32[]{:S(2)}) async-start(bf16[32,2,1280]{2,1,0:T(2,128)(2,1)} %reshape.99), calls=%async_computation | async-start | bytes 327680 | tf_op jit(solution)/shard_map/all_to_all | solution.py:235
  25.3 7.6 %collective-permute-start = (bf16[64,512]{1,0:T(8,128)(2,1)S(1)}, bf16[64,512]{1,0:T(8,128)(2,1)S(1)}, u32[]{:S(2)}, u32[]{:S(2)}) collective-permute-start(bf16[64,512]{1,0:T(8,128)(2,1)S(1)} %bitcast.52), channel_id=1, source_target_pairs={{0,0},{128,1},{32,2},{160,3},{64,4},{192,5},{96,6},{224,7},{8,8},{... | collective-permute-start | bytes 196616 | tf_op jit(solution)/shard_map/ppermute | solution.py:255
  38.3 0.9 copy-start.5
  39.2 0.9 copy-start.6
  40.1 39.6 %copy-start.8 = (bf16[1024,512]{1,0:T(8,128)(2,1)S(1)}, bf16[1024,512]{1,0:T(8,128)(2,1)}, u32[]{:S(2)}) copy-start(bf16[1024,512]{1,0:T(8,128)(2,1)} %weight_ref.2) | copy-start | bytes 3145732
  42.2 37.5 %all-to-all-start.2 = ((bf16[32,16,1024]{2,1,0:T(8,128)(2,1)}), bf16[32,16,1024]{2,1,0:T(8,128)(2,1)S(1)}, u32[]{:S(2)}, u32[]{:S(2)}) async-start(bf16[32,16,1024]{2,1,0:T(8,128)(2,1)} %broadcast_in_dim.19), calls=%async_computation.2 | async-start | bytes 2097152 | tf_op jit(solution)/shard_map/all_to_all | solution.py:53
  80.8 1.6 collective-permute-start.1
  82.5 4.9 %collective-permute-start.2 = (bf16[64,512]{1,0:T(8,128)(2,1)S(1)}, bf16[64,512]{1,0:T(8,128)(2,1)S(1)}, u32[]{:S(2)}, u32[]{:S(2)}) collective-permute-start(bf16[64,512]{1,0:T(8,128)(2,1)S(1)} %get-tuple-element.32), channel_id=1, source_target_pairs={{0,2},{2,0},{4,6},{6,4},{1,3},{3,1},{5,7},{7,5},{8,10},{10,8},{12,... | collective-permute-start | bytes 196616 | tf_op jit(solution)/shard_map/ppermute | solution.py:128
  82.6 5.7 %collective-permute-start.3 = (bf16[64,512]{1,0:T(8,128)(2,1)S(1)}, bf16[64,512]{1,0:T(8,128)(2,1)S(1)}, u32[]{:S(2)}, u32[]{:S(2)}) collective-permute-start(bf16[64,512]{1,0:T(8,128)(2,1)S(1)} %get-tuple-element.33), channel_id=1, source_target_pairs={{0,4},{2,6},{4,0},{6,2},{1,5},{3,7},{5,1},{7,3},{8,12},{10,14},{12... | collective-permute-start | bytes 196616 | tf_op jit(solution)/shard_map/ppermute | solution.py:128
  82.7 9.2 %collective-permute-start.4 = (bf16[64,512]{1,0:T(8,128)(2,1)S(1)}, bf16[64,512]{1,0:T(8,128)(2,1)S(1)}, u32[]{:S(2)}, u32[]{:S(2)}) collective-permute-start(bf16[64,512]{1,0:T(8,128)(2,1)S(1)} %get-tuple-element.34), channel_id=1, source_target_pairs={{0,6},{2,4},{4,2},{6,0},{1,7},{3,5},{5,3},{7,1},{8,14},{10,12},{12... | collective-permute-start | bytes 196616 | tf_op jit(solution)/shard_map/ppermute | solution.py:128
  91.9 9.9 %collective-permute-start.5 = (bf16[64,512]{1,0:T(8,128)(2,1)S(1)}, bf16[64,512]{1,0:T(8,128)(2,1)S(1)}, u32[]{:S(2)}, u32[]{:S(2)}) collective-permute-start(bf16[64,512]{1,0:T(8,128)(2,1)S(1)} %add_convert_fusion), channel_id=1, source_target_pairs={{0,0},{1,128},{2,32},{3,160},{4,64},{5,192},{6,96},{7,224},{8,8},{... | collective-permute-start | bytes 196616 | tf_op jit(solution)/shard_map/ppermute | solution.py:276
  93.9 8.0 %collective-permute-start.6 = (bf16[64,512]{1,0:T(8,128)(2,1)S(1)}, bf16[64,512]{1,0:T(8,128)(2,1)S(1)}, u32[]{:S(2)}, u32[]{:S(2)}) collective-permute-start(bf16[64,512]{1,0:T(8,128)(2,1)S(1)} %add_convert_fusion), channel_id=1, source_target_pairs={{0,128},{1,0},{2,160},{3,32},{4,192},{5,64},{6,224},{7,96},{8,136}... | collective-permute-start | bytes 196616 | tf_op jit(solution)/shard_map/ppermute | solution.py:277
  103.5 34.1 %all-to-all-start.3 = ((bf16[16,128,512]{2,1,0:T(8,128)(2,1)}), bf16[16,128,512]{2,1,0:T(8,128)(2,1)S(1)}, u32[]{:S(2)}, u32[]{:S(2)}) async-start(bf16[16,128,512]{2,1,0:T(8,128)(2,1)} %broadcast_in_dim.25), calls=%async_computation.3 | async-start | bytes 4194304 | tf_op jit(solution)/shard_map/all_to_all | solution.py:53
  114.1 6.0 %copy-start.9 = (bf16[2048]{0:T(1024)(128)(2,1)S(1)}, bf16[2048]{0:T(1024)(128)(2,1)}, u32[]{:S(2)}) copy-start(bf16[2048]{0:T(1024)(128)(2,1)} %param.22) | copy-start | bytes 12292
  137.6 2.0 copy-start
  139.6 2.0 copy-start.1
  146.4 1.3 copy-start.3
  148.9 2.8 %collective-permute-start.7 = (bf16[256,1728]{0,1:T(8,128)(2,1)}, bf16[256,1728]{0,1:T(8,128)(2,1)}, u32[]{:S(2)}, u32[]{:S(2)}) collective-permute-start(bf16[256,1728]{0,1:T(8,128)(2,1)} %copy.59), channel_id=1, source_target_pairs={{0,1},{1,0},{2,3},{3,2},{4,5},{5,4},{6,7},{7,6},{8,9},{9,8},{10,11... | collective-permute-start | bytes 2654216 | tf_op jit(solution)/shard_map/ppermute | solution.py:44
  153.1 1.5 copy-start.4
  154.6 39.8 %copy-start.7 = (bf16[832,2048]{1,0:T(8,128)(2,1)S(1)}, bf16[832,2048]{1,0:T(8,128)(2,1)}, u32[]{:S(2)}) copy-start(bf16[832,2048]{1,0:T(8,128)(2,1)} %weight_ref.3) | copy-start | bytes 10223620
  154.8 14.9 %collective-permute-start.10 = (bf16[64,1728]{1,0:T(8,128)(2,1)S(1)}, bf16[64,1728]{1,0:T(8,128)(2,1)S(1)}, u32[]{:S(2)}, u32[]{:S(2)}) collective-permute-start(bf16[64,1728]{1,0:T(8,128)(2,1)S(1)} %get-tuple-element.40), channel_id=1, source_target_pairs={{0,6},{2,4},{4,2},{6,0},{1,7},{3,5},{5,3},{7,1},{8,14},{10,12},{12... | collective-permute-start | bytes 663560 | tf_op jit(solution)/shard_map/ppermute | solution.py:128
  158.4 15.8 %collective-permute-start.8 = (bf16[64,1728]{1,0:T(8,128)(2,1)S(1)}, bf16[64,1728]{1,0:T(8,128)(2,1)S(1)}, u32[]{:S(2)}, u32[]{:S(2)}) collective-permute-start(bf16[64,1728]{1,0:T(8,128)(2,1)S(1)} %get-tuple-element.38), channel_id=1, source_target_pairs={{0,2},{2,0},{4,6},{6,4},{1,3},{3,1},{5,7},{7,5},{8,10},{10,8},{12,... | collective-permute-start | bytes 663560 | tf_op jit(solution)/shard_map/ppermute | solution.py:128
  161.8 16.5 %collective-permute-start.9 = (bf16[64,1728]{1,0:T(8,128)(2,1)S(1)}, bf16[64,1728]{1,0:T(8,128)(2,1)S(1)}, u32[]{:S(2)}, u32[]{:S(2)}) collective-permute-start(bf16[64,1728]{1,0:T(8,128)(2,1)S(1)} %get-tuple-element.39), channel_id=1, source_target_pairs={{0,4},{2,6},{4,0},{6,2},{1,5},{3,7},{5,1},{7,3},{8,12},{10,14},{12... | collective-permute-start | bytes 663560 | tf_op jit(solution)/shard_map/ppermute | solution.py:128
  178.5 6.1 %collective-permute-start.11 = (bf16[64,832]{1,0:T(8,128)(2,1)S(1)}, bf16[64,832]{1,0:T(8,128)(2,1)S(1)}, u32[]{:S(2)}, u32[]{:S(2)}) collective-permute-start(bf16[64,832]{1,0:T(8,128)(2,1)S(1)} %shard_map.132.own_ref), channel_id=1, source_target_pairs={{0,2},{2,0},{4,6},{6,4},{1,3},{3,1},{5,7},{7,5},{8,10},{10,8},{12,... | collective-permute-start | bytes 319496 | tf_op jit(solution)/shard_map/ppermute | solution.py:189
  180.8 9.3 %collective-permute-start.12 = (bf16[64,832]{1,0:T(8,128)(2,1)S(1)}, bf16[64,832]{1,0:T(8,128)(2,1)S(1)}, u32[]{:S(2)}, u32[]{:S(2)}) collective-permute-start(bf16[64,832]{1,0:T(8,128)(2,1)S(1)} %shard_map.132.own_ref), channel_id=1, source_target_pairs={{0,4},{2,6},{4,0},{6,2},{1,5},{3,7},{5,1},{7,3},{8,12},{10,14},{12... | collective-permute-start | bytes 319496 | tf_op jit(solution)/shard_map/ppermute | solution.py:189
  182.1 10.4 %collective-permute-start.13 = (bf16[64,832]{1,0:T(8,128)(2,1)S(1)}, bf16[64,832]{1,0:T(8,128)(2,1)S(1)}, u32[]{:S(2)}, u32[]{:S(2)}) collective-permute-start(bf16[64,832]{1,0:T(8,128)(2,1)S(1)} %shard_map.132.own_ref), channel_id=1, source_target_pairs={{0,6},{2,4},{4,2},{6,0},{1,7},{3,5},{5,3},{7,1},{8,14},{10,12},{12... | collective-permute-start | bytes 319496 | tf_op jit(solution)/shard_map/ppermute | solution.py:189
  192.5 1.9 collective-permute-start.14
  196.8 1.3 copy-start.2
  198.1 38.4 %all-to-all-start.4 = ((bf16[16,32,2048]{2,1,0:T(8,128)(2,1)}), bf16[16,32,2048]{2,1,0:T(8,128)(2,1)}, u32[]{:S(2)}, u32[]{:S(2)}) async-start(bf16[16,32,2048]{2,1,0:T(8,128)(2,1)} %bitcast.45), calls=%async_computation.4 | async-start | bytes 4194304 | tf_op jit(solution)/shard_map/all_to_all | solution.py:195
  238.5 9.0 %collective-permute-start.15 = (bf16[16,2048]{1,0:T(8,128)(2,1)S(1)}, bf16[16,2048]{1,0:T(8,128)(2,1)S(1)}, u32[]{:S(2)}, u32[]{:S(2)}) collective-permute-start(bf16[16,2048]{1,0:T(8,128)(2,1)S(1)} %slice.17), channel_id=1, source_target_pairs={{0,128},{128,0},{1,129},{129,1},{2,130},{130,2},{3,131},{131,3},{4... | collective-permute-start | bytes 196616 | tf_op jit(solution)/shard_map/ppermute | solution.py:44

commit v2 on v1

v2 whole, which is shorter than its diff:
```python
import functools
import math

import jax
import jax.numpy as jnp
import numpy as np
from jax import lax
from jax.experimental import pallas as pl
from jax.experimental.pallas import tpu as pltpu
from jax.sharding import Mesh
from jax.sharding import PartitionSpec as P

D = 16384
HD = 128
AXES = ("z_hi", "y", "x", "z_lo", "core")
SIZES = (2, 4, 4, 4, 2)
GRP = ("z_hi", "y", "x")
TP = ("z_lo", "core")
YX = ("y", "x")
BF = jnp.bfloat16
F32 = jnp.float32
MIB = 1 << 20
PAD = 896


def flat(z_hi, y, x, z_lo, core):
    return (((z_hi * 4 + y) * 4 + x) * 4 + z_lo) * 2 + core


def spread_pairs(flip):
    pairs = []
    for z_hi in range(2):
        for y in range(4):
            for x in range(4):
                for z_lo in range(4):
                    for core in range(2):
                        src = flat(z_hi, y, x, z_lo, core)
                        dst = flat(core ^ flip, z_lo, x, 2 * z_hi + y // 2, y % 2)
                        pairs.append((src, dst))
    return pairs


def swap(v, axis):
    return lax.ppermute(v, axis, [(0, 1), (1, 0)])


def pick(v, index):
    return lax.dynamic_index_in_dim(v, index, 0, keepdims=False)


def exchange(copies, *others):
    copies, *others = lax.optimization_barrier((copies, *others))
    got = lax.all_to_all(copies, YX, split_axis=0, concat_axis=0, tiled=True)
    return lax.optimization_barrier((got, *others))


def call(body, out_shape, *operands, scalars=(), streamed=(), scratch=(), limit=12):
    whole = pl.BlockSpec(memory_space=pltpu.VMEM)
    single = not isinstance(out_shape, (list, tuple))
    specs = [pl.BlockSpec(memory_space=pltpu.SMEM)] * len(scalars) + [whole] * len(operands)
    specs += [pl.BlockSpec(memory_space=pltpu.HBM)] * len(streamed)
    return pl.pallas_call(
        body,
        out_shape=out_shape,
        in_specs=specs,
        out_specs=whole if single else [whole] * len(out_shape),
        scratch_shapes=list(scratch),
        compiler_params=pltpu.CompilerParams(vmem_limit_bytes=limit * MIB),
        cost_estimate=pl.CostEstimate(flops=1, bytes_accessed=1, transcendentals=0),
    )(*[jnp.reshape(s, (1,)).astype(jnp.int32) for s in scalars], *operands, *streamed)


def shape(dims, dtype):
    return jax.ShapeDtypeStruct(dims, dtype)


def dot(a, b):
    return jnp.dot(a, b, preferred_element_type=F32)


def dot_t(a, b):
    return lax.dot_general(a, b, (((1,), (1,)), ((), ())), preferred_element_type=F32)


def attend_body(
    rows, cache_len, heads, place_x, slot_ref, got_ref, len_ref, own_tok, one_tok, two_tok, three_tok,
    key_ref, value_ref, out_ref,
):
    cols = own_tok.shape[1]
    for step, piece in enumerate((own_tok, one_tok, two_tok, three_tok)):
        group = place_x[0] ^ step
        at = pl.ds(pl.multiple_of(rows + (group & 1) * rows, rows), rows)
        out_ref[at, pl.ds(pl.multiple_of((group >> 1) * cols, cols), cols)] = piece[...]
    slots = lax.broadcasted_iota(jnp.int32, (rows, got_ref.shape[0]), 1)
    compact = (slot_ref[...] == slots).astype(F32).astype(BF)
    arrived = dot(compact, got_ref[...])
    q_cols = heads * HD
    rounded = arrived[:, :q_cols].astype(BF)
    tall = jnp.concatenate([rounded[:, j * HD : (j + 1) * HD] for j in range(heads)], axis=0)
    key_new = jnp.concatenate([arrived[:, q_cols : q_cols + HD]] * heads, axis=0)
    value_new = jnp.concatenate([arrived[:, q_cols + HD :]] * heads, axis=0)
    scale = 1.0 / math.sqrt(HD)
    own = jnp.sum(tall.astype(F32) * key_new, axis=1, keepdims=True) * scale
    scores = dot_t(tall, key_ref[...]) * scale
    spot = lax.broadcasted_iota(jnp.int32, scores.shape, 1)
    row = lax.rem(lax.broadcasted_iota(jnp.int32, scores.shape, 0), rows)
    start = row * cache_len
    lens = jnp.concatenate([len_ref[...]] * heads, axis=0)
    live = (spot >= start) & (spot < start + lens)
    masked = jnp.where(live, scores, -1e30)
    top = jnp.maximum(jnp.max(masked, axis=1, keepdims=True), own)
    exp_live = jnp.where(live, jnp.exp(masked - top), 0.0)
    exp_own = jnp.exp(own - top)
    total = jnp.sum(exp_live, axis=1, keepdims=True) + exp_own
    weights = (exp_live / total).astype(BF)
    own_weight = (exp_own / total).astype(BF).astype(F32)
    out = (dot(weights, value_ref[...]) + own_weight * value_new).astype(BF)
    for j in range(heads):
        out_ref[:rows, j * HD : (j + 1) * HD] = out[j * rows : (j + 1) * rows]


def project_body(send_pos, keep_pos, heads_ref, weight_ref, send_ref, keep_ref):
    product = dot(heads_ref[...], weight_ref[...]).astype(BF)
    for pos, out in ((send_pos, send_ref), (keep_pos, keep_ref)):
        spot = lax.broadcasted_iota(jnp.int32, (pos.shape[0], product.shape[0]), 1)
        unsort = (pos[...] == spot).astype(F32).astype(BF)
        out[...] = dot(unsort, product).astype(BF)


def split_body(z_lo, keep_ref, got_ref, own_ref, one_ref, two_ref, three_ref, mark_ref):
    rows = own_ref.shape[0]
    mark_ref[...] = jnp.zeros(mark_ref.shape, mark_ref.dtype)
    for step, out in enumerate((own_ref, one_ref, two_ref, three_ref)):
        at = pl.ds(pl.multiple_of((z_lo[0] ^ step) * rows, rows), rows)
        out[...] = (keep_ref[at, :].astype(F32) + got_ref[at, :].astype(F32)).astype(out.dtype)


MARK = jax.ShapeDtypeStruct((8, 128), F32)


def line_reduce(keep, got, z_lo):
    rows, cols = keep.shape[0] // 4, keep.shape[1]
    outs = [shape((rows, cols), F32)] + [shape((rows, cols), BF)] * 3 + [MARK]
    own, *pieces, mark = call(split_body, outs, keep, got, scalars=(z_lo,))
    return [own] + line_send(pieces), mark


def line_send(pieces):
    return [
        lax.ppermute(piece, "z_lo", [(i, i ^ step) for i in range(4)])
        for step, piece in zip((1, 2, 3), pieces)
    ]


def gate_up_body(core, rows_ref, gain_ref, gate_ref, up_ref, *refs):
    send_ref, keep_ref, mark_ref, total = refs[-4:]
    mark_ref[...] = jnp.zeros(mark_ref.shape, mark_ref.dtype)
    hid = gate_ref.shape[0]
    planes, blocks, count, cols = rows_ref.shape
    rows = planes * count
    squares = jnp.zeros((rows, 1), F32)
    parts = []
    for b in range(blocks):
        wide = rows_ref[:, b].reshape(rows, cols).astype(F32)
        squares += jnp.sum(wide * wide, axis=1, keepdims=True)
        parts.append((wide * gain_ref[:, b * cols : (b + 1) * cols].astype(F32)).astype(BF))
    scaled = jnp.concatenate(parts, axis=1)
    total[:, :hid] = dot_t(scaled, gate_ref[...])
    total[:, PAD : PAD + hid] = dot_t(scaled, up_ref[...])
    total[:, PAD + hid :] = jnp.zeros((rows, PAD - hid), F32)
    high = squares.astype(BF).astype(F32)
    lane = lax.broadcasted_iota(jnp.int32, (rows, PAD - hid), 1)
    total[:, hid:PAD] = jnp.where(lane == 0, high, jnp.where(lane == 1, squares - high, 0.0))
    half = rows // 2
    send_ref[...] = total[pl.ds(pl.multiple_of((1 - core[0]) * half, half), half), :].astype(BF)
    keep_ref[...] = total[pl.ds(pl.multiple_of(core[0] * half, half), half), :].astype(BF)


def hidden_body(own_ref, one_ref, two_ref, three_ref, mark_ref, out_ref):
    hid = out_ref.shape[1]
    sums = own_ref[...] + one_ref[...].astype(F32) + two_ref[...].astype(F32) + three_ref[...].astype(F32)
    mean_square = (sums[:, hid : hid + 1] + sums[:, hid + 1 : hid + 2]) / D
    inv = lax.rsqrt(mean_square + 1e-05)
    gate = sums[:, :hid] * inv
    up = sums[:, PAD : PAD + hid] * inv
    out_ref[...] = (gate / (1.0 + jnp.exp(-gate)) * up).astype(BF)


def join_body(z_lo, own_ref, one_ref, two_ref, three_ref, mark_ref, out_ref):
    rows = own_ref.shape[0]
    for step, piece in enumerate((own_ref, one_ref, two_ref, three_ref)):
        out_ref[pl.ds(pl.multiple_of((z_lo[0] ^ step) * rows, rows), rows), :] = piece[...]


def part_body(x, rows_ref, *outs):
    cols = outs[0].shape[1]
    for step, out in enumerate(outs):
        out[...] = rows_ref[:, pl.ds(pl.multiple_of((x[0] ^ step) * cols, cols), cols)]


def heads_body(rows, near_ref, far_ref, out_ref):
    for copy in range(out_ref.shape[0]):
        out_ref[copy, :rows] = near_ref[:rows]
        out_ref[copy, rows:] = far_ref[:rows]


def residual_body(rows, attn_ref, tok_ref, out_ref):
    cols = attn_ref.shape[1]
    for group in range(attn_ref.shape[0] // rows):
        at = rows + (group & 1) * rows
        side = (group >> 1) * cols
        tok = tok_ref[at : at + rows, side : side + cols].astype(F32)
        total = (attn_ref[group * rows : (group + 1) * rows].astype(F32) + tok).astype(BF)
        for copy in range(out_ref.shape[0]):
            out_ref[copy, group * rows : (group + 1) * rows] = total


def fold_body(parts_ref, out_ref):
    total = parts_ref[0].astype(F32)
    for part in range(1, parts_ref.shape[0]):
        total += parts_ref[part].astype(F32)
    out_ref[...] = total.astype(out_ref.dtype)


def down_body(core, own_ref, other_ref, weight_ref, out_ref, mark_ref):
    mark_ref[...] = jnp.zeros(mark_ref.shape, mark_ref.dtype)
    half = own_ref.shape[0]
    for place, rows_ref in ((core[0], own_ref), (1 - core[0], other_ref)):
        at = pl.ds(pl.multiple_of(place * half, half), half)
        out_ref[at, :] = dot(rows_ref[...], weight_ref[...]).astype(BF)


def gate_up(gathered, gain, gate_t, up_t, core, *marks):
    rows = gathered.shape[0] * gathered.shape[2]
    outs = [shape((rows // 2, 2 * PAD), BF)] * 2 + [MARK]
    return call(
        gate_up_body, outs, gathered, gain, gate_t, up_t, *marks,
        scalars=(core,), scratch=[pltpu.VMEM((rows, 2 * PAD), F32)], limit=20,
    )


def hidden_gather(pieces, hid, mark):
    hidden = call(hidden_body, shape((pieces[0].shape[0], hid), BF), *pieces, mark)
    return [hidden] + line_send([hidden] * 3)


def down_project(pieces, down_weight, z_lo, core, mark):
    quarter, hid = pieces[0].shape
    width = down_weight.shape[1]
    half = call(join_body, shape((4 * quarter, hid), BF), *pieces, mark, scalars=(z_lo,))
    return call(
        down_body, [shape((8 * quarter, width), BF), MARK], half, swap(half, "core"), down_weight,
        scalars=(core,), limit=16,
    )


def all_to_all(v, axes):
    return lax.all_to_all(v, axes, split_axis=0, concat_axis=0, tiled=True)


def shards(
    tokens,
    queries,
    new_key,
    new_value,
    key_cache,
    value_cache,
    lengths,
    group_of,
    out_weight,
    norm_gain,
    gate_weight,
    up_weight,
    down_weight,
):
    groups = 32
    rows_dev, width = tokens.shape
    rows = group_of.shape[0]
    q_cols = queries.shape[1]
    cache_len = key_cache.shape[1]
    capacity = 2
    quarter = width // 4
    own_group = lax.axis_index(GRP)
    z_lo = lax.axis_index("z_lo")
    core = lax.axis_index("core")
    place_z = lax.axis_index("z_hi")
    place_y = lax.axis_index("y")
    place_x = lax.axis_index("x")

    blocks = group_of.reshape(groups, rows_dev)
    mine = pick(blocks, own_group)
    earlier = jnp.arange(rows_dev)[:, None] > jnp.arange(rows_dev)[None, :]
    my_ranks = jnp.sum((mine[:, None] == mine[None, :]) & earlier, axis=1, dtype=jnp.int32)
    my_slots = mine * capacity + my_ranks
    selector = (jnp.arange(groups * capacity, dtype=jnp.int32)[:, None] == my_slots[None, :]).astype(BF)
    packed = jnp.concatenate([queries, new_key, new_value], axis=1)
    bucket = dot(selector, packed).astype(BF).reshape(groups, capacity, packed.shape[1])
    bucket, tokens_in = lax.optimization_barrier((bucket, tokens))
    received = lax.all_to_all(bucket, GRP, split_axis=0, concat_axis=0, tiled=True)

    flat_groups = group_of.reshape(rows)
    same = flat_groups[:, None] == flat_groups[None, :]
    index = jnp.arange(rows, dtype=jnp.int32)
    before = same & (index[:, None] > index[None, :])
    in_block = index // rows_dev
    ahead = jnp.sum(before, axis=1, dtype=jnp.int32)
    block_rank = jnp.sum(before & (in_block[:, None] == in_block[None, :]), axis=1, dtype=jnp.int32)
    slot_of = in_block * capacity + block_rank
    wanted = own_group * rows_dev + jnp.arange(rows_dev, dtype=jnp.int32)
    position = flat_groups * rows_dev + ahead
    arrival = jnp.sum(
        jnp.where(position[None, :] == wanted[:, None], slot_of[None, :], 0), axis=1, keepdims=True, dtype=jnp.int32
    )
    plane = groups // 2
    gathered_at = ((flat_groups % plane) * 2 + (flat_groups // plane ^ place_z)) * rows_dev + ahead
    halves = gathered_at.reshape(2, rows // 2, 1)
    send_pos, keep_pos = pick(halves, 1 - core), pick(halves, core)

    pieces = call(part_body, [shape((rows_dev, quarter), BF)] * 4, tokens_in, scalars=(place_x,))
    pieces = [pieces[0]] + [
        lax.ppermute(pieces[step], "x", [(i, i ^ step) for i in range(4)]) for step in (1, 2, 3)
    ]

    caches = [cache.reshape(rows_dev * cache_len, HD) for cache in (key_cache, value_cache)]
    heads = call(
        functools.partial(attend_body, rows_dev, cache_len, q_cols // HD),
        shape((3 * rows_dev, q_cols), BF),
        arrival,
        received.reshape(groups * capacity, packed.shape[1]),
        lengths.reshape(rows_dev, 1),
        *pieces,
        *caches,
        scalars=(place_x,),
    )
    far_heads = swap(heads, "z_hi")
    copies = call(
        functools.partial(heads_body, rows_dev), shape((plane, 2 * rows_dev, q_cols), BF), heads, far_heads
    )
    gathered, send_pos, keep_pos = exchange(copies, send_pos, keep_pos)
    outs = [shape((rows // 2, out_weight.shape[1]), BF)] * 2
    send, keep = call(
        project_body, outs, send_pos, keep_pos, gathered.reshape(rows, q_cols), out_weight,
    )
    (own, one, two, three), _ = line_reduce(keep, swap(send, "core"), z_lo)
    attn_out = (own + one.astype(F32) + two.astype(F32) + three.astype(F32)).astype(BF)
    far = lax.ppermute(attn_out, AXES, spread_pairs(1))
    near = lax.ppermute(attn_out, AXES, spread_pairs(0))
    gain = norm_gain.reshape(1, width)
    hid = down_weight.shape[0]
    gate_t, up_t = gate_weight.T, up_weight.T
    gathered = []
    for attn, tok in ((far, far_heads), (near, heads)):
        copies = call(
            functools.partial(residual_body, rows_dev), shape((plane, rows // 8, quarter), BF), attn, tok
        )
        gathered.append(all_to_all(copies, YX).reshape(4, 4, rows // 8, quarter))
    far_send, far_keep, _ = gate_up(gathered[0], gain, gate_t, up_t, core)
    far_pieces, far_sent = line_reduce(far_keep, swap(far_send, "core"), z_lo)
    near_gathered = gathered[1]
    near_send, near_keep, near_done = gate_up(near_gathered, gain, gate_t, up_t, core, far_sent)
    far_hidden = call(hidden_body, shape((far_pieces[0].shape[0], hid), BF), *far_pieces, near_done)
    near_send, far_hidden = lax.optimization_barrier((near_send, far_hidden))
    near_pieces, near_sent = line_reduce(near_keep, swap(near_send, "core"), z_lo)
    far_hidden = [far_hidden] + line_send([far_hidden] * 3)
    far_down, far_done = down_project(far_hidden, down_weight, z_lo, core, near_sent)
    far_down, near_pieces = lax.optimization_barrier((far_down, near_pieces))
    far_parts = all_to_all(far_down.reshape(plane, rows_dev, width), YX)
    near_hidden = hidden_gather(near_pieces, hid, far_done)
    near_down, near_done = down_project(near_hidden, down_weight, z_lo, core, far_done)
    near_parts = all_to_all(near_down.reshape(plane, rows_dev, width), YX)
    kept = lax.dynamic_slice_in_dim(pick(near_gathered, place_y), place_x * rows_dev, rows_dev, axis=1)
    kept = kept.transpose(1, 0, 2).reshape(rows_dev, width)
    far_sum = call(fold_body, shape((rows_dev, width), BF), far_parts)
    near_sum = call(fold_body, shape((rows_dev, width), F32), near_parts)
    return (kept.astype(F32) + (near_sum + swap(far_sum, "z_hi").astype(F32))).astype(BF)


def solution(mesh):
    fine = Mesh(np.asarray(mesh.devices).reshape(SIZES), AXES)
    in_specs = (
        P(GRP, TP),
        P(GRP, TP),
        P(GRP, TP),
        P(GRP, TP),
        P(GRP, None, TP),
        P(GRP, None, TP),
        P(GRP),
        P(),
        P(TP, GRP),
        P(TP),
        P(TP, GRP),
        P(TP, GRP),
        P(GRP, TP),
    )
    return jax.shard_map(shards, mesh=fine, in_specs=in_specs, out_specs=P(GRP, TP), check_vma=False)
```

time: 249 us -> 206 us (0.83)
  waiting for transfers between devices: 133 us -> 74.6 us
  blocking collectives: 0 us -> 17.8 us
  local copies, waits for them, and re-layouts: 31.6 us -> 18.6 us
  Pallas kernels: 9.44 us -> 17.3 us
  starting transfers between devices: 67.4 us -> 70.8 us
    all_to_all x4, waiting for transfers between devices: 80.9 us -> 21.9 us  [all_to_all(): return lax.all_to_all(v, axes, split_axis=0, concat_axis=0, tiled=True)]
    all_to_all x0 -> x1, blocking collectives: none -> 17.8 us  [exchange(): got = lax.all_to_all(copies, YX, split_axis=0, concat_axis=0, tiled=True)]
    pallas_call x8 -> x19, Pallas kernels: 9.44 us -> 17.3 us  [call(): pl.pallas_call(body, out_shape=out_shape, in_specs=specs, out_specs=whole...]
    unnamed x22 -> x50, local copies, waits for them, and re-layouts: 22 us -> 15.9 us
    ppermute x12 -> x20, starting transfers between devices: 26 us -> 31.7 us  [the longest x15 20.9 us: line_send(): lax.ppermute(piece, 'z_lo', [(i, i ^ step) for i in range(4)])]
    all_to_all x4, starting transfers between devices: 24 us -> 19.6 us  [all_to_all(): return lax.all_to_all(v, axes, split_axis=0, concat_axis=0, tiled=True)]
    ppermute x4 -> x7, waiting for transfers between devices: 9.02 us -> 11.9 us  [swap(): return lax.ppermute(v, axis, [(0, 1), (1, 0)])]
    broadcast_in_dim x2 -> x1, local copies, waits for them, and re-layouts: 2.76 us -> 0.08 us  [shards(): jnp.sum(jnp.where(position[None, :] == wanted[:, None], slot_of[None, :],...]
  transfers between devices with their start and end apart: 21 -> 32, of which waited for: 21 -> 25; matrix products, arithmetic and copies ran while one was open for 6% -> 2% of each run, Pallas kernels for 0% -> 7%
where the time goes in v2:
time: 206 us; the launch traced here: 205 us
  waiting for transfers between devices  74.6 us (36%)
  starting transfers between devices  70.8 us (34%)
  local copies, waits for them, and re-layouts  18.6 us (9%)
  blocking collectives  17.8 us (9%)
  Pallas kernels  17.3 us (8%)
  other arithmetic  3.85 us (2%)
    ppermute x15, waiting for transfers between devices, line_send(): lax.ppermute(piece, 'z_lo', [(i, i ^ step) for i in range(4)])  25.4 us
    all_to_all x4, waiting for transfers between devices, all_to_all(): return lax.all_to_all(v, axes, split_axis=0, concat_axis=0, tiled=True)  21.9 us
    ppermute x15, starting transfers between devices, line_send(): lax.ppermute(piece, 'z_lo', [(i, i ^ step) for i in range(4)])  20.9 us
    all_to_all x4, starting transfers between devices, all_to_all(): return lax.all_to_all(v, axes, split_axis=0, concat_axis=0, tiled=True)  19.6 us
    all_to_all x1, blocking collectives, exchange(): got = lax.all_to_all(copies, YX, split_axis=0, concat_axis=0, tiled=True)  17.8 us
    pallas_call x19, Pallas kernels, call(): pl.pallas_call(body, out_shape=out_shape, in_specs=specs, out_specs=whole...  17.3 us
    unnamed x50, local copies, waits for them, and re-layouts  15.9 us
    all_to_all x1, starting transfers between devices, shards(): lax.all_to_all(bucket, GRP, split_axis=0, concat_axis=0, tiled=True)  13 us
  transfers between devices with their start and end apart: 32, of which 25 were waited for; matrix products, arithmetic and copies ran while one was open for 2% of the time, Pallas kernels for 7%

profile of v2, /device:TPU:32, one launch (start us, length us, event | category | flops | bytes accessed | tf_op | source)
XLA Modules:
  0.0 204.5 jit_solution(7618899598820921051)
XLA Ops:
  1.1 1.0 convolution_convert_fusion
  2.8 13.0 %all-to-all-start = ((bf16[32,2,1280]{2,1,0:T(2,128)(2,1)}), bf16[32,2,1280]{2,1,0:T(2,128)(2,1)S(1)}, u32[]{:S(2)}, u32[]{:S(2)}) async-start(bf16[32,2,1280]{2,1,0:T(2,128)(2,1)} %reshape.107), calls=%async_computation | async-start | bytes 327680 | tf_op jit(solution)/shard_map/all_to_all | solution.py:299
  16.7 1.8 collective-permute-start
  18.5 2.7 %collective-permute-start.1 = (bf16[16,512]{1,0:T(8,128)(2,1)S(1)}, bf16[16,512]{1,0:T(8,128)(2,1)S(1)}, u32[]{:S(2)}, u32[]{:S(2)}) collective-permute-start(bf16[16,512]{1,0:T(8,128)(2,1)S(1)} %get-tuple-element.52), channel_id=1, source_target_pairs={{0,16},{8,24},{16,0},{24,8},{1,17},{9,25},{17,1},{25,9},{2,18},{10... | collective-permute-start | bytes 49160 | tf_op jit(solution)/shard_map/ppermute | solution.py:321
  21.4 1.2 convert_reduce_fusion.1
  24.3 4.5 %all-to-all-done = bf16[32,2,1280]{2,1,0:T(2,128)(2,1)S(1)} async-done(((bf16[32,2,1280]{2,1,0:T(2,128)(2,1)}), bf16[32,2,1280]{2,1,0:T(2,128)(2,1)S(1)}, u32[]{:S(2)}, u32[]{:S(2)}) %all-to-all-start) | async-done | bytes 163872 | tf_op jit(solution)/shard_map/all_to_all | solution.py:299
  28.9 0.9 copy-done.16
  29.8 0.9 copy-done.17
  31.6 2.7 %collective-permute-start.3 = (bf16[48,1024]{1,0:T(8,128)(2,1)S(1)}, bf16[48,1024]{1,0:T(8,128)(2,1)S(1)}, u32[]{:S(2)}, u32[]{:S(2)}) collective-permute-start(bf16[48,1024]{1,0:T(8,128)(2,1)S(1)} %shard_map.128.near_ref.tok_ref), channel_id=1, source_target_pairs={{0,128},{128,0},{1,129},{129,1},{2,130},{130,2},{3,131},{131,3},{4... | collective-permute-start | bytes 294920 | tf_op jit(solution)/shard_map/ppermute | solution.py:44
  34.3 7.0 %collective-permute-done.3.far_ref.tok_ref = bf16[48,1024]{1,0:T(8,128)(2,1)S(1)} collective-permute-done((bf16[48,1024]{1,0:T(8,128)(2,1)S(1)}, bf16[48,1024]{1,0:T(8,128)(2,1)S(1)}, u32[]{:S(2)}, u32[]{:S(2)}) %collective-permute-start.3) | collective-permute-done | bytes 98336 | tf_op jit(solution)/shard_map/ppermute | solution.py:44
  42.0 17.8 %all_to_all.30 = bf16[16,32,1024]{2,1,0:T(8,128)(2,1)S(1)} all-to-all(bf16[16,32,1024]{2,1,0:T(8,128)(2,1)S(1)} %shard_map.129), channel_id=1, replica_groups=mesh['z_hi'=2,'y'=4,'x'=4,'z_lo'=4,'core'=2] {'y','x'}, dimensions={0} | all-to-all | bytes 2097152 | tf_op jit(solution)/shard_map/all_to_all | solution.py:53
  60.1 1.1 shard_map.130
  61.3 1.5 collective-permute-done.4.got_ref
  63.8 2.0 collective-permute-start.6
  65.9 1.0 collective-permute-start.7
  66.9 1.3 collective-permute-done.5
  68.2 2.3 %collective-permute-done.6 = bf16[64,512]{1,0:T(8,128)(2,1)S(1)} collective-permute-done((bf16[64,512]{1,0:T(8,128)(2,1)S(1)}, bf16[64,512]{1,0:T(8,128)(2,1)S(1)}, u32[]{:S(2)}, u32[]{:S(2)}) %collective-permute-start.6) | collective-permute-done | bytes 65568 | tf_op jit(solution)/shard_map/ppermute | solution.py:150
  70.5 2.3 %collective-permute-done.7 = bf16[64,512]{1,0:T(8,128)(2,1)S(1)} collective-permute-done((bf16[64,512]{1,0:T(8,128)(2,1)S(1)}, bf16[64,512]{1,0:T(8,128)(2,1)S(1)}, u32[]{:S(2)}, u32[]{:S(2)}) %collective-permute-start.7) | collective-permute-done | bytes 65568 | tf_op jit(solution)/shard_map/ppermute | solution.py:150
  72.9 2.1 %collective-permute-start.9 = (bf16[64,512]{1,0:T(8,128)(2,1)S(1)}, bf16[64,512]{1,0:T(8,128)(2,1)S(1)}, u32[]{:S(2)}, u32[]{:S(2)}) collective-permute-start(bf16[64,512]{1,0:T(8,128)(2,1)S(1)} %add_convert_fusion.1), channel_id=1, source_target_pairs={{0,128},{1,0},{2,160},{3,32},{4,192},{5,64},{6,224},{7,96},{8,136}... | collective-permute-start | bytes 196616 | tf_op jit(solution)/shard_map/ppermute | solution.py:346
  75.0 4.5 %collective-permute-done.9.attn_ref = bf16[64,512]{1,0:T(8,128)(2,1)S(1)} collective-permute-done((bf16[64,512]{1,0:T(8,128)(2,1)S(1)}, bf16[64,512]{1,0:T(8,128)(2,1)S(1)}, u32[]{:S(2)}, u32[]{:S(2)}) %collective-permute-start.9) | collective-permute-done | bytes 65568 | tf_op jit(solution)/shard_map/ppermute | solution.py:346
  80.5 1.0 copy-done.6
  81.5 4.3 %all-to-all-start.3 = ((bf16[16,64,512]{2,1,0:T(8,128)(2,1)}), bf16[16,64,512]{2,1,0:T(8,128)(2,1)}, u32[]{:S(2)}, u32[]{:S(2)}) async-start(bf16[16,64,512]{2,1,0:T(8,128)(2,1)} %copy-done.6), calls=%async_computation.3 | async-start | bytes 2097152 | tf_op jit(solution)/shard_map/all_to_all | solution.py:258
  85.9 4.1 %collective-permute-start.8 = (bf16[64,512]{1,0:T(8,128)(2,1)}, bf16[64,512]{1,0:T(8,128)(2,1)S(1)}, u32[]{:S(2)}, u32[]{:S(2)}) collective-permute-start(bf16[64,512]{1,0:T(8,128)(2,1)} %copy-done.23), channel_id=1, source_target_pairs={{0,0},{1,128},{2,32},{3,160},{4,64},{5,192},{6,96},{7,224},{8,8},{... | collective-permute-start | bytes 196616 | tf_op jit(solution)/shard_map/ppermute | solution.py:347
  90.0 6.5 %collective-permute-done.8.attn_ref = bf16[64,512]{1,0:T(8,128)(2,1)S(1)} collective-permute-done((bf16[64,512]{1,0:T(8,128)(2,1)}, bf16[64,512]{1,0:T(8,128)(2,1)S(1)}, u32[]{:S(2)}, u32[]{:S(2)}) %collective-permute-start.8) | collective-permute-done | bytes 65568 | tf_op jit(solution)/shard_map/ppermute | solution.py:347
  96.7 1.0 copy-done.5
  97.6 5.0 %all-to-all-done.3 = bf16[16,64,512]{2,1,0:T(8,128)(2,1)} async-done(((bf16[16,64,512]{2,1,0:T(8,128)(2,1)}), bf16[16,64,512]{2,1,0:T(8,128)(2,1)}, u32[]{:S(2)}, u32[]{:S(2)}) %all-to-all-start.3) | async-done | bytes 1048608 | tf_op jit(solution)/shard_map/all_to_all | solution.py:258
  102.7 4.3 %all-to-all-start.2 = ((bf16[16,64,512]{2,1,0:T(8,128)(2,1)}), bf16[16,64,512]{2,1,0:T(8,128)(2,1)}, u32[]{:S(2)}, u32[]{:S(2)}) async-start(bf16[16,64,512]{2,1,0:T(8,128)(2,1)} %copy-done.5), calls=%async_computation.2 | async-start | bytes 2097152 | tf_op jit(solution)/shard_map/all_to_all | solution.py:258
  107.1 2.0 copy-done.1
  109.0 4.0 %shard_map.134 = (bf16[128,1792]{1,0:T(8,128)(2,1)S(1)}, bf16[128,1792]{1,0:T(8,128)(2,1)S(1)}, f32[8,128]{1,0:T(8,128)}) custom-call(s32[1]{0:T(128)} %bitcast.15.core, bf16[4,4,64,512]{3,2,1,0:T(8,128)(2,1)} %bitcast.18.rows_ref, bf16[1,2048]{1,0:T(2,128)(2,1)S(1)} %reshape.116.gain_ref, bf16[832,2048]{1,0:T(8,128)(2,1)S(1)} %bitcast.33, ...), custom_call_target="tpu_custom_call" | custom-call | flops 1 | bytes 1 | tf_op jit(solution)/shard_map/pallas_call | solution.py:62
  113.0 1.8 collective-permute-done.10.got_ref
  116.4 5.7 %collective-permute-start.12 = (bf16[32,1792]{1,0:T(8,128)(2,1)}, bf16[32,1792]{1,0:T(8,128)(2,1)}, u32[]{:S(2)}, u32[]{:S(2)}) collective-permute-start(bf16[32,1792]{1,0:T(8,128)(2,1)} %get-tuple-element.72), channel_id=1, source_target_pairs={{0,4},{2,6},{4,0},{6,2},{1,5},{3,7},{5,1},{7,3},{8,12},{10,14},{12... | collective-permute-start | bytes 344072 | tf_op jit(solution)/shard_map/ppermute | solution.py:150
  122.7 1.4 all-to-all-done.2
  124.0 2.0 copy-done.2
  126.0 3.8 %shard_map.136 = (bf16[128,1792]{1,0:T(8,128)(2,1)S(1)}, bf16[128,1792]{1,0:T(8,128)(2,1)S(1)}, f32[8,128]{1,0:T(8,128)S(1)}) custom-call(s32[1]{0:T(128)} %bitcast.15.core, bf16[4,4,64,512]{3,2,1,0:T(8,128)(2,1)} %bitcast.12.rows_ref, bf16[1,2048]{1,0:T(2,128)(2,1)S(1)} %reshape.116.gain_ref, bf16[832,2048]{1,0:T(8,128)(2,1)S(1)} %bitcast.34, ...), custom_call_target="tpu_custom_call" | custom-call | flops 1 | bytes 1 | tf_op jit(solution)/shard_map/pallas_call | solution.py:62
  129.8 1.0 collective-permute-done.12.two_ref
  130.9 2.6 %collective-permute-done.13.three_ref = bf16[32,1792]{1,0:T(8,128)(2,1)} collective-permute-done((bf16[32,1792]{1,0:T(8,128)(2,1)}, bf16[32,1792]{1,0:T(8,128)(2,1)}, u32[]{:S(2)}, u32[]{:S(2)}) %collective-permute-start.13) | collective-permute-done | bytes 114720 | tf_op jit(solution)/shard_map/ppermute | solution.py:150
  133.5 1.2 shard_map.137.own_ref
  134.8 1.6 collective-permute-start.16
  137.0 1.3 collective-permute-start.14
  138.5 3.1 %collective-permute-done.16.three_ref = bf16[32,832]{1,0:T(8,128)(2,1)S(1)} collective-permute-done((bf16[32,832]{1,0:T(8,128)(2,1)S(1)}, bf16[32,832]{1,0:T(8,128)(2,1)S(1)}, u32[]{:S(2)}, u32[]{:S(2)}) %collective-permute-start.16) | collective-permute-done | bytes 53280 | tf_op jit(solution)/shard_map/ppermute | solution.py:150
  142.2 2.3 %collective-permute-start.19 = (bf16[32,1792]{1,0:T(8,128)(2,1)S(1)}, bf16[32,1792]{1,0:T(8,128)(2,1)S(1)}, u32[]{:S(2)}, u32[]{:S(2)}) collective-permute-start(bf16[32,1792]{1,0:T(8,128)(2,1)S(1)} %get-tuple-element.81), channel_id=1, source_target_pairs={{0,2},{2,0},{4,6},{6,4},{1,3},{3,1},{5,7},{7,5},{8,10},{10,8},{12,... | collective-permute-start | bytes 344072 | tf_op jit(solution)/shard_map/ppermute | solution.py:150
  144.5 1.0 collective-permute-start.20
  146.1 1.3 shard_map.140
  147.4 2.2 %collective-permute-done.19.one_ref = bf16[32,1792]{1,0:T(8,128)(2,1)S(1)} collective-permute-done((bf16[32,1792]{1,0:T(8,128)(2,1)S(1)}, bf16[32,1792]{1,0:T(8,128)(2,1)S(1)}, u32[]{:S(2)}, u32[]{:S(2)}) %collective-permute-start.19) | collective-permute-done | bytes 114720 | tf_op jit(solution)/shard_map/ppermute | solution.py:150
  149.5 4.4 %collective-permute-done.20.two_ref = bf16[32,1792]{1,0:T(8,128)(2,1)S(1)} collective-permute-done((bf16[32,1792]{1,0:T(8,128)(2,1)S(1)}, bf16[32,1792]{1,0:T(8,128)(2,1)S(1)}, u32[]{:S(2)}, u32[]{:S(2)}) %collective-permute-start.20) | collective-permute-done | bytes 114720 | tf_op jit(solution)/shard_map/ppermute | solution.py:150
  154.6 2.2 %collective-permute-done.21.three_ref = bf16[32,1792]{1,0:T(8,128)(2,1)S(1)} collective-permute-done((bf16[32,1792]{1,0:T(8,128)(2,1)S(1)}, bf16[32,1792]{1,0:T(8,128)(2,1)S(1)}, u32[]{:S(2)}, u32[]{:S(2)}) %collective-permute-start.21) | collective-permute-done | bytes 114720 | tf_op jit(solution)/shard_map/ppermute | solution.py:150
  157.5 7.1 %all-to-all-start.5 = ((bf16[16,16,2048]{2,1,0:T(8,128)(2,1)}), bf16[16,16,2048]{2,1,0:T(8,128)(2,1)}, u32[]{:S(2)}, u32[]{:S(2)}) async-start(bf16[16,16,2048]{2,1,0:T(8,128)(2,1)} %bitcast.38), calls=%async_computation.5 | async-start | bytes 2097152 | tf_op jit(solution)/shard_map/all_to_all | solution.py:258
  164.7 0.9 copy-done.13
  165.6 0.9 copy-done.19
  166.5 0.9 copy-done.21
  167.6 1.5 collective-permute-start.24
  169.1 1.1 collective-permute-start.23
  170.3 0.9 collective-permute-start.22
  171.2 1.9 collective-permute-done.24.three_ref
  173.1 1.2 collective-permute-done.23.two_ref
  174.6 1.5 collective-permute-done.25.other_ref
  176.0 1.7 shard_map.143
  177.8 1.0 copy-done.9
  178.7 3.4 %all-to-all-done.5.parts_ref = bf16[16,16,2048]{2,1,0:T(8,128)(2,1)} async-done(((bf16[16,16,2048]{2,1,0:T(8,128)(2,1)}), bf16[16,16,2048]{2,1,0:T(8,128)(2,1)}, u32[]{:S(2)}, u32[]{:S(2)}) %all-to-all-start.5) | async-done | bytes 1048608 | tf_op jit(solution)/shard_map/all_to_all | solution.py:258
  182.1 3.8 %all-to-all-start.4 = ((bf16[16,16,2048]{2,1,0:T(8,128)(2,1)}), bf16[16,16,2048]{2,1,0:T(8,128)(2,1)S(1)}, u32[]{:S(2)}, u32[]{:S(2)}) async-start(bf16[16,16,2048]{2,1,0:T(8,128)(2,1)} %bitcast.39), calls=%async_computation.4 | async-start | bytes 2097152 | tf_op jit(solution)/shard_map/all_to_all | solution.py:258
  185.9 1.4 shard_map.145
  187.3 3.4 %collective-permute-start.26 = (bf16[16,2048]{1,0:T(8,128)(2,1)S(1)}, bf16[16,2048]{1,0:T(8,128)(2,1)S(1)}, u32[]{:S(2)}, u32[]{:S(2)}) collective-permute-start(bf16[16,2048]{1,0:T(8,128)(2,1)S(1)} %shard_map.145), channel_id=1, source_target_pairs={{0,128},{128,0},{1,129},{129,1},{2,130},{130,2},{3,131},{131,3},{4... | collective-permute-start | bytes 196616 | tf_op jit(solution)/shard_map/ppermute | solution.py:44
  190.7 0.9 convert_bitcast_fusion
  191.6 12.1 %all-to-all-done.4.parts_ref = bf16[16,16,2048]{2,1,0:T(8,128)(2,1)S(1)} async-done(((bf16[16,16,2048]{2,1,0:T(8,128)(2,1)}), bf16[16,16,2048]{2,1,0:T(8,128)(2,1)S(1)}, u32[]{:S(2)}, u32[]{:S(2)}) %all-to-all-start.4) | async-done | bytes 1048608 | tf_op jit(solution)/shard_map/all_to_all | solution.py:258
  (93 shorter events, 15.4 us)
Async XLA Ops:
  0.0 60.1 %copy-start.7 = (bf16[1024,512]{1,0:T(8,128)(2,1)S(1)}, bf16[1024,512]{1,0:T(8,128)(2,1)}, u32[]{:S(2)}) copy-start(bf16[1024,512]{1,0:T(8,128)(2,1)} %weight_ref.3) | copy-start | bytes 3145732
  2.8 26.0 %all-to-all-start = ((bf16[32,2,1280]{2,1,0:T(2,128)(2,1)}), bf16[32,2,1280]{2,1,0:T(2,128)(2,1)S(1)}, u32[]{:S(2)}, u32[]{:S(2)}) async-start(bf16[32,2,1280]{2,1,0:T(2,128)(2,1)} %reshape.107), calls=%async_computation | async-start | bytes 327680 | tf_op jit(solution)/shard_map/all_to_all | solution.py:299
  15.8 0.8 copy-start.22
  16.7 12.2 %collective-permute-start = (bf16[16,512]{1,0:T(8,128)(2,1)S(1)}, bf16[16,512]{1,0:T(8,128)(2,1)S(1)}, u32[]{:S(2)}, u32[]{:S(2)}) collective-permute-start(bf16[16,512]{1,0:T(8,128)(2,1)S(1)} %get-tuple-element.51), channel_id=1, source_target_pairs={{0,8},{8,0},{16,24},{24,16},{1,9},{9,1},{17,25},{25,17},{2,10},{10... | collective-permute-start | bytes 49160 | tf_op jit(solution)/shard_map/ppermute | solution.py:321
  18.5 10.4 %collective-permute-start.1 = (bf16[16,512]{1,0:T(8,128)(2,1)S(1)}, bf16[16,512]{1,0:T(8,128)(2,1)S(1)}, u32[]{:S(2)}, u32[]{:S(2)}) collective-permute-start(bf16[16,512]{1,0:T(8,128)(2,1)S(1)} %get-tuple-element.52), channel_id=1, source_target_pairs={{0,16},{8,24},{16,0},{24,8},{1,17},{9,25},{17,1},{25,9},{2,18},{10... | collective-permute-start | bytes 49160 | tf_op jit(solution)/shard_map/ppermute | solution.py:321
  21.1 7.7 %collective-permute-start.2 = (bf16[16,512]{1,0:T(8,128)(2,1)S(1)}, bf16[16,512]{1,0:T(8,128)(2,1)S(1)}, u32[]{:S(2)}, u32[]{:S(2)}) collective-permute-start(bf16[16,512]{1,0:T(8,128)(2,1)S(1)} %get-tuple-element.53), channel_id=1, source_target_pairs={{0,24},{8,16},{16,8},{24,0},{1,25},{9,17},{17,9},{25,1},{2,26},{10... | collective-permute-start | bytes 49160 | tf_op jit(solution)/shard_map/ppermute | solution.py:321
  28.9 0.9 copy-start.16
  29.8 0.9 copy-start.17
  31.6 9.7 %collective-permute-start.3 = (bf16[48,1024]{1,0:T(8,128)(2,1)S(1)}, bf16[48,1024]{1,0:T(8,128)(2,1)S(1)}, u32[]{:S(2)}, u32[]{:S(2)}) collective-permute-start(bf16[48,1024]{1,0:T(8,128)(2,1)S(1)} %shard_map.128.near_ref.tok_ref), channel_id=1, source_target_pairs={{0,128},{128,0},{1,129},{129,1},{2,130},{130,2},{3,131},{131,3},{4... | collective-permute-start | bytes 294920 | tf_op jit(solution)/shard_map/ppermute | solution.py:44
  41.3 0.6 copy-start.10
  61.2 1.6 collective-permute-start.4
  63.4 4.8 %collective-permute-start.5 = (bf16[64,512]{1,0:T(8,128)(2,1)S(1)}, bf16[64,512]{1,0:T(8,128)(2,1)S(1)}, u32[]{:S(2)}, u32[]{:S(2)}) collective-permute-start(bf16[64,512]{1,0:T(8,128)(2,1)S(1)} %get-tuple-element.63), channel_id=1, source_target_pairs={{0,2},{2,0},{4,6},{6,4},{1,3},{3,1},{5,7},{7,5},{8,10},{10,8},{12,... | collective-permute-start | bytes 196616 | tf_op jit(solution)/shard_map/ppermute | solution.py:150
  63.8 6.7 %collective-permute-start.6 = (bf16[64,512]{1,0:T(8,128)(2,1)S(1)}, bf16[64,512]{1,0:T(8,128)(2,1)S(1)}, u32[]{:S(2)}, u32[]{:S(2)}) collective-permute-start(bf16[64,512]{1,0:T(8,128)(2,1)S(1)} %get-tuple-element.64), channel_id=1, source_target_pairs={{0,4},{2,6},{4,0},{6,2},{1,5},{3,7},{5,1},{7,3},{8,12},{10,14},{12... | collective-permute-start | bytes 196616 | tf_op jit(solution)/shard_map/ppermute | solution.py:150
  65.9 7.0 %collective-permute-start.7 = (bf16[64,512]{1,0:T(8,128)(2,1)S(1)}, bf16[64,512]{1,0:T(8,128)(2,1)S(1)}, u32[]{:S(2)}, u32[]{:S(2)}) collective-permute-start(bf16[64,512]{1,0:T(8,128)(2,1)S(1)} %get-tuple-element.65), channel_id=1, source_target_pairs={{0,6},{2,4},{4,2},{6,0},{1,7},{3,5},{5,3},{7,1},{8,14},{10,12},{12... | collective-permute-start | bytes 196616 | tf_op jit(solution)/shard_map/ppermute | solution.py:150
  72.9 34.1 %copy-start.24 = (bf16[2048]{0:T(1024)(128)(2,1)S(1)}, bf16[2048]{0:T(1024)(128)(2,1)}, u32[]{:S(2)}) copy-start(bf16[2048]{0:T(1024)(128)(2,1)} %param.22) | copy-start | bytes 12292
  72.9 2.1 %copy-start.23 = (bf16[64,512]{1,0:T(8,128)(2,1)}, bf16[64,512]{1,0:T(8,128)(2,1)S(1)}, u32[]{:S(2)}) copy-start(bf16[64,512]{1,0:T(8,128)(2,1)S(1)} %add_convert_fusion.1) | copy-start | bytes 196612
  72.9 34.1 %copy-start = (bf16[2048,832]{0,1:T(8,128)(2,1)S(1)}, bf16[2048,832]{0,1:T(8,128)(2,1)}, u32[]{:S(2)}) copy-start(bf16[2048,832]{0,1:T(8,128)(2,1)} %param.23) | copy-start | bytes 10223620
  72.9 6.6 %collective-permute-start.9 = (bf16[64,512]{1,0:T(8,128)(2,1)S(1)}, bf16[64,512]{1,0:T(8,128)(2,1)S(1)}, u32[]{:S(2)}, u32[]{:S(2)}) collective-permute-start(bf16[64,512]{1,0:T(8,128)(2,1)S(1)} %add_convert_fusion.1), channel_id=1, source_target_pairs={{0,128},{1,0},{2,160},{3,32},{4,192},{5,64},{6,224},{7,96},{8,136}... | collective-permute-start | bytes 196616 | tf_op jit(solution)/shard_map/ppermute | solution.py:346
  79.5 0.9 copy-start.11
  80.5 1.0 copy-start.6
  81.5 21.1 %all-to-all-start.3 = ((bf16[16,64,512]{2,1,0:T(8,128)(2,1)}), bf16[16,64,512]{2,1,0:T(8,128)(2,1)}, u32[]{:S(2)}, u32[]{:S(2)}) async-start(bf16[16,64,512]{2,1,0:T(8,128)(2,1)} %copy-done.6), calls=%async_computation.3 | async-start | bytes 2097152 | tf_op jit(solution)/shard_map/all_to_all | solution.py:258
  85.9 10.6 %collective-permute-start.8 = (bf16[64,512]{1,0:T(8,128)(2,1)}, bf16[64,512]{1,0:T(8,128)(2,1)S(1)}, u32[]{:S(2)}, u32[]{:S(2)}) collective-permute-start(bf16[64,512]{1,0:T(8,128)(2,1)} %copy-done.23), channel_id=1, source_target_pairs={{0,0},{1,128},{2,32},{3,160},{4,64},{5,192},{6,96},{7,224},{8,8},{... | collective-permute-start | bytes 196616 | tf_op jit(solution)/shard_map/ppermute | solution.py:347
  96.6 1.0 copy-start.5
  102.7 21.4 %all-to-all-start.2 = ((bf16[16,64,512]{2,1,0:T(8,128)(2,1)}), bf16[16,64,512]{2,1,0:T(8,128)(2,1)}, u32[]{:S(2)}, u32[]{:S(2)}) async-start(bf16[16,64,512]{2,1,0:T(8,128)(2,1)} %copy-done.5), calls=%async_computation.2 | async-start | bytes 2097152 | tf_op jit(solution)/shard_map/all_to_all | solution.py:258
  107.0 2.0 copy-start.1
  113.0 1.8 collective-permute-start.10
  115.6 0.7 copy-start.14
  116.3 13.5 %collective-permute-start.11 = (bf16[32,1792]{1,0:T(8,128)(2,1)}, bf16[32,1792]{1,0:T(8,128)(2,1)S(1)}, u32[]{:S(2)}, u32[]{:S(2)}) collective-permute-start(bf16[32,1792]{1,0:T(8,128)(2,1)} %get-tuple-element.71), channel_id=1, source_target_pairs={{0,2},{2,0},{4,6},{6,4},{1,3},{3,1},{5,7},{7,5},{8,10},{10,8},{12,... | collective-permute-start | bytes 344072 | tf_op jit(solution)/shard_map/ppermute | solution.py:150
  116.4 14.5 %collective-permute-start.12 = (bf16[32,1792]{1,0:T(8,128)(2,1)}, bf16[32,1792]{1,0:T(8,128)(2,1)}, u32[]{:S(2)}, u32[]{:S(2)}) collective-permute-start(bf16[32,1792]{1,0:T(8,128)(2,1)} %get-tuple-element.72), channel_id=1, source_target_pairs={{0,4},{2,6},{4,0},{6,2},{1,5},{3,7},{5,1},{7,3},{8,12},{10,14},{12... | collective-permute-start | bytes 344072 | tf_op jit(solution)/shard_map/ppermute | solution.py:150
  122.1 11.4 %collective-permute-start.13 = (bf16[32,1792]{1,0:T(8,128)(2,1)}, bf16[32,1792]{1,0:T(8,128)(2,1)}, u32[]{:S(2)}, u32[]{:S(2)}) collective-permute-start(bf16[32,1792]{1,0:T(8,128)(2,1)} %get-tuple-element.73), channel_id=1, source_target_pairs={{0,6},{2,4},{4,2},{6,0},{1,7},{3,5},{5,3},{7,1},{8,14},{10,12},{12... | collective-permute-start | bytes 344072 | tf_op jit(solution)/shard_map/ppermute | solution.py:150
  124.0 2.0 copy-start.2
  126.0 7.5 %copy-start.15 = (f32[32,1792]{1,0:T(8,128)S(1)}, f32[32,1792]{1,0:T(8,128)}, u32[]{:S(2)}) copy-start(f32[32,1792]{1,0:T(8,128)} %copy-done.14) | copy-start | bytes 688132
  126.0 20.1 %copy-start.3 = (bf16[832,2048]{1,0:T(8,128)(2,1)S(1)}, bf16[832,2048]{1,0:T(8,128)(2,1)}, u32[]{:S(2)}) copy-start(bf16[832,2048]{1,0:T(8,128)(2,1)} %weight_ref.5) | copy-start | bytes 10223620
  134.7 3.7 %collective-permute-start.17 = (bf16[128,1792]{1,0:T(8,128)(2,1)S(1)}, bf16[128,1792]{1,0:T(8,128)(2,1)S(1)}, u32[]{:S(2)}, u32[]{:S(2)}) collective-permute-start(bf16[128,1792]{1,0:T(8,128)(2,1)S(1)} %get-tuple-element.77), channel_id=1, source_target_pairs={{0,1},{1,0},{2,3},{3,2},{4,5},{5,4},{6,7},{7,6},{8,9},{9,8},{10,11... | collective-permute-start | bytes 1376264 | tf_op jit(solution)/shard_map/ppermute | solution.py:44
  134.8 6.8 %collective-permute-start.16 = (bf16[32,832]{1,0:T(8,128)(2,1)S(1)}, bf16[32,832]{1,0:T(8,128)(2,1)S(1)}, u32[]{:S(2)}, u32[]{:S(2)}) collective-permute-start(bf16[32,832]{1,0:T(8,128)(2,1)S(1)} %shard_map.137.own_ref), channel_id=1, source_target_pairs={{0,6},{2,4},{4,2},{6,0},{1,7},{3,5},{5,3},{7,1},{8,14},{10,12},{12... | collective-permute-start | bytes 159752 | tf_op jit(solution)/shard_map/ppermute | solution.py:150
  136.4 5.6 %collective-permute-start.15 = (bf16[32,832]{1,0:T(8,128)(2,1)S(1)}, bf16[32,832]{1,0:T(8,128)(2,1)S(1)}, u32[]{:S(2)}, u32[]{:S(2)}) collective-permute-start(bf16[32,832]{1,0:T(8,128)(2,1)S(1)} %shard_map.137.own_ref), channel_id=1, source_target_pairs={{0,4},{2,6},{4,0},{6,2},{1,5},{3,7},{5,1},{7,3},{8,12},{10,14},{12... | collective-permute-start | bytes 159752 | tf_op jit(solution)/shard_map/ppermute | solution.py:150
  137.0 5.0 %collective-permute-start.14 = (bf16[32,832]{1,0:T(8,128)(2,1)S(1)}, bf16[32,832]{1,0:T(8,128)(2,1)S(1)}, u32[]{:S(2)}, u32[]{:S(2)}) collective-permute-start(bf16[32,832]{1,0:T(8,128)(2,1)S(1)} %shard_map.137.own_ref), channel_id=1, source_target_pairs={{0,2},{2,0},{4,6},{6,4},{1,3},{3,1},{5,7},{7,5},{8,10},{10,8},{12,... | collective-permute-start | bytes 159752 | tf_op jit(solution)/shard_map/ppermute | solution.py:150
  138.5 7.6 %copy-start.12 = (f32[32,1792]{1,0:T(8,128)}, f32[32,1792]{1,0:T(8,128)S(1)}, u32[]{:S(2)}) copy-start(f32[32,1792]{1,0:T(8,128)S(1)} %get-tuple-element.84.own_ref) | copy-start | bytes 688132
  142.1 3.9 %collective-permute-start.18 = (bf16[128,832]{1,0:T(8,128)(2,1)S(1)}, bf16[128,832]{1,0:T(8,128)(2,1)S(1)}, u32[]{:S(2)}, u32[]{:S(2)}) collective-permute-start(bf16[128,832]{1,0:T(8,128)(2,1)S(1)} %shard_map.139.own_ref), channel_id=1, source_target_pairs={{0,1},{1,0},{2,3},{3,2},{4,5},{5,4},{6,7},{7,6},{8,9},{9,8},{10,11... | collective-permute-start | bytes 638984 | tf_op jit(solution)/shard_map/ppermute | solution.py:44
  142.2 7.3 %collective-permute-start.19 = (bf16[32,1792]{1,0:T(8,128)(2,1)S(1)}, bf16[32,1792]{1,0:T(8,128)(2,1)S(1)}, u32[]{:S(2)}, u32[]{:S(2)}) collective-permute-start(bf16[32,1792]{1,0:T(8,128)(2,1)S(1)} %get-tuple-element.81), channel_id=1, source_target_pairs={{0,2},{2,0},{4,6},{6,4},{1,3},{3,1},{5,7},{7,5},{8,10},{10,8},{12,... | collective-permute-start | bytes 344072 | tf_op jit(solution)/shard_map/ppermute | solution.py:150
  144.5 9.5 %collective-permute-start.20 = (bf16[32,1792]{1,0:T(8,128)(2,1)S(1)}, bf16[32,1792]{1,0:T(8,128)(2,1)S(1)}, u32[]{:S(2)}, u32[]{:S(2)}) collective-permute-start(bf16[32,1792]{1,0:T(8,128)(2,1)S(1)} %get-tuple-element.82), channel_id=1, source_target_pairs={{0,4},{2,6},{4,0},{6,2},{1,5},{3,7},{5,1},{7,3},{8,12},{10,14},{12... | collective-permute-start | bytes 344072 | tf_op jit(solution)/shard_map/ppermute | solution.py:150
  145.5 30.5 %copy-start.4 = (bf16[832,2048]{1,0:T(8,128)(2,1)S(1)}, bf16[832,2048]{1,0:T(8,128)(2,1)}, u32[]{:S(2)}) copy-start(bf16[832,2048]{1,0:T(8,128)(2,1)} %weight_ref.5) | copy-start | bytes 10223620
  145.5 11.3 %collective-permute-start.21 = (bf16[32,1792]{1,0:T(8,128)(2,1)S(1)}, bf16[32,1792]{1,0:T(8,128)(2,1)S(1)}, u32[]{:S(2)}, u32[]{:S(2)}) collective-permute-start(bf16[32,1792]{1,0:T(8,128)(2,1)S(1)} %get-tuple-element.83), channel_id=1, source_target_pairs={{0,6},{2,4},{4,2},{6,0},{1,7},{3,5},{5,3},{7,1},{8,14},{10,12},{12... | collective-permute-start | bytes 344072 | tf_op jit(solution)/shard_map/ppermute | solution.py:150
  147.3 10.2 %copy-start.8 = (bf16[256,2048]{1,0:T(8,128)(2,1)}, bf16[256,2048]{1,0:T(8,128)(2,1)S(1)}, u32[]{:S(2)}) copy-start(bf16[256,2048]{1,0:T(8,128)(2,1)S(1)} %get-tuple-element.90) | copy-start | bytes 3145732
  154.0 0.7 copy-start.18
  156.9 0.7 copy-start.20
  157.5 24.6 %all-to-all-start.5 = ((bf16[16,16,2048]{2,1,0:T(8,128)(2,1)}), bf16[16,16,2048]{2,1,0:T(8,128)(2,1)}, u32[]{:S(2)}, u32[]{:S(2)}) async-start(bf16[16,16,2048]{2,1,0:T(8,128)(2,1)} %bitcast.38), calls=%async_computation.5 | async-start | bytes 2097152 | tf_op jit(solution)/shard_map/all_to_all | solution.py:258
  164.7 0.9 copy-start.13
  165.6 0.9 copy-start.19
  166.5 0.9 copy-start.21
  167.6 5.5 %collective-permute-start.24 = (bf16[32,832]{1,0:T(8,128)(2,1)S(1)}, bf16[32,832]{1,0:T(8,128)(2,1)S(1)}, u32[]{:S(2)}, u32[]{:S(2)}) collective-permute-start(bf16[32,832]{1,0:T(8,128)(2,1)S(1)} %shard_map.141.own_ref), channel_id=1, source_target_pairs={{0,6},{2,4},{4,2},{6,0},{1,7},{3,5},{5,3},{7,1},{8,14},{10,12},{12... | collective-permute-start | bytes 159752 | tf_op jit(solution)/shard_map/ppermute | solution.py:150
  169.1 5.2 %collective-permute-start.23 = (bf16[32,832]{1,0:T(8,128)(2,1)S(1)}, bf16[32,832]{1,0:T(8,128)(2,1)S(1)}, u32[]{:S(2)}, u32[]{:S(2)}) collective-permute-start(bf16[32,832]{1,0:T(8,128)(2,1)S(1)} %shard_map.141.own_ref), channel_id=1, source_target_pairs={{0,4},{2,6},{4,0},{6,2},{1,5},{3,7},{5,1},{7,3},{8,12},{10,14},{12... | collective-permute-start | bytes 159752 | tf_op jit(solution)/shard_map/ppermute | solution.py:150
  170.3 4.2 %collective-permute-start.22 = (bf16[32,832]{1,0:T(8,128)(2,1)S(1)}, bf16[32,832]{1,0:T(8,128)(2,1)S(1)}, u32[]{:S(2)}, u32[]{:S(2)}) collective-permute-start(bf16[32,832]{1,0:T(8,128)(2,1)S(1)} %shard_map.141.own_ref), channel_id=1, source_target_pairs={{0,2},{2,0},{4,6},{6,4},{1,3},{3,1},{5,7},{7,5},{8,10},{10,8},{12,... | collective-permute-start | bytes 159752 | tf_op jit(solution)/shard_map/ppermute | solution.py:150
  174.5 1.6 collective-permute-start.25
  177.8 1.0 copy-start.9
  182.1 21.6 %all-to-all-start.4 = ((bf16[16,16,2048]{2,1,0:T(8,128)(2,1)}), bf16[16,16,2048]{2,1,0:T(8,128)(2,1)S(1)}, u32[]{:S(2)}, u32[]{:S(2)}) async-start(bf16[16,16,2048]{2,1,0:T(8,128)(2,1)} %bitcast.39), calls=%async_computation.4 | async-start | bytes 2097152 | tf_op jit(solution)/shard_map/all_to_all | solution.py:258
  187.3 16.6 %collective-permute-start.26 = (bf16[16,2048]{1,0:T(8,128)(2,1)S(1)}, bf16[16,2048]{1,0:T(8,128)(2,1)S(1)}, u32[]{:S(2)}, u32[]{:S(2)}) collective-permute-start(bf16[16,2048]{1,0:T(8,128)(2,1)S(1)} %shard_map.145), channel_id=1, source_target_pairs={{0,128},{128,0},{1,129},{129,1},{2,130},{130,2},{3,131},{131,3},{4... | collective-permute-start | bytes 196616 | tf_op jit(solution)/shard_map/ppermute | solution.py:44

commit v3 on v2

--- a/solution.py
+++ b/solution.py
@@ -20,6 +20,7 @@
 BF = jnp.bfloat16
 F32 = jnp.float32
 MIB = 1 << 20
+LONG = 30_000_000_000
 PAD = 896
 
 
@@ -54,7 +55,7 @@
     return lax.optimization_barrier((got, *others))
 
 
-def call(body, out_shape, *operands, scalars=(), streamed=(), scratch=(), limit=12):
+def call(body, out_shape, *operands, scalars=(), streamed=(), scratch=(), limit=12, weight=1):
     whole = pl.BlockSpec(memory_space=pltpu.VMEM)
     single = not isinstance(out_shape, (list, tuple))
     specs = [pl.BlockSpec(memory_space=pltpu.SMEM)] * len(scalars) + [whole] * len(operands)
@@ -66,7 +67,7 @@
         out_specs=whole if single else [whole] * len(out_shape),
         scratch_shapes=list(scratch),
         compiler_params=pltpu.CompilerParams(vmem_limit_bytes=limit * MIB),
-        cost_estimate=pl.CostEstimate(flops=1, bytes_accessed=1, transcendentals=0),
+        cost_estimate=pl.CostEstimate(flops=weight, bytes_accessed=1, transcendentals=0),
     )(*[jnp.reshape(s, (1,)).astype(jnp.int32) for s in scalars], *operands, *streamed)
 
 
@@ -240,7 +241,7 @@
 
 
 def hidden_gather(pieces, hid, mark):
-    hidden = call(hidden_body, shape((pieces[0].shape[0], hid), BF), *pieces, mark)
+    hidden = call(hidden_body, shape((pieces[0].shape[0], hid), BF), *pieces, mark, weight=LONG)
     return [hidden] + line_send([hidden] * 3)
 
 
@@ -363,7 +364,6 @@
     near_pieces, near_sent = line_reduce(near_keep, swap(near_send, "core"), z_lo)
     far_hidden = [far_hidden] + line_send([far_hidden] * 3)
     far_down, far_done = down_project(far_hidden, down_weight, z_lo, core, near_sent)
-    far_down, near_pieces = lax.optimization_barrier((far_down, near_pieces))
     far_parts = all_to_all(far_down.reshape(plane, rows_dev, width), YX)
     near_hidden = hidden_gather(near_pieces, hid, far_done)
     near_down, near_done = down_project(near_hidden, down_weight, z_lo, core, far_done)

time: 206 us -> 197 us (0.956)
  local copies, waits for them, and re-layouts: 18.6 us -> 13.5 us
  waiting for transfers between devices: 74.6 us -> 69.8 us
    ppermute x15, waiting for transfers between devices: 25.4 us -> 18.9 us  [line_send(): lax.ppermute(piece, 'z_lo', [(i, i ^ step) for i in range(4)])]
    unnamed x50 -> x32, local copies, waits for them, and re-layouts: 15.9 us -> 10.7 us
  transfers between devices with their start and end apart: 32 -> 32, of which waited for: 25 -> 22; matrix products, arithmetic and copies ran while one was open for 2% -> 2% of each run, Pallas kernels for 7% -> 7%
where the time goes in v3:
time: 197 us; the launch traced here: 196 us
  starting transfers between devices  71 us (36%)
  waiting for transfers between devices  69.8 us (35%)
  blocking collectives  17.8 us (9%)
  Pallas kernels  17.7 us (9%)
  local copies, waits for them, and re-layouts  13.5 us (7%)
  other arithmetic  4.48 us (2%)
    all_to_all x4, waiting for transfers between devices, all_to_all(): return lax.all_to_all(v, axes, split_axis=0, concat_axis=0, tiled=True)  23.5 us
    ppermute x15, starting transfers between devices, line_send(): lax.ppermute(piece, 'z_lo', [(i, i ^ step) for i in range(4)])  21.3 us
    all_to_all x4, starting transfers between devices, all_to_all(): return lax.all_to_all(v, axes, split_axis=0, concat_axis=0, tiled=True)  19.4 us
    ppermute x15, waiting for transfers between devices, line_send(): lax.ppermute(piece, 'z_lo', [(i, i ^ step) for i in range(4)])  18.9 us
    all_to_all x1, blocking collectives, exchange(): got = lax.all_to_all(copies, YX, split_axis=0, concat_axis=0, tiled=True)  17.8 us
    pallas_call x19, Pallas kernels, call(): pl.pallas_call(body, out_shape=out_shape, in_specs=specs, out_specs=whole...  17.7 us
    all_to_all x1, starting transfers between devices, shards(): lax.all_to_all(bucket, GRP, split_axis=0, concat_axis=0, tiled=True)  13 us
    ppermute x7, waiting for transfers between devices, swap(): return lax.ppermute(v, axis, [(0, 1), (1, 0)])  11.8 us
  transfers between devices with their start and end apart: 32, of which 22 were waited for; matrix products, arithmetic and copies ran while one was open for 2% of the time, Pallas kernels for 7%

profile of v3, /device:TPU:32, one launch (start us, length us, event | category | flops | bytes accessed | tf_op | source)
XLA Modules:
  0.0 195.7 jit_solution(4784855486374593190)
XLA Ops:
  0.0 0.8 reshape.106
  1.1 1.0 convolution_convert_fusion
  2.0 0.7 reshape.107
  2.8 13.0 %all-to-all-start = ((bf16[32,2,1280]{2,1,0:T(2,128)(2,1)}), bf16[32,2,1280]{2,1,0:T(2,128)(2,1)S(1)}, u32[]{:S(2)}, u32[]{:S(2)}) async-start(bf16[32,2,1280]{2,1,0:T(2,128)(2,1)} %reshape.107), calls=%async_computation | async-start | bytes 327680 | tf_op jit(solution)/shard_map/all_to_all | solution.py:300
  15.8 0.8 copy-done.14
  16.7 1.8 collective-permute-start
  18.5 2.7 %collective-permute-start.1 = (bf16[16,512]{1,0:T(8,128)(2,1)S(1)}, bf16[16,512]{1,0:T(8,128)(2,1)S(1)}, u32[]{:S(2)}, u32[]{:S(2)}) collective-permute-start(bf16[16,512]{1,0:T(8,128)(2,1)S(1)} %get-tuple-element.47), channel_id=1, source_target_pairs={{0,16},{8,24},{16,0},{24,8},{1,17},{9,25},{17,1},{25,9},{2,18},{10... | collective-permute-start | bytes 49160 | tf_op jit(solution)/shard_map/ppermute | solution.py:322
  21.4 1.2 convert_reduce_fusion.1
  23.5 0.7 copy.26.len_ref
  24.3 4.5 %all-to-all-done = bf16[32,2,1280]{2,1,0:T(2,128)(2,1)S(1)} async-done(((bf16[32,2,1280]{2,1,0:T(2,128)(2,1)}), bf16[32,2,1280]{2,1,0:T(2,128)(2,1)S(1)}, u32[]{:S(2)}, u32[]{:S(2)}) %all-to-all-start) | async-done | bytes 163872 | tf_op jit(solution)/shard_map/all_to_all | solution.py:300
  28.9 0.9 copy-done.12
  29.8 0.9 copy-done.13
  30.7 0.9 shard_map.128.near_ref.tok_ref
  31.6 2.7 %collective-permute-start.3 = (bf16[48,1024]{1,0:T(8,128)(2,1)S(1)}, bf16[48,1024]{1,0:T(8,128)(2,1)S(1)}, u32[]{:S(2)}, u32[]{:S(2)}) collective-permute-start(bf16[48,1024]{1,0:T(8,128)(2,1)S(1)} %shard_map.128.near_ref.tok_ref), channel_id=1, source_target_pairs={{0,128},{128,0},{1,129},{129,1},{2,130},{130,2},{3,131},{131,3},{4... | collective-permute-start | bytes 294920 | tf_op jit(solution)/shard_map/ppermute | solution.py:45
  34.3 7.0 %collective-permute-done.3.far_ref.tok_ref = bf16[48,1024]{1,0:T(8,128)(2,1)S(1)} collective-permute-done((bf16[48,1024]{1,0:T(8,128)(2,1)S(1)}, bf16[48,1024]{1,0:T(8,128)(2,1)S(1)}, u32[]{:S(2)}, u32[]{:S(2)}) %collective-permute-start.3) | collective-permute-done | bytes 98336 | tf_op jit(solution)/shard_map/ppermute | solution.py:45
  42.0 17.8 %all_to_all.30 = bf16[16,32,1024]{2,1,0:T(8,128)(2,1)S(1)} all-to-all(bf16[16,32,1024]{2,1,0:T(8,128)(2,1)S(1)} %shard_map.129), channel_id=1, replica_groups=mesh['z_hi'=2,'y'=4,'x'=4,'z_lo'=4,'core'=2] {'y','x'}, dimensions={0} | all-to-all | bytes 2097152 | tf_op jit(solution)/shard_map/all_to_all | solution.py:54
  60.1 1.1 shard_map.130
  61.3 1.5 collective-permute-done.4.got_ref
  63.8 2.0 %collective-permute-start.6 = (bf16[64,512]{1,0:T(8,128)(2,1)S(1)}, bf16[64,512]{1,0:T(8,128)(2,1)S(1)}, u32[]{:S(2)}, u32[]{:S(2)}) collective-permute-start(bf16[64,512]{1,0:T(8,128)(2,1)S(1)} %get-tuple-element.59), channel_id=1, source_target_pairs={{0,4},{2,6},{4,0},{6,2},{1,5},{3,7},{5,1},{7,3},{8,12},{10,14},{12... | collective-permute-start | bytes 196616 | tf_op jit(solution)/shard_map/ppermute | solution.py:151
  65.8 1.0 collective-permute-start.7
  66.9 1.3 collective-permute-done.5
  68.2 2.3 %collective-permute-done.6 = bf16[64,512]{1,0:T(8,128)(2,1)S(1)} collective-permute-done((bf16[64,512]{1,0:T(8,128)(2,1)S(1)}, bf16[64,512]{1,0:T(8,128)(2,1)S(1)}, u32[]{:S(2)}, u32[]{:S(2)}) %collective-permute-start.6) | collective-permute-done | bytes 65568 | tf_op jit(solution)/shard_map/ppermute | solution.py:151
  70.5 2.3 %collective-permute-done.7 = bf16[64,512]{1,0:T(8,128)(2,1)S(1)} collective-permute-done((bf16[64,512]{1,0:T(8,128)(2,1)S(1)}, bf16[64,512]{1,0:T(8,128)(2,1)S(1)}, u32[]{:S(2)}, u32[]{:S(2)}) %collective-permute-start.7) | collective-permute-done | bytes 65568 | tf_op jit(solution)/shard_map/ppermute | solution.py:151
  73.5 2.0 %collective-permute-start.9 = (bf16[64,512]{1,0:T(8,128)(2,1)}, bf16[64,512]{1,0:T(8,128)(2,1)S(1)}, u32[]{:S(2)}, u32[]{:S(2)}) collective-permute-start(bf16[64,512]{1,0:T(8,128)(2,1)} %add_convert_fusion.1), channel_id=1, source_target_pairs={{0,128},{1,0},{2,160},{3,32},{4,192},{5,64},{6,224},{7,96},{8,136}... | collective-permute-start | bytes 196616 | tf_op jit(solution)/shard_map/ppermute | solution.py:347
  75.5 4.7 %collective-permute-done.9.attn_ref = bf16[64,512]{1,0:T(8,128)(2,1)S(1)} collective-permute-done((bf16[64,512]{1,0:T(8,128)(2,1)}, bf16[64,512]{1,0:T(8,128)(2,1)S(1)}, u32[]{:S(2)}, u32[]{:S(2)}) %collective-permute-start.9) | collective-permute-done | bytes 65568 | tf_op jit(solution)/shard_map/ppermute | solution.py:347
  80.2 0.9 copy-done.9
  81.2 1.0 copy-done.6
  82.2 4.3 %all-to-all-start.3 = ((bf16[16,64,512]{2,1,0:T(8,128)(2,1)}), bf16[16,64,512]{2,1,0:T(8,128)(2,1)}, u32[]{:S(2)}, u32[]{:S(2)}) async-start(bf16[16,64,512]{2,1,0:T(8,128)(2,1)} %copy-done.6), calls=%async_computation.3 | async-start | bytes 2097152 | tf_op jit(solution)/shard_map/all_to_all | solution.py:259
  86.6 4.2 %collective-permute-start.8 = (bf16[64,512]{1,0:T(8,128)(2,1)}, bf16[64,512]{1,0:T(8,128)(2,1)S(1)}, u32[]{:S(2)}, u32[]{:S(2)}) collective-permute-start(bf16[64,512]{1,0:T(8,128)(2,1)} %add_convert_fusion.1), channel_id=1, source_target_pairs={{0,0},{1,128},{2,32},{3,160},{4,64},{5,192},{6,96},{7,224},{8,8},{... | collective-permute-start | bytes 196616 | tf_op jit(solution)/shard_map/ppermute | solution.py:348
  90.8 6.4 %collective-permute-done.8.attn_ref = bf16[64,512]{1,0:T(8,128)(2,1)S(1)} collective-permute-done((bf16[64,512]{1,0:T(8,128)(2,1)}, bf16[64,512]{1,0:T(8,128)(2,1)S(1)}, u32[]{:S(2)}, u32[]{:S(2)}) %collective-permute-start.8) | collective-permute-done | bytes 65568 | tf_op jit(solution)/shard_map/ppermute | solution.py:348
  97.3 1.0 copy-done.5
  98.3 5.0 %all-to-all-done.3 = bf16[16,64,512]{2,1,0:T(8,128)(2,1)} async-done(((bf16[16,64,512]{2,1,0:T(8,128)(2,1)}), bf16[16,64,512]{2,1,0:T(8,128)(2,1)}, u32[]{:S(2)}, u32[]{:S(2)}) %all-to-all-start.3) | async-done | bytes 1048608 | tf_op jit(solution)/shard_map/all_to_all | solution.py:259
  103.3 4.3 %all-to-all-start.2 = ((bf16[16,64,512]{2,1,0:T(8,128)(2,1)}), bf16[16,64,512]{2,1,0:T(8,128)(2,1)}, u32[]{:S(2)}, u32[]{:S(2)}) async-start(bf16[16,64,512]{2,1,0:T(8,128)(2,1)} %copy-done.5), calls=%async_computation.2 | async-start | bytes 2097152 | tf_op jit(solution)/shard_map/all_to_all | solution.py:259
  107.7 2.0 copy-done.1
  109.7 4.0 %shard_map.134 = (bf16[128,1792]{1,0:T(8,128)(2,1)S(1)}, bf16[128,1792]{1,0:T(8,128)(2,1)S(1)}, f32[8,128]{1,0:T(8,128)}) custom-call(s32[1]{0:T(128)} %bitcast.15.core, bf16[4,4,64,512]{3,2,1,0:T(8,128)(2,1)} %bitcast.18.rows_ref, bf16[1,2048]{1,0:T(2,128)(2,1)S(1)} %reshape.116.gain_ref, bf16[832,2048]{1,0:T(8,128)(2,1)S(1)} %bitcast.33, ...), custom_call_target="tpu_custom_call" | custom-call | flops 1 | bytes 1 | tf_op jit(solution)/shard_map/pallas_call | solution.py:63
  113.7 1.8 collective-permute-done.10.got_ref
  115.5 0.8 shard_map.135
  116.2 0.7 copy-done.10
  117.2 5.6 %collective-permute-start.12 = (bf16[32,1792]{1,0:T(8,128)(2,1)}, bf16[32,1792]{1,0:T(8,128)(2,1)}, u32[]{:S(2)}, u32[]{:S(2)}) collective-permute-start(bf16[32,1792]{1,0:T(8,128)(2,1)} %get-tuple-element.68), channel_id=1, source_target_pairs={{0,4},{2,6},{4,0},{6,2},{1,5},{3,7},{5,1},{7,3},{8,12},{10,14},{12... | collective-permute-start | bytes 344072 | tf_op jit(solution)/shard_map/ppermute | solution.py:151
  123.4 1.3 all-to-all-done.2
  124.7 2.0 %copy-done.2 = bf16[2048,832]{0,1:T(8,128)(2,1)S(1)} copy-done((bf16[2048,832]{0,1:T(8,128)(2,1)S(1)}, bf16[2048,832]{0,1:T(8,128)(2,1)}, u32[]{:S(2)}) %copy-start.2) | copy-done | bytes 3407896
  126.6 3.8 %shard_map.136 = (bf16[128,1792]{1,0:T(8,128)(2,1)S(1)}, bf16[128,1792]{1,0:T(8,128)(2,1)S(1)}, f32[8,128]{1,0:T(8,128)S(1)}) custom-call(s32[1]{0:T(128)} %bitcast.15.core, bf16[4,4,64,512]{3,2,1,0:T(8,128)(2,1)} %bitcast.12.rows_ref, bf16[1,2048]{1,0:T(2,128)(2,1)S(1)} %reshape.116.gain_ref, bf16[832,2048]{1,0:T(8,128)(2,1)S(1)} %bitcast.34, ...), custom_call_target="tpu_custom_call" | custom-call | flops 1 | bytes 1 | tf_op jit(solution)/shard_map/pallas_call | solution.py:63
  130.5 1.1 collective-permute-done.12.two_ref
  131.6 2.6 %collective-permute-done.13.three_ref = bf16[32,1792]{1,0:T(8,128)(2,1)} collective-permute-done((bf16[32,1792]{1,0:T(8,128)(2,1)}, bf16[32,1792]{1,0:T(8,128)(2,1)}, u32[]{:S(2)}, u32[]{:S(2)}) %collective-permute-start.13) | collective-permute-done | bytes 114720 | tf_op jit(solution)/shard_map/ppermute | solution.py:151
  134.2 1.2 shard_map.137.own_ref
  135.5 1.6 collective-permute-start.20
  137.8 1.3 collective-permute-start.18
  139.2 3.1 %collective-permute-done.20.three_ref = bf16[32,832]{1,0:T(8,128)(2,1)S(1)} collective-permute-done((bf16[32,832]{1,0:T(8,128)(2,1)S(1)}, bf16[32,832]{1,0:T(8,128)(2,1)S(1)}, u32[]{:S(2)}, u32[]{:S(2)}) %collective-permute-start.20) | collective-permute-done | bytes 53280 | tf_op jit(solution)/shard_map/ppermute | solution.py:151
  142.9 2.3 %collective-permute-start.15 = (bf16[32,1792]{1,0:T(8,128)(2,1)S(1)}, bf16[32,1792]{1,0:T(8,128)(2,1)S(1)}, u32[]{:S(2)}, u32[]{:S(2)}) collective-permute-start(bf16[32,1792]{1,0:T(8,128)(2,1)S(1)} %get-tuple-element.73), channel_id=1, source_target_pairs={{0,2},{2,0},{4,6},{6,4},{1,3},{3,1},{5,7},{7,5},{8,10},{10,8},{12,... | collective-permute-start | bytes 344072 | tf_op jit(solution)/shard_map/ppermute | solution.py:151
  145.2 1.0 collective-permute-start.16
  146.8 2.2 %shard_map.140 = (bf16[256,2048]{1,0:T(8,128)(2,1)}, f32[8,128]{1,0:T(8,128)S(1)}) custom-call(s32[1]{0:T(128)} %bitcast.15.core, bf16[128,832]{1,0:T(8,128)(2,1)S(1)} %shard_map.139.own_ref, bf16[128,832]{1,0:T(8,128)(2,1)S(1)} %collective-permute-done.21.other_ref, bf16[832,2048]{1,0:T(8,128)(2,1)S(1)} %copy-done.3), custom_call_target="tpu_custom_call" | custom-call | flops 1 | bytes 1 | tf_op jit(solution)/shard_map/pallas_call | solution.py:63
  149.0 7.1 %all-to-all-start.5 = ((bf16[16,16,2048]{2,1,0:T(8,128)(2,1)}), bf16[16,16,2048]{2,1,0:T(8,128)(2,1)S(1)}, u32[]{:S(2)}, u32[]{:S(2)}) async-start(bf16[16,16,2048]{2,1,0:T(8,128)(2,1)} %bitcast.20), calls=%async_computation.5 | async-start | bytes 2097152 | tf_op jit(solution)/shard_map/all_to_all | solution.py:259
  156.1 1.4 collective-permute-done.17.three_ref
  157.8 1.5 collective-permute-start.24
  159.3 2.3 %collective-permute-start.23 = (bf16[32,832]{1,0:T(8,128)(2,1)S(1)}, bf16[32,832]{1,0:T(8,128)(2,1)S(1)}, u32[]{:S(2)}, u32[]{:S(2)}) collective-permute-start(bf16[32,832]{1,0:T(8,128)(2,1)S(1)} %shard_map.141.own_ref), channel_id=1, source_target_pairs={{0,4},{2,6},{4,0},{6,2},{1,5},{3,7},{5,1},{7,3},{8,12},{10,14},{12... | collective-permute-start | bytes 159752 | tf_op jit(solution)/shard_map/ppermute | solution.py:151
  161.7 3.3 %collective-permute-done.24.three_ref = bf16[32,832]{1,0:T(8,128)(2,1)S(1)} collective-permute-done((bf16[32,832]{1,0:T(8,128)(2,1)S(1)}, bf16[32,832]{1,0:T(8,128)(2,1)S(1)}, u32[]{:S(2)}, u32[]{:S(2)}) %collective-permute-start.24) | collective-permute-done | bytes 53280 | tf_op jit(solution)/shard_map/ppermute | solution.py:151
  165.0 0.9 collective-permute-done.22.one_ref
  165.9 1.5 collective-permute-done.25.other_ref
  167.4 2.3 %shard_map.143 = (bf16[256,2048]{1,0:T(8,128)(2,1)}, f32[8,128]{1,0:T(8,128)}) custom-call(s32[1]{0:T(128)} %bitcast.15.core, bf16[128,832]{1,0:T(8,128)(2,1)S(1)} %shard_map.142.own_ref, bf16[128,832]{1,0:T(8,128)(2,1)S(1)} %collective-permute-done.25.other_ref, bf16[832,2048]{1,0:T(8,128)(2,1)S(1)} %copy-done.4), custom_call_target="tpu_custom_call" | custom-call | flops 1 | bytes 1 | tf_op jit(solution)/shard_map/pallas_call | solution.py:63
  169.7 4.1 %all-to-all-done.5.parts_ref = bf16[16,16,2048]{2,1,0:T(8,128)(2,1)S(1)} async-done(((bf16[16,16,2048]{2,1,0:T(8,128)(2,1)}), bf16[16,16,2048]{2,1,0:T(8,128)(2,1)S(1)}, u32[]{:S(2)}, u32[]{:S(2)}) %all-to-all-start.5) | async-done | bytes 1048608 | tf_op jit(solution)/shard_map/all_to_all | solution.py:259
  173.7 3.7 %all-to-all-start.4 = ((bf16[16,16,2048]{2,1,0:T(8,128)(2,1)}), bf16[16,16,2048]{2,1,0:T(8,128)(2,1)S(1)}, u32[]{:S(2)}, u32[]{:S(2)}) async-start(bf16[16,16,2048]{2,1,0:T(8,128)(2,1)} %bitcast.19), calls=%async_computation.4 | async-start | bytes 2097152 | tf_op jit(solution)/shard_map/all_to_all | solution.py:259
  177.6 3.3 %collective-permute-start.26 = (bf16[16,2048]{1,0:T(8,128)(2,1)S(1)}, bf16[16,2048]{1,0:T(8,128)(2,1)S(1)}, u32[]{:S(2)}, u32[]{:S(2)}) collective-permute-start(bf16[16,2048]{1,0:T(8,128)(2,1)S(1)} %shard_map.145), channel_id=1, source_target_pairs={{0,128},{128,0},{1,129},{129,1},{2,130},{130,2},{3,131},{131,3},{4... | collective-permute-start | bytes 196616 | tf_op jit(solution)/shard_map/ppermute | solution.py:45
  180.8 0.9 convert_bitcast_fusion
  181.8 13.1 %all-to-all-done.4.parts_ref = bf16[16,16,2048]{2,1,0:T(8,128)(2,1)S(1)} async-done(((bf16[16,16,2048]{2,1,0:T(8,128)(2,1)}), bf16[16,16,2048]{2,1,0:T(8,128)(2,1)S(1)}, u32[]{:S(2)}, u32[]{:S(2)}) %all-to-all-start.4) | async-done | bytes 1048608 | tf_op jit(solution)/shard_map/all_to_all | solution.py:259
  (75 shorter events, 8.5 us)
Async XLA Ops:
  0.0 60.1 %copy-start.7 = (bf16[1024,512]{1,0:T(8,128)(2,1)S(1)}, bf16[1024,512]{1,0:T(8,128)(2,1)}, u32[]{:S(2)}) copy-start(bf16[1024,512]{1,0:T(8,128)(2,1)} %weight_ref.3) | copy-start | bytes 3145732
  2.8 26.0 %all-to-all-start = ((bf16[32,2,1280]{2,1,0:T(2,128)(2,1)}), bf16[32,2,1280]{2,1,0:T(2,128)(2,1)S(1)}, u32[]{:S(2)}, u32[]{:S(2)}) async-start(bf16[32,2,1280]{2,1,0:T(2,128)(2,1)} %reshape.107), calls=%async_computation | async-start | bytes 327680 | tf_op jit(solution)/shard_map/all_to_all | solution.py:300
  15.8 0.8 copy-start.14
  16.7 12.2 %collective-permute-start = (bf16[16,512]{1,0:T(8,128)(2,1)S(1)}, bf16[16,512]{1,0:T(8,128)(2,1)S(1)}, u32[]{:S(2)}, u32[]{:S(2)}) collective-permute-start(bf16[16,512]{1,0:T(8,128)(2,1)S(1)} %get-tuple-element.46), channel_id=1, source_target_pairs={{0,8},{8,0},{16,24},{24,16},{1,9},{9,1},{17,25},{25,17},{2,10},{10... | collective-permute-start | bytes 49160 | tf_op jit(solution)/shard_map/ppermute | solution.py:322
  18.5 10.4 %collective-permute-start.1 = (bf16[16,512]{1,0:T(8,128)(2,1)S(1)}, bf16[16,512]{1,0:T(8,128)(2,1)S(1)}, u32[]{:S(2)}, u32[]{:S(2)}) collective-permute-start(bf16[16,512]{1,0:T(8,128)(2,1)S(1)} %get-tuple-element.47), channel_id=1, source_target_pairs={{0,16},{8,24},{16,0},{24,8},{1,17},{9,25},{17,1},{25,9},{2,18},{10... | collective-permute-start | bytes 49160 | tf_op jit(solution)/shard_map/ppermute | solution.py:322
  21.1 7.7 %collective-permute-start.2 = (bf16[16,512]{1,0:T(8,128)(2,1)S(1)}, bf16[16,512]{1,0:T(8,128)(2,1)S(1)}, u32[]{:S(2)}, u32[]{:S(2)}) collective-permute-start(bf16[16,512]{1,0:T(8,128)(2,1)S(1)} %get-tuple-element.48), channel_id=1, source_target_pairs={{0,24},{8,16},{16,8},{24,0},{1,25},{9,17},{17,9},{25,1},{2,26},{10... | collective-permute-start | bytes 49160 | tf_op jit(solution)/shard_map/ppermute | solution.py:322
  28.9 0.9 copy-start.12
  29.8 0.9 copy-start.13
  31.6 9.7 %collective-permute-start.3 = (bf16[48,1024]{1,0:T(8,128)(2,1)S(1)}, bf16[48,1024]{1,0:T(8,128)(2,1)S(1)}, u32[]{:S(2)}, u32[]{:S(2)}) collective-permute-start(bf16[48,1024]{1,0:T(8,128)(2,1)S(1)} %shard_map.128.near_ref.tok_ref), channel_id=1, source_target_pairs={{0,128},{128,0},{1,129},{129,1},{2,130},{130,2},{3,131},{131,3},{4... | collective-permute-start | bytes 294920 | tf_op jit(solution)/shard_map/ppermute | solution.py:45
  41.3 0.6 copy-start.8
  61.1 1.6 collective-permute-start.4
  63.4 4.8 %collective-permute-start.5 = (bf16[64,512]{1,0:T(8,128)(2,1)S(1)}, bf16[64,512]{1,0:T(8,128)(2,1)S(1)}, u32[]{:S(2)}, u32[]{:S(2)}) collective-permute-start(bf16[64,512]{1,0:T(8,128)(2,1)S(1)} %get-tuple-element.58), channel_id=1, source_target_pairs={{0,2},{2,0},{4,6},{6,4},{1,3},{3,1},{5,7},{7,5},{8,10},{10,8},{12,... | collective-permute-start | bytes 196616 | tf_op jit(solution)/shard_map/ppermute | solution.py:151
  63.8 6.7 %collective-permute-start.6 = (bf16[64,512]{1,0:T(8,128)(2,1)S(1)}, bf16[64,512]{1,0:T(8,128)(2,1)S(1)}, u32[]{:S(2)}, u32[]{:S(2)}) collective-permute-start(bf16[64,512]{1,0:T(8,128)(2,1)S(1)} %get-tuple-element.59), channel_id=1, source_target_pairs={{0,4},{2,6},{4,0},{6,2},{1,5},{3,7},{5,1},{7,3},{8,12},{10,14},{12... | collective-permute-start | bytes 196616 | tf_op jit(solution)/shard_map/ppermute | solution.py:151
  65.8 7.0 %collective-permute-start.7 = (bf16[64,512]{1,0:T(8,128)(2,1)S(1)}, bf16[64,512]{1,0:T(8,128)(2,1)S(1)}, u32[]{:S(2)}, u32[]{:S(2)}) collective-permute-start(bf16[64,512]{1,0:T(8,128)(2,1)S(1)} %get-tuple-element.60), channel_id=1, source_target_pairs={{0,6},{2,4},{4,2},{6,0},{1,7},{3,5},{5,3},{7,1},{8,14},{10,12},{12... | collective-permute-start | bytes 196616 | tf_op jit(solution)/shard_map/ppermute | solution.py:151
  72.9 34.8 %copy-start.15 = (bf16[2048]{0:T(1024)(128)(2,1)S(1)}, bf16[2048]{0:T(1024)(128)(2,1)}, u32[]{:S(2)}) copy-start(bf16[2048]{0:T(1024)(128)(2,1)} %param.22) | copy-start | bytes 12292
  73.5 34.2 %copy-start = (bf16[2048,832]{0,1:T(8,128)(2,1)S(1)}, bf16[2048,832]{0,1:T(8,128)(2,1)}, u32[]{:S(2)}) copy-start(bf16[2048,832]{0,1:T(8,128)(2,1)} %param.23) | copy-start | bytes 10223620
  73.5 6.7 %collective-permute-start.9 = (bf16[64,512]{1,0:T(8,128)(2,1)}, bf16[64,512]{1,0:T(8,128)(2,1)S(1)}, u32[]{:S(2)}, u32[]{:S(2)}) collective-permute-start(bf16[64,512]{1,0:T(8,128)(2,1)} %add_convert_fusion.1), channel_id=1, source_target_pairs={{0,128},{1,0},{2,160},{3,32},{4,192},{5,64},{6,224},{7,96},{8,136}... | collective-permute-start | bytes 196616 | tf_op jit(solution)/shard_map/ppermute | solution.py:347
  80.2 0.9 copy-start.9
  81.2 1.0 copy-start.6
  82.2 21.1 %all-to-all-start.3 = ((bf16[16,64,512]{2,1,0:T(8,128)(2,1)}), bf16[16,64,512]{2,1,0:T(8,128)(2,1)}, u32[]{:S(2)}, u32[]{:S(2)}) async-start(bf16[16,64,512]{2,1,0:T(8,128)(2,1)} %copy-done.6), calls=%async_computation.3 | async-start | bytes 2097152 | tf_op jit(solution)/shard_map/all_to_all | solution.py:259
  86.6 10.6 %collective-permute-start.8 = (bf16[64,512]{1,0:T(8,128)(2,1)}, bf16[64,512]{1,0:T(8,128)(2,1)S(1)}, u32[]{:S(2)}, u32[]{:S(2)}) collective-permute-start(bf16[64,512]{1,0:T(8,128)(2,1)} %add_convert_fusion.1), channel_id=1, source_target_pairs={{0,0},{1,128},{2,32},{3,160},{4,64},{5,192},{6,96},{7,224},{8,8},{... | collective-permute-start | bytes 196616 | tf_op jit(solution)/shard_map/ppermute | solution.py:348
  97.3 1.0 copy-start.5
  103.3 21.4 %all-to-all-start.2 = ((bf16[16,64,512]{2,1,0:T(8,128)(2,1)}), bf16[16,64,512]{2,1,0:T(8,128)(2,1)}, u32[]{:S(2)}, u32[]{:S(2)}) async-start(bf16[16,64,512]{2,1,0:T(8,128)(2,1)} %copy-done.5), calls=%async_computation.2 | async-start | bytes 2097152 | tf_op jit(solution)/shard_map/all_to_all | solution.py:259
  107.7 2.0 %copy-start.1 = (bf16[2048,832]{0,1:T(8,128)(2,1)S(1)}, bf16[2048,832]{0,1:T(8,128)(2,1)}, u32[]{:S(2)}) copy-start(bf16[2048,832]{0,1:T(8,128)(2,1)} %param.24) | copy-start | bytes 10223620
  113.7 1.8 collective-permute-start.10
  116.2 0.7 copy-start.10
  117.0 13.5 %collective-permute-start.11 = (bf16[32,1792]{1,0:T(8,128)(2,1)}, bf16[32,1792]{1,0:T(8,128)(2,1)S(1)}, u32[]{:S(2)}, u32[]{:S(2)}) collective-permute-start(bf16[32,1792]{1,0:T(8,128)(2,1)} %get-tuple-element.67), channel_id=1, source_target_pairs={{0,2},{2,0},{4,6},{6,4},{1,3},{3,1},{5,7},{7,5},{8,10},{10,8},{12,... | collective-permute-start | bytes 344072 | tf_op jit(solution)/shard_map/ppermute | solution.py:151
  117.2 14.4 %collective-permute-start.12 = (bf16[32,1792]{1,0:T(8,128)(2,1)}, bf16[32,1792]{1,0:T(8,128)(2,1)}, u32[]{:S(2)}, u32[]{:S(2)}) collective-permute-start(bf16[32,1792]{1,0:T(8,128)(2,1)} %get-tuple-element.68), channel_id=1, source_target_pairs={{0,4},{2,6},{4,0},{6,2},{1,5},{3,7},{5,1},{7,3},{8,12},{10,14},{12... | collective-permute-start | bytes 344072 | tf_op jit(solution)/shard_map/ppermute | solution.py:151
  122.8 11.4 %collective-permute-start.13 = (bf16[32,1792]{1,0:T(8,128)(2,1)}, bf16[32,1792]{1,0:T(8,128)(2,1)}, u32[]{:S(2)}, u32[]{:S(2)}) collective-permute-start(bf16[32,1792]{1,0:T(8,128)(2,1)} %get-tuple-element.69), channel_id=1, source_target_pairs={{0,6},{2,4},{4,2},{6,0},{1,7},{3,5},{5,3},{7,1},{8,14},{10,12},{12... | collective-permute-start | bytes 344072 | tf_op jit(solution)/shard_map/ppermute | solution.py:151
  124.7 2.0 %copy-start.2 = (bf16[2048,832]{0,1:T(8,128)(2,1)S(1)}, bf16[2048,832]{0,1:T(8,128)(2,1)}, u32[]{:S(2)}) copy-start(bf16[2048,832]{0,1:T(8,128)(2,1)} %param.24) | copy-start | bytes 10223620
  126.6 7.6 %copy-start.11 = (f32[32,1792]{1,0:T(8,128)S(1)}, f32[32,1792]{1,0:T(8,128)}, u32[]{:S(2)}) copy-start(f32[32,1792]{1,0:T(8,128)} %copy-done.10) | copy-start | bytes 688132
  126.6 20.1 %copy-start.3 = (bf16[832,2048]{1,0:T(8,128)(2,1)S(1)}, bf16[832,2048]{1,0:T(8,128)(2,1)}, u32[]{:S(2)}) copy-start(bf16[832,2048]{1,0:T(8,128)(2,1)} %weight_ref.5) | copy-start | bytes 10223620
  135.4 3.7 %collective-permute-start.14 = (bf16[128,1792]{1,0:T(8,128)(2,1)S(1)}, bf16[128,1792]{1,0:T(8,128)(2,1)S(1)}, u32[]{:S(2)}, u32[]{:S(2)}) collective-permute-start(bf16[128,1792]{1,0:T(8,128)(2,1)S(1)} %get-tuple-element.71), channel_id=1, source_target_pairs={{0,1},{1,0},{2,3},{3,2},{4,5},{5,4},{6,7},{7,6},{8,9},{9,8},{10,11... | collective-permute-start | bytes 1376264 | tf_op jit(solution)/shard_map/ppermute | solution.py:45
  135.5 6.8 %collective-permute-start.20 = (bf16[32,832]{1,0:T(8,128)(2,1)S(1)}, bf16[32,832]{1,0:T(8,128)(2,1)S(1)}, u32[]{:S(2)}, u32[]{:S(2)}) collective-permute-start(bf16[32,832]{1,0:T(8,128)(2,1)S(1)} %shard_map.137.own_ref), channel_id=1, source_target_pairs={{0,6},{2,4},{4,2},{6,0},{1,7},{3,5},{5,3},{7,1},{8,14},{10,12},{12... | collective-permute-start | bytes 159752 | tf_op jit(solution)/shard_map/ppermute | solution.py:151
  137.1 5.5 %collective-permute-start.19 = (bf16[32,832]{1,0:T(8,128)(2,1)S(1)}, bf16[32,832]{1,0:T(8,128)(2,1)S(1)}, u32[]{:S(2)}, u32[]{:S(2)}) collective-permute-start(bf16[32,832]{1,0:T(8,128)(2,1)S(1)} %shard_map.137.own_ref), channel_id=1, source_target_pairs={{0,4},{2,6},{4,0},{6,2},{1,5},{3,7},{5,1},{7,3},{8,12},{10,14},{12... | collective-permute-start | bytes 159752 | tf_op jit(solution)/shard_map/ppermute | solution.py:151
  137.8 5.0 %collective-permute-start.18 = (bf16[32,832]{1,0:T(8,128)(2,1)S(1)}, bf16[32,832]{1,0:T(8,128)(2,1)S(1)}, u32[]{:S(2)}, u32[]{:S(2)}) collective-permute-start(bf16[32,832]{1,0:T(8,128)(2,1)S(1)} %shard_map.137.own_ref), channel_id=1, source_target_pairs={{0,2},{2,0},{4,6},{6,4},{1,3},{3,1},{5,7},{7,5},{8,10},{10,8},{12,... | collective-permute-start | bytes 159752 | tf_op jit(solution)/shard_map/ppermute | solution.py:151
  142.8 4.0 %collective-permute-start.21 = (bf16[128,832]{1,0:T(8,128)(2,1)S(1)}, bf16[128,832]{1,0:T(8,128)(2,1)S(1)}, u32[]{:S(2)}, u32[]{:S(2)}) collective-permute-start(bf16[128,832]{1,0:T(8,128)(2,1)S(1)} %shard_map.139.own_ref), channel_id=1, source_target_pairs={{0,1},{1,0},{2,3},{3,2},{4,5},{5,4},{6,7},{7,6},{8,9},{9,8},{10,11... | collective-permute-start | bytes 638984 | tf_op jit(solution)/shard_map/ppermute | solution.py:45
  142.9 13.2 %collective-permute-start.15 = (bf16[32,1792]{1,0:T(8,128)(2,1)S(1)}, bf16[32,1792]{1,0:T(8,128)(2,1)S(1)}, u32[]{:S(2)}, u32[]{:S(2)}) collective-permute-start(bf16[32,1792]{1,0:T(8,128)(2,1)S(1)} %get-tuple-element.73), channel_id=1, source_target_pairs={{0,2},{2,0},{4,6},{6,4},{1,3},{3,1},{5,7},{7,5},{8,10},{10,8},{12,... | collective-permute-start | bytes 344072 | tf_op jit(solution)/shard_map/ppermute | solution.py:151
  145.2 10.9 %collective-permute-start.16 = (bf16[32,1792]{1,0:T(8,128)(2,1)S(1)}, bf16[32,1792]{1,0:T(8,128)(2,1)S(1)}, u32[]{:S(2)}, u32[]{:S(2)}) collective-permute-start(bf16[32,1792]{1,0:T(8,128)(2,1)S(1)} %get-tuple-element.74), channel_id=1, source_target_pairs={{0,4},{2,6},{4,0},{6,2},{1,5},{3,7},{5,1},{7,3},{8,12},{10,14},{12... | collective-permute-start | bytes 344072 | tf_op jit(solution)/shard_map/ppermute | solution.py:151
  146.2 11.3 %collective-permute-start.17 = (bf16[32,1792]{1,0:T(8,128)(2,1)S(1)}, bf16[32,1792]{1,0:T(8,128)(2,1)S(1)}, u32[]{:S(2)}, u32[]{:S(2)}) collective-permute-start(bf16[32,1792]{1,0:T(8,128)(2,1)S(1)} %get-tuple-element.75), channel_id=1, source_target_pairs={{0,6},{2,4},{4,2},{6,0},{1,7},{3,5},{5,3},{7,1},{8,14},{10,12},{12... | collective-permute-start | bytes 344072 | tf_op jit(solution)/shard_map/ppermute | solution.py:151
  149.0 24.7 %all-to-all-start.5 = ((bf16[16,16,2048]{2,1,0:T(8,128)(2,1)}), bf16[16,16,2048]{2,1,0:T(8,128)(2,1)S(1)}, u32[]{:S(2)}, u32[]{:S(2)}) async-start(bf16[16,16,2048]{2,1,0:T(8,128)(2,1)} %bitcast.20), calls=%async_computation.5 | async-start | bytes 2097152 | tf_op jit(solution)/shard_map/all_to_all | solution.py:259
  157.6 9.8 %copy-start.4 = (bf16[832,2048]{1,0:T(8,128)(2,1)S(1)}, bf16[832,2048]{1,0:T(8,128)(2,1)}, u32[]{:S(2)}) copy-start(bf16[832,2048]{1,0:T(8,128)(2,1)} %weight_ref.5) | copy-start | bytes 10223620
  157.8 7.2 %collective-permute-start.24 = (bf16[32,832]{1,0:T(8,128)(2,1)S(1)}, bf16[32,832]{1,0:T(8,128)(2,1)S(1)}, u32[]{:S(2)}, u32[]{:S(2)}) collective-permute-start(bf16[32,832]{1,0:T(8,128)(2,1)S(1)} %shard_map.141.own_ref), channel_id=1, source_target_pairs={{0,6},{2,4},{4,2},{6,0},{1,7},{3,5},{5,3},{7,1},{8,14},{10,12},{12... | collective-permute-start | bytes 159752 | tf_op jit(solution)/shard_map/ppermute | solution.py:151
  159.3 5.6 %collective-permute-start.23 = (bf16[32,832]{1,0:T(8,128)(2,1)S(1)}, bf16[32,832]{1,0:T(8,128)(2,1)S(1)}, u32[]{:S(2)}, u32[]{:S(2)}) collective-permute-start(bf16[32,832]{1,0:T(8,128)(2,1)S(1)} %shard_map.141.own_ref), channel_id=1, source_target_pairs={{0,4},{2,6},{4,0},{6,2},{1,5},{3,7},{5,1},{7,3},{8,12},{10,14},{12... | collective-permute-start | bytes 159752 | tf_op jit(solution)/shard_map/ppermute | solution.py:151
  161.6 4.2 %collective-permute-start.22 = (bf16[32,832]{1,0:T(8,128)(2,1)S(1)}, bf16[32,832]{1,0:T(8,128)(2,1)S(1)}, u32[]{:S(2)}, u32[]{:S(2)}) collective-permute-start(bf16[32,832]{1,0:T(8,128)(2,1)S(1)} %shard_map.141.own_ref), channel_id=1, source_target_pairs={{0,2},{2,0},{4,6},{6,4},{1,3},{3,1},{5,7},{7,5},{8,10},{10,8},{12,... | collective-permute-start | bytes 159752 | tf_op jit(solution)/shard_map/ppermute | solution.py:151
  165.8 1.6 collective-permute-start.25
  173.7 21.1 %all-to-all-start.4 = ((bf16[16,16,2048]{2,1,0:T(8,128)(2,1)}), bf16[16,16,2048]{2,1,0:T(8,128)(2,1)S(1)}, u32[]{:S(2)}, u32[]{:S(2)}) async-start(bf16[16,16,2048]{2,1,0:T(8,128)(2,1)} %bitcast.19), calls=%async_computation.4 | async-start | bytes 2097152 | tf_op jit(solution)/shard_map/all_to_all | solution.py:259
  177.6 17.4 %collective-permute-start.26 = (bf16[16,2048]{1,0:T(8,128)(2,1)S(1)}, bf16[16,2048]{1,0:T(8,128)(2,1)S(1)}, u32[]{:S(2)}, u32[]{:S(2)}) collective-permute-start(bf16[16,2048]{1,0:T(8,128)(2,1)S(1)} %shard_map.145), channel_id=1, source_target_pairs={{0,128},{128,0},{1,129},{129,1},{2,130},{130,2},{3,131},{131,3},{4... | collective-permute-start | bytes 196616 | tf_op jit(solution)/shard_map/ppermute | solution.py:45

commit v4 on v3

--- a/solution.py
+++ b/solution.py
@@ -141,7 +141,7 @@
 
 def line_reduce(keep, got, z_lo):
     rows, cols = keep.shape[0] // 4, keep.shape[1]
-    outs = [shape((rows, cols), F32)] + [shape((rows, cols), BF)] * 3 + [MARK]
+    outs = [shape((rows, cols), BF)] * 4 + [MARK]
     own, *pieces, mark = call(split_body, outs, keep, got, scalars=(z_lo,))
     return [own] + line_send(pieces), mark
 
@@ -153,33 +153,38 @@
     ]
 
 
-def gate_up_body(core, rows_ref, gain_ref, gate_ref, up_ref, *refs):
-    send_ref, keep_ref, mark_ref, total = refs[-4:]
-    mark_ref[...] = jnp.zeros(mark_ref.shape, mark_ref.dtype)
+def gate_body(rows_ref, gain_ref, gate_ref, *refs):
+    scaled_ref, part_ref = refs[-2:]
     hid = gate_ref.shape[0]
     planes, blocks, count, cols = rows_ref.shape
     rows = planes * count
     squares = jnp.zeros((rows, 1), F32)
-    parts = []
     for b in range(blocks):
         wide = rows_ref[:, b].reshape(rows, cols).astype(F32)
         squares += jnp.sum(wide * wide, axis=1, keepdims=True)
-        parts.append((wide * gain_ref[:, b * cols : (b + 1) * cols].astype(F32)).astype(BF))
-    scaled = jnp.concatenate(parts, axis=1)
-    total[:, :hid] = dot_t(scaled, gate_ref[...])
-    total[:, PAD : PAD + hid] = dot_t(scaled, up_ref[...])
-    total[:, PAD + hid :] = jnp.zeros((rows, PAD - hid), F32)
+        at = slice(b * cols, (b + 1) * cols)
+        scaled_ref[:, at] = (wide * gain_ref[:, at].astype(F32)).astype(BF)
+    part_ref[:, :hid] = dot_t(scaled_ref[...], gate_ref[...]).astype(BF)
     high = squares.astype(BF).astype(F32)
     lane = lax.broadcasted_iota(jnp.int32, (rows, PAD - hid), 1)
-    total[:, hid:PAD] = jnp.where(lane == 0, high, jnp.where(lane == 1, squares - high, 0.0))
+    part_ref[:, hid:] = jnp.where(lane == 0, high, jnp.where(lane == 1, squares - high, 0.0)).astype(BF)
+
+
+def up_body(core, scaled_ref, part_ref, up_ref, send_ref, keep_ref, mark_ref, total):
+    mark_ref[...] = jnp.zeros(mark_ref.shape, mark_ref.dtype)
+    rows, hid = scaled_ref.shape[0], up_ref.shape[0]
     half = rows // 2
-    send_ref[...] = total[pl.ds(pl.multiple_of((1 - core[0]) * half, half), half), :].astype(BF)
-    keep_ref[...] = total[pl.ds(pl.multiple_of(core[0] * half, half), half), :].astype(BF)
+    total[:, :hid] = dot_t(scaled_ref[...], up_ref[...])
+    total[:, hid:] = jnp.zeros((rows, PAD - hid), F32)
+    for place, out in ((1 - core[0], send_ref), (core[0], keep_ref)):
+        at = pl.ds(pl.multiple_of(place * half, half), half)
+        out[:, :PAD] = part_ref[at, :]
+        out[:, PAD:] = total[at, :].astype(BF)
 
 
 def hidden_body(own_ref, one_ref, two_ref, three_ref, mark_ref, out_ref):
     hid = out_ref.shape[1]
-    sums = own_ref[...] + one_ref[...].astype(F32) + two_ref[...].astype(F32) + three_ref[...].astype(F32)
+    sums = own_ref[...].astype(F32) + one_ref[...].astype(F32) + two_ref[...].astype(F32) + three_ref[...].astype(F32)
     mean_square = (sums[:, hid : hid + 1] + sums[:, hid + 1 : hid + 2]) / D
     inv = lax.rsqrt(mean_square + 1e-05)
     gate = sums[:, :hid] * inv
@@ -233,10 +238,12 @@
 
 def gate_up(gathered, gain, gate_t, up_t, core, *marks):
     rows = gathered.shape[0] * gathered.shape[2]
+    scaled, part = call(
+        gate_body, [shape((rows, gate_t.shape[1]), BF), shape((rows, PAD), BF)], gathered, gain, gate_t, *marks
+    )
     outs = [shape((rows // 2, 2 * PAD), BF)] * 2 + [MARK]
     return call(
-        gate_up_body, outs, gathered, gain, gate_t, up_t, *marks,
-        scalars=(core,), scratch=[pltpu.VMEM((rows, 2 * PAD), F32)], limit=20,
+        up_body, outs, scaled, part, up_t, scalars=(core,), scratch=[pltpu.VMEM((rows, PAD), F32)]
     )
 
 
@@ -343,7 +350,7 @@
         project_body, outs, send_pos, keep_pos, gathered.reshape(rows, q_cols), out_weight,
     )
     (own, one, two, three), _ = line_reduce(keep, swap(send, "core"), z_lo)
-    attn_out = (own + one.astype(F32) + two.astype(F32) + three.astype(F32)).astype(BF)
+    attn_out = (own.astype(F32) + one.astype(F32) + two.astype(F32) + three.astype(F32)).astype(BF)
     far = lax.ppermute(attn_out, AXES, spread_pairs(1))
     near = lax.ppermute(attn_out, AXES, spread_pairs(0))
     gain = norm_gain.reshape(1, width)
@@ -359,8 +366,7 @@
     far_pieces, far_sent = line_reduce(far_keep, swap(far_send, "core"), z_lo)
     near_gathered = gathered[1]
     near_send, near_keep, near_done = gate_up(near_gathered, gain, gate_t, up_t, core, far_sent)
-    far_hidden = call(hidden_body, shape((far_pieces[0].shape[0], hid), BF), *far_pieces, near_done)
-    near_send, far_hidden = lax.optimization_barrier((near_send, far_hidden))
+    far_hidden = call(hidden_body, shape((far_pieces[0].shape[0], hid), BF), *far_pieces, near_done, weight=LONG)
     near_pieces, near_sent = line_reduce(near_keep, swap(near_send, "core"), z_lo)
     far_hidden = [far_hidden] + line_send([far_hidden] * 3)
     far_down, far_done = down_project(far_hidden, down_weight, z_lo, core, near_sent)

time: 197 us -> 194 us (0.985)
  local copies, waits for them, and re-layouts: 13.5 us -> 10.9 us
  Pallas kernels: 17.7 us -> 19.7 us
    unnamed x32, local copies, waits for them, and re-layouts: 10.7 us -> 8.09 us
    pallas_call x19 -> x21, Pallas kernels: 17.7 us -> 19.7 us  [call(): pl.pallas_call(body, out_shape=out_shape, in_specs=specs, out_specs=whole...]
  transfers between devices with their start and end apart: 32 -> 32, of which waited for: 22 -> 21; matrix products, arithmetic and copies ran while one was open for 2% -> 2% of each run, Pallas kernels for 7% -> 9%
where the time goes in v4:
time: 194 us; the launch traced here: 193 us
  starting transfers between devices  70.9 us (37%)
  waiting for transfers between devices  68.2 us (35%)
  Pallas kernels  19.7 us (10%)
  blocking collectives  17.8 us (9%)
  local copies, waits for them, and re-layouts  10.9 us (6%)
  other arithmetic  3.86 us (2%)
    all_to_all x4, waiting for transfers between devices, all_to_all(): return lax.all_to_all(v, axes, split_axis=0, concat_axis=0, tiled=True)  22.5 us
    ppermute x15, starting transfers between devices, line_send(): lax.ppermute(piece, 'z_lo', [(i, i ^ step) for i in range(4)])  20.6 us
    pallas_call x21, Pallas kernels, call(): pl.pallas_call(body, out_shape=out_shape, in_specs=specs, out_specs=whole...  19.7 us
    all_to_all x4, starting transfers between devices, all_to_all(): return lax.all_to_all(v, axes, split_axis=0, concat_axis=0, tiled=True)  18.8 us
    ppermute x15, waiting for transfers between devices, line_send(): lax.ppermute(piece, 'z_lo', [(i, i ^ step) for i in range(4)])  18.3 us
    all_to_all x1, blocking collectives, exchange(): got = lax.all_to_all(copies, YX, split_axis=0, concat_axis=0, tiled=True)  17.8 us
    all_to_all x1, starting transfers between devices, shards(): lax.all_to_all(bucket, GRP, split_axis=0, concat_axis=0, tiled=True)  13 us
    ppermute x7, waiting for transfers between devices, swap(): return lax.ppermute(v, axis, [(0, 1), (1, 0)])  11.9 us
  transfers between devices with their start and end apart: 32, of which 21 were waited for; matrix products, arithmetic and copies ran while one was open for 2% of the time, Pallas kernels for 9%

profile of v4, /device:TPU:32, one launch (start us, length us, event | category | flops | bytes accessed | tf_op | source)
XLA Modules:
  0.0 192.7 jit_solution(11350476850756690698)
XLA Ops:
  1.1 1.0 convolution_convert_fusion
  2.8 13.0 %all-to-all-start = ((bf16[32,2,1280]{2,1,0:T(2,128)(2,1)}), bf16[32,2,1280]{2,1,0:T(2,128)(2,1)S(1)}, u32[]{:S(2)}, u32[]{:S(2)}) async-start(bf16[32,2,1280]{2,1,0:T(2,128)(2,1)} %reshape.107), calls=%async_computation | async-start | bytes 327680 | tf_op jit(solution)/shard_map/all_to_all | solution.py:307
  16.7 1.8 collective-permute-start
  18.5 2.7 %collective-permute-start.1 = (bf16[16,512]{1,0:T(8,128)(2,1)S(1)}, bf16[16,512]{1,0:T(8,128)(2,1)S(1)}, u32[]{:S(2)}, u32[]{:S(2)}) collective-permute-start(bf16[16,512]{1,0:T(8,128)(2,1)S(1)} %get-tuple-element.49), channel_id=1, source_target_pairs={{0,16},{8,24},{16,0},{24,8},{1,17},{9,25},{17,1},{25,9},{2,18},{10... | collective-permute-start | bytes 49160 | tf_op jit(solution)/shard_map/ppermute | solution.py:329
  21.4 1.2 convert_reduce_fusion.1
  24.3 4.5 %all-to-all-done = bf16[32,2,1280]{2,1,0:T(2,128)(2,1)S(1)} async-done(((bf16[32,2,1280]{2,1,0:T(2,128)(2,1)}), bf16[32,2,1280]{2,1,0:T(2,128)(2,1)S(1)}, u32[]{:S(2)}, u32[]{:S(2)}) %all-to-all-start) | async-done | bytes 163872 | tf_op jit(solution)/shard_map/all_to_all | solution.py:307
  28.9 0.9 copy-done.11
  29.8 0.9 copy-done.12
  30.7 0.9 shard_map.128.near_ref.tok_ref
  31.6 2.7 %collective-permute-start.3 = (bf16[48,1024]{1,0:T(8,128)(2,1)S(1)}, bf16[48,1024]{1,0:T(8,128)(2,1)S(1)}, u32[]{:S(2)}, u32[]{:S(2)}) collective-permute-start(bf16[48,1024]{1,0:T(8,128)(2,1)S(1)} %shard_map.128.near_ref.tok_ref), channel_id=1, source_target_pairs={{0,128},{128,0},{1,129},{129,1},{2,130},{130,2},{3,131},{131,3},{4... | collective-permute-start | bytes 294920 | tf_op jit(solution)/shard_map/ppermute | solution.py:45
  34.3 7.0 %collective-permute-done.3.far_ref.tok_ref = bf16[48,1024]{1,0:T(8,128)(2,1)S(1)} collective-permute-done((bf16[48,1024]{1,0:T(8,128)(2,1)S(1)}, bf16[48,1024]{1,0:T(8,128)(2,1)S(1)}, u32[]{:S(2)}, u32[]{:S(2)}) %collective-permute-start.3) | collective-permute-done | bytes 98336 | tf_op jit(solution)/shard_map/ppermute | solution.py:45
  42.0 17.8 %all_to_all.30 = bf16[16,32,1024]{2,1,0:T(8,128)(2,1)S(1)} all-to-all(bf16[16,32,1024]{2,1,0:T(8,128)(2,1)S(1)} %shard_map.129), channel_id=1, replica_groups=mesh['z_hi'=2,'y'=4,'x'=4,'z_lo'=4,'core'=2] {'y','x'}, dimensions={0} | all-to-all | bytes 2097152 | tf_op jit(solution)/shard_map/all_to_all | solution.py:54
  60.1 1.1 shard_map.130
  61.3 1.5 collective-permute-done.4.got_ref
  63.8 2.0 %collective-permute-start.6 = (bf16[64,512]{1,0:T(8,128)(2,1)S(1)}, bf16[64,512]{1,0:T(8,128)(2,1)S(1)}, u32[]{:S(2)}, u32[]{:S(2)}) collective-permute-start(bf16[64,512]{1,0:T(8,128)(2,1)S(1)} %get-tuple-element.61), channel_id=1, source_target_pairs={{0,4},{2,6},{4,0},{6,2},{1,5},{3,7},{5,1},{7,3},{8,12},{10,14},{12... | collective-permute-start | bytes 196616 | tf_op jit(solution)/shard_map/ppermute | solution.py:151
  65.8 1.0 collective-permute-start.7
  66.9 1.3 collective-permute-done.5
  68.2 2.3 %collective-permute-done.6 = bf16[64,512]{1,0:T(8,128)(2,1)S(1)} collective-permute-done((bf16[64,512]{1,0:T(8,128)(2,1)S(1)}, bf16[64,512]{1,0:T(8,128)(2,1)S(1)}, u32[]{:S(2)}, u32[]{:S(2)}) %collective-permute-start.6) | collective-permute-done | bytes 65568 | tf_op jit(solution)/shard_map/ppermute | solution.py:151
  70.5 2.3 %collective-permute-done.7 = bf16[64,512]{1,0:T(8,128)(2,1)S(1)} collective-permute-done((bf16[64,512]{1,0:T(8,128)(2,1)S(1)}, bf16[64,512]{1,0:T(8,128)(2,1)S(1)}, u32[]{:S(2)}, u32[]{:S(2)}) %collective-permute-start.7) | collective-permute-done | bytes 65568 | tf_op jit(solution)/shard_map/ppermute | solution.py:151
  72.9 2.1 %collective-permute-start.9 = (bf16[64,512]{1,0:T(8,128)(2,1)S(1)}, bf16[64,512]{1,0:T(8,128)(2,1)S(1)}, u32[]{:S(2)}, u32[]{:S(2)}) collective-permute-start(bf16[64,512]{1,0:T(8,128)(2,1)S(1)} %add_convert_fusion.1), channel_id=1, source_target_pairs={{0,128},{1,0},{2,160},{3,32},{4,192},{5,64},{6,224},{7,96},{8,136}... | collective-permute-start | bytes 196616 | tf_op jit(solution)/shard_map/ppermute | solution.py:354
  75.0 4.5 %collective-permute-done.9.attn_ref = bf16[64,512]{1,0:T(8,128)(2,1)S(1)} collective-permute-done((bf16[64,512]{1,0:T(8,128)(2,1)S(1)}, bf16[64,512]{1,0:T(8,128)(2,1)S(1)}, u32[]{:S(2)}, u32[]{:S(2)}) %collective-permute-start.9) | collective-permute-done | bytes 65568 | tf_op jit(solution)/shard_map/ppermute | solution.py:354
  79.5 0.9 copy-done.10
  80.5 1.0 copy-done.5
  81.5 4.3 %all-to-all-start.3 = ((bf16[16,64,512]{2,1,0:T(8,128)(2,1)}), bf16[16,64,512]{2,1,0:T(8,128)(2,1)}, u32[]{:S(2)}, u32[]{:S(2)}) async-start(bf16[16,64,512]{2,1,0:T(8,128)(2,1)} %copy-done.5), calls=%async_computation.3 | async-start | bytes 2097152 | tf_op jit(solution)/shard_map/all_to_all | solution.py:266
  85.8 4.1 %collective-permute-start.8 = (bf16[64,512]{1,0:T(8,128)(2,1)}, bf16[64,512]{1,0:T(8,128)(2,1)S(1)}, u32[]{:S(2)}, u32[]{:S(2)}) collective-permute-start(bf16[64,512]{1,0:T(8,128)(2,1)} %copy-done.14), channel_id=1, source_target_pairs={{0,0},{1,128},{2,32},{3,160},{4,64},{5,192},{6,96},{7,224},{8,8},{... | collective-permute-start | bytes 196616 | tf_op jit(solution)/shard_map/ppermute | solution.py:355
  90.0 6.5 %collective-permute-done.8.attn_ref = bf16[64,512]{1,0:T(8,128)(2,1)S(1)} collective-permute-done((bf16[64,512]{1,0:T(8,128)(2,1)}, bf16[64,512]{1,0:T(8,128)(2,1)S(1)}, u32[]{:S(2)}, u32[]{:S(2)}) %collective-permute-start.8) | collective-permute-done | bytes 65568 | tf_op jit(solution)/shard_map/ppermute | solution.py:355
  96.6 1.0 copy-done.4
  97.6 5.0 %all-to-all-done.3 = bf16[16,64,512]{2,1,0:T(8,128)(2,1)} async-done(((bf16[16,64,512]{2,1,0:T(8,128)(2,1)}), bf16[16,64,512]{2,1,0:T(8,128)(2,1)}, u32[]{:S(2)}, u32[]{:S(2)}) %all-to-all-start.3) | async-done | bytes 1048608 | tf_op jit(solution)/shard_map/all_to_all | solution.py:266
  102.6 4.3 %all-to-all-start.2 = ((bf16[16,64,512]{2,1,0:T(8,128)(2,1)}), bf16[16,64,512]{2,1,0:T(8,128)(2,1)}, u32[]{:S(2)}, u32[]{:S(2)}) async-start(bf16[16,64,512]{2,1,0:T(8,128)(2,1)} %copy-done.4), calls=%async_computation.2 | async-start | bytes 2097152 | tf_op jit(solution)/shard_map/all_to_all | solution.py:266
  107.0 2.7 %shard_map.134 = (bf16[256,2048]{1,0:T(8,128)(2,1)S(1)}, bf16[256,896]{1,0:T(8,128)(2,1)S(1)}) custom-call(bf16[4,4,64,512]{3,2,1,0:T(8,128)(2,1)} %bitcast.17.rows_ref, bf16[1,2048]{1,0:T(2,128)(2,1)S(1)} %reshape.116.gain_ref, bf16[832,2048]{1,0:T(8,128)(2,1)S(1)} %bitcast.33), custom_call_target="tpu_custom_call" | custom-call | flops 1 | bytes 1 | tf_op jit(solution)/shard_map/pallas_call | solution.py:63
  109.7 1.6 shard_map.135
  111.3 1.8 collective-permute-done.10.got_ref
  114.0 5.8 %collective-permute-start.16 = (bf16[32,1792]{1,0:T(8,128)(2,1)}, bf16[32,1792]{1,0:T(8,128)(2,1)}, u32[]{:S(2)}, u32[]{:S(2)}) collective-permute-start(bf16[32,1792]{1,0:T(8,128)(2,1)} %get-tuple-element.78), channel_id=1, source_target_pairs={{0,4},{2,6},{4,0},{6,2},{1,5},{3,7},{5,1},{7,3},{8,12},{10,14},{12... | collective-permute-start | bytes 344072 | tf_op jit(solution)/shard_map/ppermute | solution.py:151
  120.3 3.6 %all-to-all-done.2 = bf16[16,64,512]{2,1,0:T(8,128)(2,1)} async-done(((bf16[16,64,512]{2,1,0:T(8,128)(2,1)}), bf16[16,64,512]{2,1,0:T(8,128)(2,1)}, u32[]{:S(2)}, u32[]{:S(2)}) %all-to-all-start.2) | async-done | bytes 1048608 | tf_op jit(solution)/shard_map/all_to_all | solution.py:266
  123.9 2.7 %shard_map.137 = (bf16[256,2048]{1,0:T(8,128)(2,1)S(1)}, bf16[256,896]{1,0:T(8,128)(2,1)S(1)}) custom-call(bf16[4,4,64,512]{3,2,1,0:T(8,128)(2,1)} %bitcast.12.rows_ref, bf16[1,2048]{1,0:T(2,128)(2,1)S(1)} %reshape.116.gain_ref, bf16[832,2048]{1,0:T(8,128)(2,1)S(1)} %bitcast.34, f32[8,128]{1,0:T(8,128)S(1)} %get-tuple-element.67.refs_0_), custom_call_target="tpu_custom_call" | custom-call | flops 1 | bytes 1 | tf_op jit(solution)/shard_map/pallas_call | solution.py:63
  126.6 1.3 shard_map.138
  128.5 2.6 %collective-permute-done.17.three_ref = bf16[32,1792]{1,0:T(8,128)(2,1)} collective-permute-done((bf16[32,1792]{1,0:T(8,128)(2,1)}, bf16[32,1792]{1,0:T(8,128)(2,1)}, u32[]{:S(2)}, u32[]{:S(2)}) %collective-permute-start.17) | collective-permute-done | bytes 114720 | tf_op jit(solution)/shard_map/ppermute | solution.py:151
  131.2 1.4 shard_map.140.own_ref
  132.5 1.6 collective-permute-start.20
  134.8 1.3 collective-permute-start.18
  136.9 1.6 collective-permute-done.20.three_ref
  138.5 0.9 collective-permute-done.19.two_ref
  139.3 1.2 collective-permute-done.18.one_ref
  140.6 0.9 collective-permute-start.12
  141.6 1.5 collective-permute-start.13
  143.0 1.2 collective-permute-start.14
  144.2 1.3 shard_map.142
  145.5 1.0 copy-done.7
  146.5 5.9 %all-to-all-start.5 = ((bf16[16,16,2048]{2,1,0:T(8,128)(2,1)}), bf16[16,16,2048]{2,1,0:T(8,128)(2,1)}, u32[]{:S(2)}, u32[]{:S(2)}) async-start(bf16[16,16,2048]{2,1,0:T(8,128)(2,1)} %bitcast.38), calls=%async_computation.5 | async-start | bytes 2097152 | tf_op jit(solution)/shard_map/all_to_all | solution.py:266
  152.4 2.7 %collective-permute-done.14.three_ref = bf16[32,1792]{1,0:T(8,128)(2,1)} collective-permute-done((bf16[32,1792]{1,0:T(8,128)(2,1)}, bf16[32,1792]{1,0:T(8,128)(2,1)}, u32[]{:S(2)}, u32[]{:S(2)}) %collective-permute-start.14) | collective-permute-done | bytes 114720 | tf_op jit(solution)/shard_map/ppermute | solution.py:151
  155.1 1.2 shard_map.143.own_ref
  156.3 1.0 collective-permute-start.24
  157.4 1.2 collective-permute-start.23
  158.6 1.3 collective-permute-start.22
  159.9 2.9 %collective-permute-done.24.three_ref = bf16[32,832]{1,0:T(8,128)(2,1)S(1)} collective-permute-done((bf16[32,832]{1,0:T(8,128)(2,1)S(1)}, bf16[32,832]{1,0:T(8,128)(2,1)S(1)}, u32[]{:S(2)}, u32[]{:S(2)}) %collective-permute-start.24) | collective-permute-done | bytes 53280 | tf_op jit(solution)/shard_map/ppermute | solution.py:151
  162.9 1.5 collective-permute-done.25.other_ref
  164.4 1.7 shard_map.145
  166.1 1.0 copy-done.8
  167.1 2.7 %all-to-all-done.5.parts_ref = bf16[16,16,2048]{2,1,0:T(8,128)(2,1)} async-done(((bf16[16,16,2048]{2,1,0:T(8,128)(2,1)}), bf16[16,16,2048]{2,1,0:T(8,128)(2,1)}, u32[]{:S(2)}, u32[]{:S(2)}) %all-to-all-start.5) | async-done | bytes 1048608 | tf_op jit(solution)/shard_map/all_to_all | solution.py:266
  169.8 4.3 %all-to-all-start.4 = ((bf16[16,16,2048]{2,1,0:T(8,128)(2,1)}), bf16[16,16,2048]{2,1,0:T(8,128)(2,1)S(1)}, u32[]{:S(2)}, u32[]{:S(2)}) async-start(bf16[16,16,2048]{2,1,0:T(8,128)(2,1)} %bitcast.39), calls=%async_computation.4 | async-start | bytes 2097152 | tf_op jit(solution)/shard_map/all_to_all | solution.py:266
  174.1 1.4 shard_map.147
  175.5 4.4 %collective-permute-start.26 = (bf16[16,2048]{1,0:T(8,128)(2,1)S(1)}, bf16[16,2048]{1,0:T(8,128)(2,1)S(1)}, u32[]{:S(2)}, u32[]{:S(2)}) collective-permute-start(bf16[16,2048]{1,0:T(8,128)(2,1)S(1)} %shard_map.147), channel_id=1, source_target_pairs={{0,128},{128,0},{1,129},{129,1},{2,130},{130,2},{3,131},{131,3},{4... | collective-permute-start | bytes 196616 | tf_op jit(solution)/shard_map/ppermute | solution.py:45
  179.9 0.9 convert_bitcast_fusion
  180.8 11.1 %all-to-all-done.4.parts_ref = bf16[16,16,2048]{2,1,0:T(8,128)(2,1)S(1)} async-done(((bf16[16,16,2048]{2,1,0:T(8,128)(2,1)}), bf16[16,16,2048]{2,1,0:T(8,128)(2,1)S(1)}, u32[]{:S(2)}, u32[]{:S(2)}) %all-to-all-start.4) | async-done | bytes 1048608 | tf_op jit(solution)/shard_map/all_to_all | solution.py:266
  (77 shorter events, 11.4 us)
Async XLA Ops:
  0.0 60.1 %copy-start.6 = (bf16[1024,512]{1,0:T(8,128)(2,1)S(1)}, bf16[1024,512]{1,0:T(8,128)(2,1)}, u32[]{:S(2)}) copy-start(bf16[1024,512]{1,0:T(8,128)(2,1)} %weight_ref.3) | copy-start | bytes 3145732
  2.8 26.0 %all-to-all-start = ((bf16[32,2,1280]{2,1,0:T(2,128)(2,1)}), bf16[32,2,1280]{2,1,0:T(2,128)(2,1)S(1)}, u32[]{:S(2)}, u32[]{:S(2)}) async-start(bf16[32,2,1280]{2,1,0:T(2,128)(2,1)} %reshape.107), calls=%async_computation | async-start | bytes 327680 | tf_op jit(solution)/shard_map/all_to_all | solution.py:307
  15.8 0.8 copy-start.13
  16.7 12.2 %collective-permute-start = (bf16[16,512]{1,0:T(8,128)(2,1)S(1)}, bf16[16,512]{1,0:T(8,128)(2,1)S(1)}, u32[]{:S(2)}, u32[]{:S(2)}) collective-permute-start(bf16[16,512]{1,0:T(8,128)(2,1)S(1)} %get-tuple-element.48), channel_id=1, source_target_pairs={{0,8},{8,0},{16,24},{24,16},{1,9},{9,1},{17,25},{25,17},{2,10},{10... | collective-permute-start | bytes 49160 | tf_op jit(solution)/shard_map/ppermute | solution.py:329
  18.5 10.4 %collective-permute-start.1 = (bf16[16,512]{1,0:T(8,128)(2,1)S(1)}, bf16[16,512]{1,0:T(8,128)(2,1)S(1)}, u32[]{:S(2)}, u32[]{:S(2)}) collective-permute-start(bf16[16,512]{1,0:T(8,128)(2,1)S(1)} %get-tuple-element.49), channel_id=1, source_target_pairs={{0,16},{8,24},{16,0},{24,8},{1,17},{9,25},{17,1},{25,9},{2,18},{10... | collective-permute-start | bytes 49160 | tf_op jit(solution)/shard_map/ppermute | solution.py:329
  21.1 7.7 %collective-permute-start.2 = (bf16[16,512]{1,0:T(8,128)(2,1)S(1)}, bf16[16,512]{1,0:T(8,128)(2,1)S(1)}, u32[]{:S(2)}, u32[]{:S(2)}) collective-permute-start(bf16[16,512]{1,0:T(8,128)(2,1)S(1)} %get-tuple-element.50), channel_id=1, source_target_pairs={{0,24},{8,16},{16,8},{24,0},{1,25},{9,17},{17,9},{25,1},{2,26},{10... | collective-permute-start | bytes 49160 | tf_op jit(solution)/shard_map/ppermute | solution.py:329
  28.9 0.9 copy-start.11
  29.8 0.9 copy-start.12
  31.6 9.7 %collective-permute-start.3 = (bf16[48,1024]{1,0:T(8,128)(2,1)S(1)}, bf16[48,1024]{1,0:T(8,128)(2,1)S(1)}, u32[]{:S(2)}, u32[]{:S(2)}) collective-permute-start(bf16[48,1024]{1,0:T(8,128)(2,1)S(1)} %shard_map.128.near_ref.tok_ref), channel_id=1, source_target_pairs={{0,128},{128,0},{1,129},{129,1},{2,130},{130,2},{3,131},{131,3},{4... | collective-permute-start | bytes 294920 | tf_op jit(solution)/shard_map/ppermute | solution.py:45
  41.3 0.6 copy-start.9
  61.1 1.6 collective-permute-start.4
  63.4 4.8 %collective-permute-start.5 = (bf16[64,512]{1,0:T(8,128)(2,1)S(1)}, bf16[64,512]{1,0:T(8,128)(2,1)S(1)}, u32[]{:S(2)}, u32[]{:S(2)}) collective-permute-start(bf16[64,512]{1,0:T(8,128)(2,1)S(1)} %get-tuple-element.60), channel_id=1, source_target_pairs={{0,2},{2,0},{4,6},{6,4},{1,3},{3,1},{5,7},{7,5},{8,10},{10,8},{12,... | collective-permute-start | bytes 196616 | tf_op jit(solution)/shard_map/ppermute | solution.py:151
  63.8 6.7 %collective-permute-start.6 = (bf16[64,512]{1,0:T(8,128)(2,1)S(1)}, bf16[64,512]{1,0:T(8,128)(2,1)S(1)}, u32[]{:S(2)}, u32[]{:S(2)}) collective-permute-start(bf16[64,512]{1,0:T(8,128)(2,1)S(1)} %get-tuple-element.61), channel_id=1, source_target_pairs={{0,4},{2,6},{4,0},{6,2},{1,5},{3,7},{5,1},{7,3},{8,12},{10,14},{12... | collective-permute-start | bytes 196616 | tf_op jit(solution)/shard_map/ppermute | solution.py:151
  65.8 7.0 %collective-permute-start.7 = (bf16[64,512]{1,0:T(8,128)(2,1)S(1)}, bf16[64,512]{1,0:T(8,128)(2,1)S(1)}, u32[]{:S(2)}, u32[]{:S(2)}) collective-permute-start(bf16[64,512]{1,0:T(8,128)(2,1)S(1)} %get-tuple-element.62), channel_id=1, source_target_pairs={{0,6},{2,4},{4,2},{6,0},{1,7},{3,5},{5,3},{7,1},{8,14},{10,12},{12... | collective-permute-start | bytes 196616 | tf_op jit(solution)/shard_map/ppermute | solution.py:151
  72.9 34.1 %copy-start = (bf16[2048,832]{0,1:T(8,128)(2,1)S(1)}, bf16[2048,832]{0,1:T(8,128)(2,1)}, u32[]{:S(2)}) copy-start(bf16[2048,832]{0,1:T(8,128)(2,1)} %param.23) | copy-start | bytes 10223620
  72.9 2.1 %copy-start.14 = (bf16[64,512]{1,0:T(8,128)(2,1)}, bf16[64,512]{1,0:T(8,128)(2,1)S(1)}, u32[]{:S(2)}) copy-start(bf16[64,512]{1,0:T(8,128)(2,1)S(1)} %add_convert_fusion.1) | copy-start | bytes 196612
  72.9 6.6 %collective-permute-start.9 = (bf16[64,512]{1,0:T(8,128)(2,1)S(1)}, bf16[64,512]{1,0:T(8,128)(2,1)S(1)}, u32[]{:S(2)}, u32[]{:S(2)}) collective-permute-start(bf16[64,512]{1,0:T(8,128)(2,1)S(1)} %add_convert_fusion.1), channel_id=1, source_target_pairs={{0,128},{1,0},{2,160},{3,32},{4,192},{5,64},{6,224},{7,96},{8,136}... | collective-permute-start | bytes 196616 | tf_op jit(solution)/shard_map/ppermute | solution.py:354
  79.5 0.9 copy-start.10
  80.4 26.6 %copy-start.15 = (bf16[2048]{0:T(1024)(128)(2,1)S(1)}, bf16[2048]{0:T(1024)(128)(2,1)}, u32[]{:S(2)}) copy-start(bf16[2048]{0:T(1024)(128)(2,1)} %param.22) | copy-start | bytes 12292
  80.5 1.0 copy-start.5
  81.5 21.1 %all-to-all-start.3 = ((bf16[16,64,512]{2,1,0:T(8,128)(2,1)}), bf16[16,64,512]{2,1,0:T(8,128)(2,1)}, u32[]{:S(2)}, u32[]{:S(2)}) async-start(bf16[16,64,512]{2,1,0:T(8,128)(2,1)} %copy-done.5), calls=%async_computation.3 | async-start | bytes 2097152 | tf_op jit(solution)/shard_map/all_to_all | solution.py:266
  85.8 10.6 %collective-permute-start.8 = (bf16[64,512]{1,0:T(8,128)(2,1)}, bf16[64,512]{1,0:T(8,128)(2,1)S(1)}, u32[]{:S(2)}, u32[]{:S(2)}) collective-permute-start(bf16[64,512]{1,0:T(8,128)(2,1)} %copy-done.14), channel_id=1, source_target_pairs={{0,0},{1,128},{2,32},{3,160},{4,64},{5,192},{6,96},{7,224},{8,8},{... | collective-permute-start | bytes 196616 | tf_op jit(solution)/shard_map/ppermute | solution.py:355
  96.6 1.0 copy-start.4
  102.6 21.3 %all-to-all-start.2 = ((bf16[16,64,512]{2,1,0:T(8,128)(2,1)}), bf16[16,64,512]{2,1,0:T(8,128)(2,1)}, u32[]{:S(2)}, u32[]{:S(2)}) async-start(bf16[16,64,512]{2,1,0:T(8,128)(2,1)} %copy-done.4), calls=%async_computation.2 | async-start | bytes 2097152 | tf_op jit(solution)/shard_map/all_to_all | solution.py:266
  107.0 2.7 %copy-start.1 = (bf16[2048,832]{0,1:T(8,128)(2,1)S(1)}, bf16[2048,832]{0,1:T(8,128)(2,1)}, u32[]{:S(2)}) copy-start(bf16[2048,832]{0,1:T(8,128)(2,1)} %param.24) | copy-start | bytes 10223620
  111.3 1.8 collective-permute-start.10
  113.9 14.2 %collective-permute-start.15 = (bf16[32,1792]{1,0:T(8,128)(2,1)}, bf16[32,1792]{1,0:T(8,128)(2,1)}, u32[]{:S(2)}, u32[]{:S(2)}) collective-permute-start(bf16[32,1792]{1,0:T(8,128)(2,1)} %get-tuple-element.77), channel_id=1, source_target_pairs={{0,2},{2,0},{4,6},{6,4},{1,3},{3,1},{5,7},{7,5},{8,10},{10,8},{12,... | collective-permute-start | bytes 344072 | tf_op jit(solution)/shard_map/ppermute | solution.py:151
  114.0 14.6 %collective-permute-start.16 = (bf16[32,1792]{1,0:T(8,128)(2,1)}, bf16[32,1792]{1,0:T(8,128)(2,1)}, u32[]{:S(2)}, u32[]{:S(2)}) collective-permute-start(bf16[32,1792]{1,0:T(8,128)(2,1)} %get-tuple-element.78), channel_id=1, source_target_pairs={{0,4},{2,6},{4,0},{6,2},{1,5},{3,7},{5,1},{7,3},{8,12},{10,14},{12... | collective-permute-start | bytes 344072 | tf_op jit(solution)/shard_map/ppermute | solution.py:151
  119.7 11.4 %collective-permute-start.17 = (bf16[32,1792]{1,0:T(8,128)(2,1)}, bf16[32,1792]{1,0:T(8,128)(2,1)}, u32[]{:S(2)}, u32[]{:S(2)}) collective-permute-start(bf16[32,1792]{1,0:T(8,128)(2,1)} %get-tuple-element.79), channel_id=1, source_target_pairs={{0,6},{2,4},{4,2},{6,0},{1,7},{3,5},{5,3},{7,1},{8,14},{10,12},{12... | collective-permute-start | bytes 344072 | tf_op jit(solution)/shard_map/ppermute | solution.py:151
  123.9 2.7 %copy-start.2 = (bf16[2048,832]{0,1:T(8,128)(2,1)S(1)}, bf16[2048,832]{0,1:T(8,128)(2,1)}, u32[]{:S(2)}) copy-start(bf16[2048,832]{0,1:T(8,128)(2,1)} %param.24) | copy-start | bytes 10223620
  128.0 8.1 %collective-permute-start.11 = (bf16[128,1792]{1,0:T(8,128)(2,1)S(1)}, bf16[128,1792]{1,0:T(8,128)(2,1)S(1)}, u32[]{:S(2)}, u32[]{:S(2)}) collective-permute-start(bf16[128,1792]{1,0:T(8,128)(2,1)S(1)} %get-tuple-element.71), channel_id=1, source_target_pairs={{0,1},{1,0},{2,3},{3,2},{4,5},{5,4},{6,7},{7,6},{8,9},{9,8},{10,11... | collective-permute-start | bytes 1376264 | tf_op jit(solution)/shard_map/ppermute | solution.py:45
  131.2 13.1 %copy-start.3 = (bf16[832,2048]{1,0:T(8,128)(2,1)S(1)}, bf16[832,2048]{1,0:T(8,128)(2,1)}, u32[]{:S(2)}) copy-start(bf16[832,2048]{1,0:T(8,128)(2,1)} %weight_ref.5) | copy-start | bytes 10223620
  132.5 5.9 %collective-permute-start.20 = (bf16[32,832]{1,0:T(8,128)(2,1)S(1)}, bf16[32,832]{1,0:T(8,128)(2,1)S(1)}, u32[]{:S(2)}, u32[]{:S(2)}) collective-permute-start(bf16[32,832]{1,0:T(8,128)(2,1)S(1)} %shard_map.140.own_ref), channel_id=1, source_target_pairs={{0,6},{2,4},{4,2},{6,0},{1,7},{3,5},{5,3},{7,1},{8,14},{10,12},{12... | collective-permute-start | bytes 159752 | tf_op jit(solution)/shard_map/ppermute | solution.py:151
  134.1 5.2 %collective-permute-start.19 = (bf16[32,832]{1,0:T(8,128)(2,1)S(1)}, bf16[32,832]{1,0:T(8,128)(2,1)S(1)}, u32[]{:S(2)}, u32[]{:S(2)}) collective-permute-start(bf16[32,832]{1,0:T(8,128)(2,1)S(1)} %shard_map.140.own_ref), channel_id=1, source_target_pairs={{0,4},{2,6},{4,0},{6,2},{1,5},{3,7},{5,1},{7,3},{8,12},{10,14},{12... | collective-permute-start | bytes 159752 | tf_op jit(solution)/shard_map/ppermute | solution.py:151
  134.8 5.7 %collective-permute-start.18 = (bf16[32,832]{1,0:T(8,128)(2,1)S(1)}, bf16[32,832]{1,0:T(8,128)(2,1)S(1)}, u32[]{:S(2)}, u32[]{:S(2)}) collective-permute-start(bf16[32,832]{1,0:T(8,128)(2,1)S(1)} %shard_map.140.own_ref), channel_id=1, source_target_pairs={{0,2},{2,0},{4,6},{6,4},{1,3},{3,1},{5,7},{7,5},{8,10},{10,8},{12,... | collective-permute-start | bytes 159752 | tf_op jit(solution)/shard_map/ppermute | solution.py:151
  140.5 3.7 %collective-permute-start.21 = (bf16[128,832]{1,0:T(8,128)(2,1)S(1)}, bf16[128,832]{1,0:T(8,128)(2,1)S(1)}, u32[]{:S(2)}, u32[]{:S(2)}) collective-permute-start(bf16[128,832]{1,0:T(8,128)(2,1)S(1)} %shard_map.141.own_ref), channel_id=1, source_target_pairs={{0,1},{1,0},{2,3},{3,2},{4,5},{5,4},{6,7},{7,6},{8,9},{9,8},{10,11... | collective-permute-start | bytes 638984 | tf_op jit(solution)/shard_map/ppermute | solution.py:45
  140.6 11.7 %collective-permute-start.12 = (bf16[32,1792]{1,0:T(8,128)(2,1)}, bf16[32,1792]{1,0:T(8,128)(2,1)}, u32[]{:S(2)}, u32[]{:S(2)}) collective-permute-start(bf16[32,1792]{1,0:T(8,128)(2,1)} %get-tuple-element.73), channel_id=1, source_target_pairs={{0,2},{2,0},{4,6},{6,4},{1,3},{3,1},{5,7},{7,5},{8,10},{10,8},{12,... | collective-permute-start | bytes 344072 | tf_op jit(solution)/shard_map/ppermute | solution.py:151
  141.6 10.8 %collective-permute-start.13 = (bf16[32,1792]{1,0:T(8,128)(2,1)}, bf16[32,1792]{1,0:T(8,128)(2,1)}, u32[]{:S(2)}, u32[]{:S(2)}) collective-permute-start(bf16[32,1792]{1,0:T(8,128)(2,1)} %get-tuple-element.74), channel_id=1, source_target_pairs={{0,4},{2,6},{4,0},{6,2},{1,5},{3,7},{5,1},{7,3},{8,12},{10,14},{12... | collective-permute-start | bytes 344072 | tf_op jit(solution)/shard_map/ppermute | solution.py:151
  143.0 12.1 %collective-permute-start.14 = (bf16[32,1792]{1,0:T(8,128)(2,1)}, bf16[32,1792]{1,0:T(8,128)(2,1)}, u32[]{:S(2)}, u32[]{:S(2)}) collective-permute-start(bf16[32,1792]{1,0:T(8,128)(2,1)} %get-tuple-element.75), channel_id=1, source_target_pairs={{0,6},{2,4},{4,2},{6,0},{1,7},{3,5},{5,3},{7,1},{8,14},{10,12},{12... | collective-permute-start | bytes 344072 | tf_op jit(solution)/shard_map/ppermute | solution.py:151
  145.5 1.0 copy-start.7
  146.5 23.3 %all-to-all-start.5 = ((bf16[16,16,2048]{2,1,0:T(8,128)(2,1)}), bf16[16,16,2048]{2,1,0:T(8,128)(2,1)}, u32[]{:S(2)}, u32[]{:S(2)}) async-start(bf16[16,16,2048]{2,1,0:T(8,128)(2,1)} %bitcast.38), calls=%async_computation.5 | async-start | bytes 2097152 | tf_op jit(solution)/shard_map/all_to_all | solution.py:266
  156.3 6.4 %collective-permute-start.24 = (bf16[32,832]{1,0:T(8,128)(2,1)S(1)}, bf16[32,832]{1,0:T(8,128)(2,1)S(1)}, u32[]{:S(2)}, u32[]{:S(2)}) collective-permute-start(bf16[32,832]{1,0:T(8,128)(2,1)S(1)} %shard_map.143.own_ref), channel_id=1, source_target_pairs={{0,6},{2,4},{4,2},{6,0},{1,7},{3,5},{5,3},{7,1},{8,14},{10,12},{12... | collective-permute-start | bytes 159752 | tf_op jit(solution)/shard_map/ppermute | solution.py:151
  157.4 5.4 %collective-permute-start.23 = (bf16[32,832]{1,0:T(8,128)(2,1)S(1)}, bf16[32,832]{1,0:T(8,128)(2,1)S(1)}, u32[]{:S(2)}, u32[]{:S(2)}) collective-permute-start(bf16[32,832]{1,0:T(8,128)(2,1)S(1)} %shard_map.143.own_ref), channel_id=1, source_target_pairs={{0,4},{2,6},{4,0},{6,2},{1,5},{3,7},{5,1},{7,3},{8,12},{10,14},{12... | collective-permute-start | bytes 159752 | tf_op jit(solution)/shard_map/ppermute | solution.py:151
  158.6 4.2 %collective-permute-start.22 = (bf16[32,832]{1,0:T(8,128)(2,1)S(1)}, bf16[32,832]{1,0:T(8,128)(2,1)S(1)}, u32[]{:S(2)}, u32[]{:S(2)}) collective-permute-start(bf16[32,832]{1,0:T(8,128)(2,1)S(1)} %shard_map.143.own_ref), channel_id=1, source_target_pairs={{0,2},{2,0},{4,6},{6,4},{1,3},{3,1},{5,7},{7,5},{8,10},{10,8},{12,... | collective-permute-start | bytes 159752 | tf_op jit(solution)/shard_map/ppermute | solution.py:151
  162.8 1.6 collective-permute-start.25
  166.1 1.0 copy-start.8
  169.8 22.1 %all-to-all-start.4 = ((bf16[16,16,2048]{2,1,0:T(8,128)(2,1)}), bf16[16,16,2048]{2,1,0:T(8,128)(2,1)S(1)}, u32[]{:S(2)}, u32[]{:S(2)}) async-start(bf16[16,16,2048]{2,1,0:T(8,128)(2,1)} %bitcast.39), calls=%async_computation.4 | async-start | bytes 2097152 | tf_op jit(solution)/shard_map/all_to_all | solution.py:266
  175.5 16.6 %collective-permute-start.26 = (bf16[16,2048]{1,0:T(8,128)(2,1)S(1)}, bf16[16,2048]{1,0:T(8,128)(2,1)S(1)}, u32[]{:S(2)}, u32[]{:S(2)}) collective-permute-start(bf16[16,2048]{1,0:T(8,128)(2,1)S(1)} %shard_map.147), channel_id=1, source_target_pairs={{0,128},{128,0},{1,129},{129,1},{2,130},{130,2},{3,131},{131,3},{4... | collective-permute-start | bytes 196616 | tf_op jit(solution)/shard_map/ppermute | solution.py:45

commit v5 on v4

--- a/solution.py
+++ b/solution.py
@@ -85,13 +85,13 @@
 
 def attend_body(
     rows, cache_len, heads, place_x, slot_ref, got_ref, len_ref, own_tok, one_tok, two_tok, three_tok,
-    key_ref, value_ref, out_ref,
+    key_ref, value_ref, out_ref, tok_ref,
 ):
     cols = own_tok.shape[1]
     for step, piece in enumerate((own_tok, one_tok, two_tok, three_tok)):
         group = place_x[0] ^ step
-        at = pl.ds(pl.multiple_of(rows + (group & 1) * rows, rows), rows)
-        out_ref[at, pl.ds(pl.multiple_of((group >> 1) * cols, cols), cols)] = piece[...]
+        at = pl.ds(pl.multiple_of((group & 1) * rows, rows), rows)
+        tok_ref[at, pl.ds(pl.multiple_of((group >> 1) * cols, cols), cols)] = piece[...]
     slots = lax.broadcasted_iota(jnp.int32, (rows, got_ref.shape[0]), 1)
     compact = (slot_ref[...] == slots).astype(F32).astype(BF)
     arrived = dot(compact, got_ref[...])
@@ -117,7 +117,7 @@
     own_weight = (exp_own / total).astype(BF).astype(F32)
     out = (dot(weights, value_ref[...]) + own_weight * value_new).astype(BF)
     for j in range(heads):
-        out_ref[:rows, j * HD : (j + 1) * HD] = out[j * rows : (j + 1) * rows]
+        out_ref[:, j * HD : (j + 1) * HD] = out[j * rows : (j + 1) * rows]
 
 
 def project_body(send_pos, keep_pos, heads_ref, weight_ref, send_ref, keep_ref):
@@ -213,7 +213,7 @@
 def residual_body(rows, attn_ref, tok_ref, out_ref):
     cols = attn_ref.shape[1]
     for group in range(attn_ref.shape[0] // rows):
-        at = rows + (group & 1) * rows
+        at = (group & 1) * rows
         side = (group >> 1) * cols
         tok = tok_ref[at : at + rows, side : side + cols].astype(F32)
         total = (attn_ref[group * rows : (group + 1) * rows].astype(F32) + tok).astype(BF)
@@ -330,9 +330,9 @@
     ]
 
     caches = [cache.reshape(rows_dev * cache_len, HD) for cache in (key_cache, value_cache)]
-    heads = call(
+    heads, near_tok = call(
         functools.partial(attend_body, rows_dev, cache_len, q_cols // HD),
-        shape((3 * rows_dev, q_cols), BF),
+        [shape((rows_dev, q_cols), BF), shape((2 * rows_dev, q_cols), BF)],
         arrival,
         received.reshape(groups * capacity, packed.shape[1]),
         lengths.reshape(rows_dev, 1),
@@ -340,7 +340,7 @@
         *caches,
         scalars=(place_x,),
     )
-    far_heads = swap(heads, "z_hi")
+    far_heads, far_tok = swap(heads, "z_hi"), swap(near_tok, "z_hi")
     copies = call(
         functools.partial(heads_body, rows_dev), shape((plane, 2 * rows_dev, q_cols), BF), heads, far_heads
     )
@@ -357,7 +357,7 @@
     hid = down_weight.shape[0]
     gate_t, up_t = gate_weight.T, up_weight.T
     gathered = []
-    for attn, tok in ((far, far_heads), (near, heads)):
+    for attn, tok in ((far, far_tok), (near, near_tok)):
         copies = call(
             functools.partial(residual_body, rows_dev), shape((plane, rows // 8, quarter), BF), attn, tok
         )

time: 194 us -> 193 us (level); the launches traced: 193 us -> 189 us
  waiting for transfers between devices: 68.2 us -> 54.4 us
  starting transfers between devices: 70.9 us -> 82.1 us
    ppermute x7 -> x8, starting transfers between devices: 7.47 us -> 16.9 us  [swap(): return lax.ppermute(v, axis, [(0, 1), (1, 0)])]
    ppermute x15, waiting for transfers between devices: 18.3 us -> 12 us  [line_send(): lax.ppermute(piece, 'z_lo', [(i, i ^ step) for i in range(4)])]
    all_to_all x4, waiting for transfers between devices: 22.5 us -> 18 us  [all_to_all(): return lax.all_to_all(v, axes, split_axis=0, concat_axis=0, tiled=True)]
    ppermute x7 -> x8, waiting for transfers between devices: 11.9 us -> 10 us  [swap(): return lax.ppermute(v, axis, [(0, 1), (1, 0)])]
    unnamed x32 -> x26, local copies, waits for them, and re-layouts: 8.09 us -> 6.59 us
  transfers between devices with their start and end apart: 32 -> 33, of which waited for: 21 -> 18; matrix products, arithmetic and copies ran while one was open for 2% -> 2% of each run, Pallas kernels for 9% -> 9%
where the time goes in v5:
time: 193 us; the launch traced here: 189 us
  starting transfers between devices  82.1 us (43%)
  waiting for transfers between devices  54.4 us (28%)
  Pallas kernels  19.7 us (10%)
  blocking collectives  17.8 us (9%)
  local copies, waits for them, and re-layouts  9.37 us (5%)
  other arithmetic  3.86 us (2%)
    pallas_call x21, Pallas kernels, call(): pl.pallas_call(body, out_shape=out_shape, in_specs=specs, out_specs=whole...  19.7 us
    ppermute x15, starting transfers between devices, line_send(): lax.ppermute(piece, 'z_lo', [(i, i ^ step) for i in range(4)])  19.7 us
    all_to_all x4, starting transfers between devices, all_to_all(): return lax.all_to_all(v, axes, split_axis=0, concat_axis=0, tiled=True)  19.1 us
    all_to_all x4, waiting for transfers between devices, all_to_all(): return lax.all_to_all(v, axes, split_axis=0, concat_axis=0, tiled=True)  18 us
    all_to_all x1, blocking collectives, exchange(): got = lax.all_to_all(copies, YX, split_axis=0, concat_axis=0, tiled=True)  17.8 us
    ppermute x8, starting transfers between devices, swap(): return lax.ppermute(v, axis, [(0, 1), (1, 0)])  16.9 us
    all_to_all x1, starting transfers between devices, shards(): lax.all_to_all(bucket, GRP, split_axis=0, concat_axis=0, tiled=True)  13 us
    ppermute x15, waiting for transfers between devices, line_send(): lax.ppermute(piece, 'z_lo', [(i, i ^ step) for i in range(4)])  12 us
  transfers between devices with their start and end apart: 33, of which 18 were waited for; matrix products, arithmetic and copies ran while one was open for 2% of the time, Pallas kernels for 9%

profile of v5, /device:TPU:32, one launch (start us, length us, event | category | flops | bytes accessed | tf_op | source)
XLA Modules:
  0.0 188.7 jit_solution(4312424727789850252)
XLA Ops:
  0.0 0.8 reshape.106
  1.1 1.0 convolution_convert_fusion
  2.8 13.0 %all-to-all-start = ((bf16[32,2,1280]{2,1,0:T(2,128)(2,1)}), bf16[32,2,1280]{2,1,0:T(2,128)(2,1)S(1)}, u32[]{:S(2)}, u32[]{:S(2)}) async-start(bf16[32,2,1280]{2,1,0:T(2,128)(2,1)} %reshape.107), calls=%async_computation | async-start | bytes 327680 | tf_op jit(solution)/shard_map/all_to_all | solution.py:307
  15.8 0.8 copy-done.11
  16.7 1.8 collective-permute-start
  18.5 2.7 %collective-permute-start.1 = (bf16[16,512]{1,0:T(8,128)(2,1)S(1)}, bf16[16,512]{1,0:T(8,128)(2,1)S(1)}, u32[]{:S(2)}, u32[]{:S(2)}) collective-permute-start(bf16[16,512]{1,0:T(8,128)(2,1)S(1)} %get-tuple-element.51), channel_id=1, source_target_pairs={{0,16},{8,24},{16,0},{24,8},{1,17},{9,25},{17,1},{25,9},{2,18},{10... | collective-permute-start | bytes 49160 | tf_op jit(solution)/shard_map/ppermute | solution.py:329
  21.4 1.2 convert_reduce_fusion.1
  24.3 4.5 %all-to-all-done = bf16[32,2,1280]{2,1,0:T(2,128)(2,1)S(1)} async-done(((bf16[32,2,1280]{2,1,0:T(2,128)(2,1)}), bf16[32,2,1280]{2,1,0:T(2,128)(2,1)S(1)}, u32[]{:S(2)}, u32[]{:S(2)}) %all-to-all-start) | async-done | bytes 163872 | tf_op jit(solution)/shard_map/all_to_all | solution.py:307
  28.9 0.9 copy-done.9
  29.8 0.9 copy-done.10
  30.7 0.9 shard_map.128
  31.6 2.7 %collective-permute-start.3 = (bf16[16,1024]{1,0:T(8,128)(2,1)S(1)}, bf16[16,1024]{1,0:T(8,128)(2,1)S(1)}, u32[]{:S(2)}, u32[]{:S(2)}) collective-permute-start(bf16[16,1024]{1,0:T(8,128)(2,1)S(1)} %get-tuple-element.53.near_ref), channel_id=1, source_target_pairs={{0,128},{128,0},{1,129},{129,1},{2,130},{130,2},{3,131},{131,3},{4... | collective-permute-start | bytes 98312 | tf_op jit(solution)/shard_map/ppermute | solution.py:45
  34.3 5.2 %collective-permute-done.3.far_ref = bf16[16,1024]{1,0:T(8,128)(2,1)S(1)} collective-permute-done((bf16[16,1024]{1,0:T(8,128)(2,1)S(1)}, bf16[16,1024]{1,0:T(8,128)(2,1)S(1)}, u32[]{:S(2)}, u32[]{:S(2)}) %collective-permute-start.3) | collective-permute-done | bytes 32800 | tf_op jit(solution)/shard_map/ppermute | solution.py:45
  39.6 17.8 %all_to_all.30 = bf16[16,32,1024]{2,1,0:T(8,128)(2,1)S(1)} all-to-all(bf16[16,32,1024]{2,1,0:T(8,128)(2,1)S(1)} %shard_map.129), channel_id=1, replica_groups=mesh['z_hi'=2,'y'=4,'x'=4,'z_lo'=4,'core'=2] {'y','x'}, dimensions={0} | all-to-all | bytes 2097152 | tf_op jit(solution)/shard_map/all_to_all | solution.py:54
  57.7 1.1 shard_map.130
  58.9 1.5 collective-permute-done.4.got_ref
  61.0 0.9 collective-permute-start.5
  61.9 1.6 collective-permute-start.6
  63.5 1.0 collective-permute-start.7
  64.5 4.3 %collective-permute-start.10 = (bf16[32,1024]{1,0:T(8,128)(2,1)S(1)}, bf16[32,1024]{1,0:T(8,128)(2,1)S(1)}, u32[]{:S(2)}, u32[]{:S(2)}) collective-permute-start(bf16[32,1024]{1,0:T(8,128)(2,1)S(1)} %get-tuple-element.66.tok_ref), channel_id=1, source_target_pairs={{0,128},{128,0},{1,129},{129,1},{2,130},{130,2},{3,131},{131,3},{4... | collective-permute-start | bytes 196616 | tf_op jit(solution)/shard_map/ppermute | solution.py:45
  68.8 2.7 %collective-permute-done.7 = bf16[64,512]{1,0:T(8,128)(2,1)S(1)} collective-permute-done((bf16[64,512]{1,0:T(8,128)(2,1)S(1)}, bf16[64,512]{1,0:T(8,128)(2,1)S(1)}, u32[]{:S(2)}, u32[]{:S(2)}) %collective-permute-start.7) | collective-permute-done | bytes 65568 | tf_op jit(solution)/shard_map/ppermute | solution.py:151
  71.6 4.0 %collective-permute-start.9 = (bf16[64,512]{1,0:T(8,128)(2,1)S(1)}, bf16[64,512]{1,0:T(8,128)(2,1)S(1)}, u32[]{:S(2)}, u32[]{:S(2)}) collective-permute-start(bf16[64,512]{1,0:T(8,128)(2,1)S(1)} %add_convert_fusion.1), channel_id=1, source_target_pairs={{0,128},{1,0},{2,160},{3,32},{4,192},{5,64},{6,224},{7,96},{8,136}... | collective-permute-start | bytes 196616 | tf_op jit(solution)/shard_map/ppermute | solution.py:354
  75.6 3.7 %collective-permute-done.9.attn_ref = bf16[64,512]{1,0:T(8,128)(2,1)S(1)} collective-permute-done((bf16[64,512]{1,0:T(8,128)(2,1)S(1)}, bf16[64,512]{1,0:T(8,128)(2,1)S(1)}, u32[]{:S(2)}, u32[]{:S(2)}) %collective-permute-start.9) | collective-permute-done | bytes 65568 | tf_op jit(solution)/shard_map/ppermute | solution.py:354
  79.4 1.0 copy-done.5
  80.4 4.3 %all-to-all-start.3 = ((bf16[16,64,512]{2,1,0:T(8,128)(2,1)}), bf16[16,64,512]{2,1,0:T(8,128)(2,1)}, u32[]{:S(2)}, u32[]{:S(2)}) async-start(bf16[16,64,512]{2,1,0:T(8,128)(2,1)} %copy-done.5), calls=%async_computation.3 | async-start | bytes 2097152 | tf_op jit(solution)/shard_map/all_to_all | solution.py:266
  84.8 4.7 %collective-permute-start.8 = (bf16[64,512]{1,0:T(8,128)(2,1)S(1)}, bf16[64,512]{1,0:T(8,128)(2,1)S(1)}, u32[]{:S(2)}, u32[]{:S(2)}) collective-permute-start(bf16[64,512]{1,0:T(8,128)(2,1)S(1)} %add_convert_fusion.1), channel_id=1, source_target_pairs={{0,0},{1,128},{2,32},{3,160},{4,64},{5,192},{6,96},{7,224},{8,8},{... | collective-permute-start | bytes 196616 | tf_op jit(solution)/shard_map/ppermute | solution.py:355
  89.4 6.2 %collective-permute-done.8.attn_ref = bf16[64,512]{1,0:T(8,128)(2,1)S(1)} collective-permute-done((bf16[64,512]{1,0:T(8,128)(2,1)S(1)}, bf16[64,512]{1,0:T(8,128)(2,1)S(1)}, u32[]{:S(2)}, u32[]{:S(2)}) %collective-permute-start.8) | collective-permute-done | bytes 65568 | tf_op jit(solution)/shard_map/ppermute | solution.py:355
  95.7 1.0 copy-done.4
  96.7 2.8 %all-to-all-done.3 = bf16[16,64,512]{2,1,0:T(8,128)(2,1)} async-done(((bf16[16,64,512]{2,1,0:T(8,128)(2,1)}), bf16[16,64,512]{2,1,0:T(8,128)(2,1)}, u32[]{:S(2)}, u32[]{:S(2)}) %all-to-all-start.3) | async-done | bytes 1048608 | tf_op jit(solution)/shard_map/all_to_all | solution.py:266
  99.5 4.3 %all-to-all-start.2 = ((bf16[16,64,512]{2,1,0:T(8,128)(2,1)}), bf16[16,64,512]{2,1,0:T(8,128)(2,1)}, u32[]{:S(2)}, u32[]{:S(2)}) async-start(bf16[16,64,512]{2,1,0:T(8,128)(2,1)} %copy-done.4), calls=%async_computation.2 | async-start | bytes 2097152 | tf_op jit(solution)/shard_map/all_to_all | solution.py:266
  103.9 2.7 %shard_map.134 = (bf16[256,2048]{1,0:T(8,128)(2,1)S(1)}, bf16[256,896]{1,0:T(8,128)(2,1)S(1)}) custom-call(bf16[4,4,64,512]{3,2,1,0:T(8,128)(2,1)} %bitcast.17.rows_ref, bf16[1,2048]{1,0:T(2,128)(2,1)S(1)} %reshape.116.gain_ref, bf16[832,2048]{1,0:T(8,128)(2,1)S(1)} %bitcast.33), custom_call_target="tpu_custom_call" | custom-call | flops 1 | bytes 1 | tf_op jit(solution)/shard_map/pallas_call | solution.py:63
  106.6 1.6 shard_map.135
  108.2 1.8 collective-permute-done.11.got_ref
  110.8 0.9 collective-permute-start.16
  111.7 4.3 %collective-permute-start.17 = (bf16[32,1792]{1,0:T(8,128)(2,1)}, bf16[32,1792]{1,0:T(8,128)(2,1)}, u32[]{:S(2)}, u32[]{:S(2)}) collective-permute-start(bf16[32,1792]{1,0:T(8,128)(2,1)} %get-tuple-element.82), channel_id=1, source_target_pairs={{0,4},{2,6},{4,0},{6,2},{1,5},{3,7},{5,1},{7,3},{8,12},{10,14},{12... | collective-permute-start | bytes 344072 | tf_op jit(solution)/shard_map/ppermute | solution.py:151
  116.0 6.0 %all-to-all-done.2 = bf16[16,64,512]{2,1,0:T(8,128)(2,1)} async-done(((bf16[16,64,512]{2,1,0:T(8,128)(2,1)}), bf16[16,64,512]{2,1,0:T(8,128)(2,1)}, u32[]{:S(2)}, u32[]{:S(2)}) %all-to-all-start.2) | async-done | bytes 1048608 | tf_op jit(solution)/shard_map/all_to_all | solution.py:266
  122.0 2.7 %shard_map.137 = (bf16[256,2048]{1,0:T(8,128)(2,1)S(1)}, bf16[256,896]{1,0:T(8,128)(2,1)S(1)}) custom-call(bf16[4,4,64,512]{3,2,1,0:T(8,128)(2,1)} %bitcast.12.rows_ref, bf16[1,2048]{1,0:T(2,128)(2,1)S(1)} %reshape.116.gain_ref, bf16[832,2048]{1,0:T(8,128)(2,1)S(1)} %bitcast.34, f32[8,128]{1,0:T(8,128)S(1)} %get-tuple-element.71.refs_0_), custom_call_target="tpu_custom_call" | custom-call | flops 1 | bytes 1 | tf_op jit(solution)/shard_map/pallas_call | solution.py:63
  124.7 1.3 shard_map.138
  126.2 1.4 shard_map.140.own_ref
  127.6 2.2 %collective-permute-start.21 = (bf16[32,832]{1,0:T(8,128)(2,1)S(1)}, bf16[32,832]{1,0:T(8,128)(2,1)S(1)}, u32[]{:S(2)}, u32[]{:S(2)}) collective-permute-start(bf16[32,832]{1,0:T(8,128)(2,1)S(1)} %shard_map.140.own_ref), channel_id=1, source_target_pairs={{0,6},{2,4},{4,2},{6,0},{1,7},{3,5},{5,3},{7,1},{8,14},{10,12},{12... | collective-permute-start | bytes 159752 | tf_op jit(solution)/shard_map/ppermute | solution.py:151
  130.5 0.8 collective-permute-start.19
  132.1 2.4 %collective-permute-done.21.three_ref = bf16[32,832]{1,0:T(8,128)(2,1)S(1)} collective-permute-done((bf16[32,832]{1,0:T(8,128)(2,1)S(1)}, bf16[32,832]{1,0:T(8,128)(2,1)S(1)}, u32[]{:S(2)}, u32[]{:S(2)}) %collective-permute-start.21) | collective-permute-done | bytes 53280 | tf_op jit(solution)/shard_map/ppermute | solution.py:151
  136.1 1.5 collective-permute-start.13
  137.6 1.3 collective-permute-start.14
  138.8 0.8 collective-permute-start.15
  139.7 1.3 shard_map.142
  141.0 1.0 copy-done.7
  141.9 6.3 %all-to-all-start.5 = ((bf16[16,16,2048]{2,1,0:T(8,128)(2,1)}), bf16[16,16,2048]{2,1,0:T(8,128)(2,1)}, u32[]{:S(2)}, u32[]{:S(2)}) async-start(bf16[16,16,2048]{2,1,0:T(8,128)(2,1)} %bitcast.38), calls=%async_computation.5 | async-start | bytes 2097152 | tf_op jit(solution)/shard_map/all_to_all | solution.py:266
  148.2 2.4 %collective-permute-done.15.three_ref = bf16[32,1792]{1,0:T(8,128)(2,1)} collective-permute-done((bf16[32,1792]{1,0:T(8,128)(2,1)}, bf16[32,1792]{1,0:T(8,128)(2,1)}, u32[]{:S(2)}, u32[]{:S(2)}) %collective-permute-start.15) | collective-permute-done | bytes 114720 | tf_op jit(solution)/shard_map/ppermute | solution.py:151
  150.6 1.2 shard_map.143.own_ref
  151.8 1.5 collective-permute-start.25
  153.2 1.0 collective-permute-start.24
  154.3 1.1 collective-permute-start.23
  155.4 2.2 %collective-permute-done.25.three_ref = bf16[32,832]{1,0:T(8,128)(2,1)S(1)} collective-permute-done((bf16[32,832]{1,0:T(8,128)(2,1)S(1)}, bf16[32,832]{1,0:T(8,128)(2,1)S(1)}, u32[]{:S(2)}, u32[]{:S(2)}) %collective-permute-start.25) | collective-permute-done | bytes 53280 | tf_op jit(solution)/shard_map/ppermute | solution.py:151
  157.6 0.8 collective-permute-done.24.two_ref
  158.8 1.5 collective-permute-done.26.other_ref
  160.3 1.7 shard_map.145
  162.0 1.0 copy-done.8
  163.0 3.0 %all-to-all-done.5.parts_ref = bf16[16,16,2048]{2,1,0:T(8,128)(2,1)} async-done(((bf16[16,16,2048]{2,1,0:T(8,128)(2,1)}), bf16[16,16,2048]{2,1,0:T(8,128)(2,1)}, u32[]{:S(2)}, u32[]{:S(2)}) %all-to-all-start.5) | async-done | bytes 1048608 | tf_op jit(solution)/shard_map/all_to_all | solution.py:266
  165.9 4.2 %all-to-all-start.4 = ((bf16[16,16,2048]{2,1,0:T(8,128)(2,1)}), bf16[16,16,2048]{2,1,0:T(8,128)(2,1)S(1)}, u32[]{:S(2)}, u32[]{:S(2)}) async-start(bf16[16,16,2048]{2,1,0:T(8,128)(2,1)} %bitcast.39), calls=%async_computation.4 | async-start | bytes 2097152 | tf_op jit(solution)/shard_map/all_to_all | solution.py:266
  170.1 1.4 shard_map.147
  171.5 9.3 %collective-permute-start.27 = (bf16[16,2048]{1,0:T(8,128)(2,1)S(1)}, bf16[16,2048]{1,0:T(8,128)(2,1)S(1)}, u32[]{:S(2)}, u32[]{:S(2)}) collective-permute-start(bf16[16,2048]{1,0:T(8,128)(2,1)S(1)} %shard_map.147), channel_id=1, source_target_pairs={{0,128},{128,0},{1,129},{129,1},{2,130},{130,2},{3,131},{131,3},{4... | collective-permute-start | bytes 196616 | tf_op jit(solution)/shard_map/ppermute | solution.py:45
  180.8 0.9 convert_bitcast_fusion
  181.7 6.2 %all-to-all-done.4.parts_ref = bf16[16,16,2048]{2,1,0:T(8,128)(2,1)S(1)} async-done(((bf16[16,16,2048]{2,1,0:T(8,128)(2,1)}), bf16[16,16,2048]{2,1,0:T(8,128)(2,1)S(1)}, u32[]{:S(2)}, u32[]{:S(2)}) %all-to-all-start.4) | async-done | bytes 1048608 | tf_op jit(solution)/shard_map/all_to_all | solution.py:266
  (73 shorter events, 9.4 us)
Async XLA Ops:
  0.0 57.7 %copy-start.6 = (bf16[1024,512]{1,0:T(8,128)(2,1)S(1)}, bf16[1024,512]{1,0:T(8,128)(2,1)}, u32[]{:S(2)}) copy-start(bf16[1024,512]{1,0:T(8,128)(2,1)} %weight_ref.3) | copy-start | bytes 3145732
  2.8 26.0 %all-to-all-start = ((bf16[32,2,1280]{2,1,0:T(2,128)(2,1)}), bf16[32,2,1280]{2,1,0:T(2,128)(2,1)S(1)}, u32[]{:S(2)}, u32[]{:S(2)}) async-start(bf16[32,2,1280]{2,1,0:T(2,128)(2,1)} %reshape.107), calls=%async_computation | async-start | bytes 327680 | tf_op jit(solution)/shard_map/all_to_all | solution.py:307
  15.8 0.8 copy-start.11
  16.7 12.2 %collective-permute-start = (bf16[16,512]{1,0:T(8,128)(2,1)S(1)}, bf16[16,512]{1,0:T(8,128)(2,1)S(1)}, u32[]{:S(2)}, u32[]{:S(2)}) collective-permute-start(bf16[16,512]{1,0:T(8,128)(2,1)S(1)} %get-tuple-element.50), channel_id=1, source_target_pairs={{0,8},{8,0},{16,24},{24,16},{1,9},{9,1},{17,25},{25,17},{2,10},{10... | collective-permute-start | bytes 49160 | tf_op jit(solution)/shard_map/ppermute | solution.py:329
  18.5 10.4 %collective-permute-start.1 = (bf16[16,512]{1,0:T(8,128)(2,1)S(1)}, bf16[16,512]{1,0:T(8,128)(2,1)S(1)}, u32[]{:S(2)}, u32[]{:S(2)}) collective-permute-start(bf16[16,512]{1,0:T(8,128)(2,1)S(1)} %get-tuple-element.51), channel_id=1, source_target_pairs={{0,16},{8,24},{16,0},{24,8},{1,17},{9,25},{17,1},{25,9},{2,18},{10... | collective-permute-start | bytes 49160 | tf_op jit(solution)/shard_map/ppermute | solution.py:329
  21.1 7.7 %collective-permute-start.2 = (bf16[16,512]{1,0:T(8,128)(2,1)S(1)}, bf16[16,512]{1,0:T(8,128)(2,1)S(1)}, u32[]{:S(2)}, u32[]{:S(2)}) collective-permute-start(bf16[16,512]{1,0:T(8,128)(2,1)S(1)} %get-tuple-element.52), channel_id=1, source_target_pairs={{0,24},{8,16},{16,8},{24,0},{1,25},{9,17},{17,9},{25,1},{2,26},{10... | collective-permute-start | bytes 49160 | tf_op jit(solution)/shard_map/ppermute | solution.py:329
  28.9 0.9 copy-start.9
  29.8 0.9 copy-start.10
  31.6 7.9 %collective-permute-start.3 = (bf16[16,1024]{1,0:T(8,128)(2,1)S(1)}, bf16[16,1024]{1,0:T(8,128)(2,1)S(1)}, u32[]{:S(2)}, u32[]{:S(2)}) collective-permute-start(bf16[16,1024]{1,0:T(8,128)(2,1)S(1)} %get-tuple-element.53.near_ref), channel_id=1, source_target_pairs={{0,128},{128,0},{1,129},{129,1},{2,130},{130,2},{3,131},{131,3},{4... | collective-permute-start | bytes 98312 | tf_op jit(solution)/shard_map/ppermute | solution.py:45
  58.8 1.6 collective-permute-start.4
  61.0 7.8 %collective-permute-start.5 = (bf16[64,512]{1,0:T(8,128)(2,1)S(1)}, bf16[64,512]{1,0:T(8,128)(2,1)S(1)}, u32[]{:S(2)}, u32[]{:S(2)}) collective-permute-start(bf16[64,512]{1,0:T(8,128)(2,1)S(1)} %get-tuple-element.63), channel_id=1, source_target_pairs={{0,2},{2,0},{4,6},{6,4},{1,3},{3,1},{5,7},{7,5},{8,10},{10,8},{12,... | collective-permute-start | bytes 196616 | tf_op jit(solution)/shard_map/ppermute | solution.py:151
  61.9 7.0 %collective-permute-start.6 = (bf16[64,512]{1,0:T(8,128)(2,1)S(1)}, bf16[64,512]{1,0:T(8,128)(2,1)S(1)}, u32[]{:S(2)}, u32[]{:S(2)}) collective-permute-start(bf16[64,512]{1,0:T(8,128)(2,1)S(1)} %get-tuple-element.64), channel_id=1, source_target_pairs={{0,4},{2,6},{4,0},{6,2},{1,5},{3,7},{5,1},{7,3},{8,12},{10,14},{12... | collective-permute-start | bytes 196616 | tf_op jit(solution)/shard_map/ppermute | solution.py:151
  63.5 8.1 %collective-permute-start.7 = (bf16[64,512]{1,0:T(8,128)(2,1)S(1)}, bf16[64,512]{1,0:T(8,128)(2,1)S(1)}, u32[]{:S(2)}, u32[]{:S(2)}) collective-permute-start(bf16[64,512]{1,0:T(8,128)(2,1)S(1)} %get-tuple-element.65), channel_id=1, source_target_pairs={{0,6},{2,4},{4,2},{6,0},{1,7},{3,5},{5,3},{7,1},{8,14},{10,12},{12... | collective-permute-start | bytes 196616 | tf_op jit(solution)/shard_map/ppermute | solution.py:151
  64.5 11.1 %collective-permute-start.10 = (bf16[32,1024]{1,0:T(8,128)(2,1)S(1)}, bf16[32,1024]{1,0:T(8,128)(2,1)S(1)}, u32[]{:S(2)}, u32[]{:S(2)}) collective-permute-start(bf16[32,1024]{1,0:T(8,128)(2,1)S(1)} %get-tuple-element.66.tok_ref), channel_id=1, source_target_pairs={{0,128},{128,0},{1,129},{129,1},{2,130},{130,2},{3,131},{131,3},{4... | collective-permute-start | bytes 196616 | tf_op jit(solution)/shard_map/ppermute | solution.py:45
  71.6 32.3 %copy-start.12 = (bf16[2048]{0:T(1024)(128)(2,1)S(1)}, bf16[2048]{0:T(1024)(128)(2,1)}, u32[]{:S(2)}) copy-start(bf16[2048]{0:T(1024)(128)(2,1)} %param.22) | copy-start | bytes 12292
  71.6 32.3 %copy-start = (bf16[2048,832]{0,1:T(8,128)(2,1)S(1)}, bf16[2048,832]{0,1:T(8,128)(2,1)}, u32[]{:S(2)}) copy-start(bf16[2048,832]{0,1:T(8,128)(2,1)} %param.23) | copy-start | bytes 10223620
  71.6 7.7 %collective-permute-start.9 = (bf16[64,512]{1,0:T(8,128)(2,1)S(1)}, bf16[64,512]{1,0:T(8,128)(2,1)S(1)}, u32[]{:S(2)}, u32[]{:S(2)}) collective-permute-start(bf16[64,512]{1,0:T(8,128)(2,1)S(1)} %add_convert_fusion.1), channel_id=1, source_target_pairs={{0,128},{1,0},{2,160},{3,32},{4,192},{5,64},{6,224},{7,96},{8,136}... | collective-permute-start | bytes 196616 | tf_op jit(solution)/shard_map/ppermute | solution.py:354
  79.4 1.0 copy-start.5
  80.4 19.1 %all-to-all-start.3 = ((bf16[16,64,512]{2,1,0:T(8,128)(2,1)}), bf16[16,64,512]{2,1,0:T(8,128)(2,1)}, u32[]{:S(2)}, u32[]{:S(2)}) async-start(bf16[16,64,512]{2,1,0:T(8,128)(2,1)} %copy-done.5), calls=%async_computation.3 | async-start | bytes 2097152 | tf_op jit(solution)/shard_map/all_to_all | solution.py:266
  84.8 10.8 %collective-permute-start.8 = (bf16[64,512]{1,0:T(8,128)(2,1)S(1)}, bf16[64,512]{1,0:T(8,128)(2,1)S(1)}, u32[]{:S(2)}, u32[]{:S(2)}) collective-permute-start(bf16[64,512]{1,0:T(8,128)(2,1)S(1)} %add_convert_fusion.1), channel_id=1, source_target_pairs={{0,0},{1,128},{2,32},{3,160},{4,64},{5,192},{6,96},{7,224},{8,8},{... | collective-permute-start | bytes 196616 | tf_op jit(solution)/shard_map/ppermute | solution.py:355
  95.7 1.0 copy-start.4
  99.5 22.5 %all-to-all-start.2 = ((bf16[16,64,512]{2,1,0:T(8,128)(2,1)}), bf16[16,64,512]{2,1,0:T(8,128)(2,1)}, u32[]{:S(2)}, u32[]{:S(2)}) async-start(bf16[16,64,512]{2,1,0:T(8,128)(2,1)} %copy-done.4), calls=%async_computation.2 | async-start | bytes 2097152 | tf_op jit(solution)/shard_map/all_to_all | solution.py:266
  103.9 2.7 %copy-start.1 = (bf16[2048,832]{0,1:T(8,128)(2,1)S(1)}, bf16[2048,832]{0,1:T(8,128)(2,1)}, u32[]{:S(2)}) copy-start(bf16[2048,832]{0,1:T(8,128)(2,1)} %param.24) | copy-start | bytes 10223620
  108.2 1.8 collective-permute-start.11
  110.8 15.4 %collective-permute-start.16 = (bf16[32,1792]{1,0:T(8,128)(2,1)}, bf16[32,1792]{1,0:T(8,128)(2,1)}, u32[]{:S(2)}, u32[]{:S(2)}) collective-permute-start(bf16[32,1792]{1,0:T(8,128)(2,1)} %get-tuple-element.81), channel_id=1, source_target_pairs={{0,2},{2,0},{4,6},{6,4},{1,3},{3,1},{5,7},{7,5},{8,10},{10,8},{12,... | collective-permute-start | bytes 344072 | tf_op jit(solution)/shard_map/ppermute | solution.py:151
  111.7 14.4 %collective-permute-start.17 = (bf16[32,1792]{1,0:T(8,128)(2,1)}, bf16[32,1792]{1,0:T(8,128)(2,1)}, u32[]{:S(2)}, u32[]{:S(2)}) collective-permute-start(bf16[32,1792]{1,0:T(8,128)(2,1)} %get-tuple-element.82), channel_id=1, source_target_pairs={{0,4},{2,6},{4,0},{6,2},{1,5},{3,7},{5,1},{7,3},{8,12},{10,14},{12... | collective-permute-start | bytes 344072 | tf_op jit(solution)/shard_map/ppermute | solution.py:151
  116.0 10.2 %collective-permute-start.18 = (bf16[32,1792]{1,0:T(8,128)(2,1)}, bf16[32,1792]{1,0:T(8,128)(2,1)}, u32[]{:S(2)}, u32[]{:S(2)}) collective-permute-start(bf16[32,1792]{1,0:T(8,128)(2,1)} %get-tuple-element.83), channel_id=1, source_target_pairs={{0,6},{2,4},{4,2},{6,0},{1,7},{3,5},{5,3},{7,1},{8,14},{10,12},{12... | collective-permute-start | bytes 344072 | tf_op jit(solution)/shard_map/ppermute | solution.py:151
  122.0 2.7 %copy-start.2 = (bf16[2048,832]{0,1:T(8,128)(2,1)S(1)}, bf16[2048,832]{0,1:T(8,128)(2,1)}, u32[]{:S(2)}) copy-start(bf16[2048,832]{0,1:T(8,128)(2,1)} %param.24) | copy-start | bytes 10223620
  126.1 5.3 %collective-permute-start.12 = (bf16[128,1792]{1,0:T(8,128)(2,1)S(1)}, bf16[128,1792]{1,0:T(8,128)(2,1)S(1)}, u32[]{:S(2)}, u32[]{:S(2)}) collective-permute-start(bf16[128,1792]{1,0:T(8,128)(2,1)S(1)} %get-tuple-element.75), channel_id=1, source_target_pairs={{0,1},{1,0},{2,3},{3,2},{4,5},{5,4},{6,7},{7,6},{8,9},{9,8},{10,11... | collective-permute-start | bytes 1376264 | tf_op jit(solution)/shard_map/ppermute | solution.py:45
  126.2 13.5 %copy-start.3 = (bf16[832,2048]{1,0:T(8,128)(2,1)S(1)}, bf16[832,2048]{1,0:T(8,128)(2,1)}, u32[]{:S(2)}) copy-start(bf16[832,2048]{1,0:T(8,128)(2,1)} %weight_ref.5) | copy-start | bytes 10223620
  127.6 7.0 %collective-permute-start.21 = (bf16[32,832]{1,0:T(8,128)(2,1)S(1)}, bf16[32,832]{1,0:T(8,128)(2,1)S(1)}, u32[]{:S(2)}, u32[]{:S(2)}) collective-permute-start(bf16[32,832]{1,0:T(8,128)(2,1)S(1)} %shard_map.140.own_ref), channel_id=1, source_target_pairs={{0,6},{2,4},{4,2},{6,0},{1,7},{3,5},{5,3},{7,1},{8,14},{10,12},{12... | collective-permute-start | bytes 159752 | tf_op jit(solution)/shard_map/ppermute | solution.py:151
  129.8 5.4 %collective-permute-start.20 = (bf16[32,832]{1,0:T(8,128)(2,1)S(1)}, bf16[32,832]{1,0:T(8,128)(2,1)S(1)}, u32[]{:S(2)}, u32[]{:S(2)}) collective-permute-start(bf16[32,832]{1,0:T(8,128)(2,1)S(1)} %shard_map.140.own_ref), channel_id=1, source_target_pairs={{0,4},{2,6},{4,0},{6,2},{1,5},{3,7},{5,1},{7,3},{8,12},{10,14},{12... | collective-permute-start | bytes 159752 | tf_op jit(solution)/shard_map/ppermute | solution.py:151
  130.5 5.4 %collective-permute-start.19 = (bf16[32,832]{1,0:T(8,128)(2,1)S(1)}, bf16[32,832]{1,0:T(8,128)(2,1)S(1)}, u32[]{:S(2)}, u32[]{:S(2)}) collective-permute-start(bf16[32,832]{1,0:T(8,128)(2,1)S(1)} %shard_map.140.own_ref), channel_id=1, source_target_pairs={{0,2},{2,0},{4,6},{6,4},{1,3},{3,1},{5,7},{7,5},{8,10},{10,8},{12,... | collective-permute-start | bytes 159752 | tf_op jit(solution)/shard_map/ppermute | solution.py:151
  136.0 3.7 %collective-permute-start.22 = (bf16[128,832]{1,0:T(8,128)(2,1)S(1)}, bf16[128,832]{1,0:T(8,128)(2,1)S(1)}, u32[]{:S(2)}, u32[]{:S(2)}) collective-permute-start(bf16[128,832]{1,0:T(8,128)(2,1)S(1)} %shard_map.141.own_ref), channel_id=1, source_target_pairs={{0,1},{1,0},{2,3},{3,2},{4,5},{5,4},{6,7},{7,6},{8,9},{9,8},{10,11... | collective-permute-start | bytes 638984 | tf_op jit(solution)/shard_map/ppermute | solution.py:45
  136.1 12.1 %collective-permute-start.13 = (bf16[32,1792]{1,0:T(8,128)(2,1)}, bf16[32,1792]{1,0:T(8,128)(2,1)}, u32[]{:S(2)}, u32[]{:S(2)}) collective-permute-start(bf16[32,1792]{1,0:T(8,128)(2,1)} %get-tuple-element.77), channel_id=1, source_target_pairs={{0,2},{2,0},{4,6},{6,4},{1,3},{3,1},{5,7},{7,5},{8,10},{10,8},{12,... | collective-permute-start | bytes 344072 | tf_op jit(solution)/shard_map/ppermute | solution.py:151
  137.6 10.6 %collective-permute-start.14 = (bf16[32,1792]{1,0:T(8,128)(2,1)}, bf16[32,1792]{1,0:T(8,128)(2,1)}, u32[]{:S(2)}, u32[]{:S(2)}) collective-permute-start(bf16[32,1792]{1,0:T(8,128)(2,1)} %get-tuple-element.78), channel_id=1, source_target_pairs={{0,4},{2,6},{4,0},{6,2},{1,5},{3,7},{5,1},{7,3},{8,12},{10,14},{12... | collective-permute-start | bytes 344072 | tf_op jit(solution)/shard_map/ppermute | solution.py:151
  138.8 11.7 %collective-permute-start.15 = (bf16[32,1792]{1,0:T(8,128)(2,1)}, bf16[32,1792]{1,0:T(8,128)(2,1)}, u32[]{:S(2)}, u32[]{:S(2)}) collective-permute-start(bf16[32,1792]{1,0:T(8,128)(2,1)} %get-tuple-element.79), channel_id=1, source_target_pairs={{0,6},{2,4},{4,2},{6,0},{1,7},{3,5},{5,3},{7,1},{8,14},{10,12},{12... | collective-permute-start | bytes 344072 | tf_op jit(solution)/shard_map/ppermute | solution.py:151
  141.0 1.0 copy-start.7
  141.9 24.0 %all-to-all-start.5 = ((bf16[16,16,2048]{2,1,0:T(8,128)(2,1)}), bf16[16,16,2048]{2,1,0:T(8,128)(2,1)}, u32[]{:S(2)}, u32[]{:S(2)}) async-start(bf16[16,16,2048]{2,1,0:T(8,128)(2,1)} %bitcast.38), calls=%async_computation.5 | async-start | bytes 2097152 | tf_op jit(solution)/shard_map/all_to_all | solution.py:266
  151.8 5.8 %collective-permute-start.25 = (bf16[32,832]{1,0:T(8,128)(2,1)S(1)}, bf16[32,832]{1,0:T(8,128)(2,1)S(1)}, u32[]{:S(2)}, u32[]{:S(2)}) collective-permute-start(bf16[32,832]{1,0:T(8,128)(2,1)S(1)} %shard_map.143.own_ref), channel_id=1, source_target_pairs={{0,6},{2,4},{4,2},{6,0},{1,7},{3,5},{5,3},{7,1},{8,14},{10,12},{12... | collective-permute-start | bytes 159752 | tf_op jit(solution)/shard_map/ppermute | solution.py:151
  153.2 5.2 %collective-permute-start.24 = (bf16[32,832]{1,0:T(8,128)(2,1)S(1)}, bf16[32,832]{1,0:T(8,128)(2,1)S(1)}, u32[]{:S(2)}, u32[]{:S(2)}) collective-permute-start(bf16[32,832]{1,0:T(8,128)(2,1)S(1)} %shard_map.143.own_ref), channel_id=1, source_target_pairs={{0,4},{2,6},{4,0},{6,2},{1,5},{3,7},{5,1},{7,3},{8,12},{10,14},{12... | collective-permute-start | bytes 159752 | tf_op jit(solution)/shard_map/ppermute | solution.py:151
  154.3 4.2 %collective-permute-start.23 = (bf16[32,832]{1,0:T(8,128)(2,1)S(1)}, bf16[32,832]{1,0:T(8,128)(2,1)S(1)}, u32[]{:S(2)}, u32[]{:S(2)}) collective-permute-start(bf16[32,832]{1,0:T(8,128)(2,1)S(1)} %shard_map.143.own_ref), channel_id=1, source_target_pairs={{0,2},{2,0},{4,6},{6,4},{1,3},{3,1},{5,7},{7,5},{8,10},{10,8},{12,... | collective-permute-start | bytes 159752 | tf_op jit(solution)/shard_map/ppermute | solution.py:151
  158.5 1.8 collective-permute-start.26
  162.0 1.0 copy-start.8
  165.9 22.0 %all-to-all-start.4 = ((bf16[16,16,2048]{2,1,0:T(8,128)(2,1)}), bf16[16,16,2048]{2,1,0:T(8,128)(2,1)S(1)}, u32[]{:S(2)}, u32[]{:S(2)}) async-start(bf16[16,16,2048]{2,1,0:T(8,128)(2,1)} %bitcast.39), calls=%async_computation.4 | async-start | bytes 2097152 | tf_op jit(solution)/shard_map/all_to_all | solution.py:266
  171.5 16.6 %collective-permute-start.27 = (bf16[16,2048]{1,0:T(8,128)(2,1)S(1)}, bf16[16,2048]{1,0:T(8,128)(2,1)S(1)}, u32[]{:S(2)}, u32[]{:S(2)}) collective-permute-start(bf16[16,2048]{1,0:T(8,128)(2,1)S(1)} %shard_map.147), channel_id=1, source_target_pairs={{0,128},{128,0},{1,129},{129,1},{2,130},{130,2},{3,131},{131,3},{4... | collective-permute-start | bytes 196616 | tf_op jit(solution)/shard_map/ppermute | solution.py:45

commit v6 on v5

--- a/solution.py
+++ b/solution.py
@@ -83,6 +83,12 @@
     return lax.dot_general(a, b, (((1,), (1,)), ((), ())), preferred_element_type=F32)
 
 
+def as_column(row_ref):
+    sizes = (row_ref.shape[1],) * 2
+    same = lax.broadcasted_iota(jnp.int32, sizes, 0) == lax.broadcasted_iota(jnp.int32, sizes, 1)
+    return jnp.sum(jnp.where(same, row_ref[...], 0), axis=1, keepdims=True)
+
+
 def attend_body(
     rows, cache_len, heads, place_x, slot_ref, got_ref, len_ref, own_tok, one_tok, two_tok, three_tok,
     key_ref, value_ref, out_ref, tok_ref,
@@ -93,7 +99,7 @@
         at = pl.ds(pl.multiple_of((group & 1) * rows, rows), rows)
         tok_ref[at, pl.ds(pl.multiple_of((group >> 1) * cols, cols), cols)] = piece[...]
     slots = lax.broadcasted_iota(jnp.int32, (rows, got_ref.shape[0]), 1)
-    compact = (slot_ref[...] == slots).astype(F32).astype(BF)
+    compact = (as_column(slot_ref) == slots).astype(F32).astype(BF)
     arrived = dot(compact, got_ref[...])
     q_cols = heads * HD
     rounded = arrived[:, :q_cols].astype(BF)
@@ -106,7 +112,7 @@
     spot = lax.broadcasted_iota(jnp.int32, scores.shape, 1)
     row = lax.rem(lax.broadcasted_iota(jnp.int32, scores.shape, 0), rows)
     start = row * cache_len
-    lens = jnp.concatenate([len_ref[...]] * heads, axis=0)
+    lens = jnp.concatenate([as_column(len_ref)] * heads, axis=0)
     live = (spot >= start) & (spot < start + lens)
     masked = jnp.where(live, scores, -1e30)
     top = jnp.maximum(jnp.max(masked, axis=1, keepdims=True), own)
@@ -317,8 +323,8 @@
     wanted = own_group * rows_dev + jnp.arange(rows_dev, dtype=jnp.int32)
     position = flat_groups * rows_dev + ahead
     arrival = jnp.sum(
-        jnp.where(position[None, :] == wanted[:, None], slot_of[None, :], 0), axis=1, keepdims=True, dtype=jnp.int32
-    )
+        jnp.where(position[None, :] == wanted[:, None], slot_of[None, :], 0), axis=1, dtype=jnp.int32
+    )[None, :]
     plane = groups // 2
     gathered_at = ((flat_groups % plane) * 2 + (flat_groups // plane ^ place_z)) * rows_dev + ahead
     halves = gathered_at.reshape(2, rows // 2, 1)
@@ -335,7 +341,7 @@
         [shape((rows_dev, q_cols), BF), shape((2 * rows_dev, q_cols), BF)],
         arrival,
         received.reshape(groups * capacity, packed.shape[1]),
-        lengths.reshape(rows_dev, 1),
+        lengths.reshape(1, rows_dev),
         *pieces,
         *caches,
         scalars=(place_x,),

time: 193 us -> 191 us (0.990); the launches traced: 189 us -> 190 us
  waiting for transfers between devices: 54.4 us -> 60.1 us
  starting transfers between devices: 82.1 us -> 77.4 us
    ppermute x8, starting transfers between devices: 16.9 us -> 12.9 us  [swap(): return lax.ppermute(v, axis, [(0, 1), (1, 0)])]
    all_to_all x4, waiting for transfers between devices: 18 us -> 21.9 us  [all_to_all(): return lax.all_to_all(v, axes, split_axis=0, concat_axis=0, tiled=True)]
    ppermute x1, starting transfers between devices: 4 us -> 1.92 us  [shards(): far = lax.ppermute(attn_out, AXES, spread_pairs(1))]
    unnamed x26 -> x28, local copies, waits for them, and re-layouts: 6.59 us -> 7.27 us
  transfers between devices with their start and end apart: 33 -> 33, of which waited for: 18 -> 22; matrix products, arithmetic and copies ran while one was open for 2% -> 2% of each run, Pallas kernels for 9% -> 9%
where the time goes in v6:
time: 191 us; the launch traced here: 190 us
  starting transfers between devices  77.4 us (41%)
  waiting for transfers between devices  60.1 us (31%)
  Pallas kernels  19.7 us (10%)
  blocking collectives  17.8 us (9%)
  local copies, waits for them, and re-layouts  9.23 us (5%)
  other arithmetic  3.86 us (2%)
    all_to_all x4, waiting for transfers between devices, all_to_all(): return lax.all_to_all(v, axes, split_axis=0, concat_axis=0, tiled=True)  21.9 us
    ppermute x15, starting transfers between devices, line_send(): lax.ppermute(piece, 'z_lo', [(i, i ^ step) for i in range(4)])  20.4 us
    pallas_call x21, Pallas kernels, call(): pl.pallas_call(body, out_shape=out_shape, in_specs=specs, out_specs=whole...  19.7 us
    all_to_all x4, starting transfers between devices, all_to_all(): return lax.all_to_all(v, axes, split_axis=0, concat_axis=0, tiled=True)  19.3 us
    all_to_all x1, blocking collectives, exchange(): got = lax.all_to_all(copies, YX, split_axis=0, concat_axis=0, tiled=True)  17.8 us
    ppermute x15, waiting for transfers between devices, line_send(): lax.ppermute(piece, 'z_lo', [(i, i ^ step) for i in range(4)])  13.1 us
    all_to_all x1, starting transfers between devices, shards(): lax.all_to_all(bucket, GRP, split_axis=0, concat_axis=0, tiled=True)  13 us
    ppermute x8, starting transfers between devices, swap(): return lax.ppermute(v, axis, [(0, 1), (1, 0)])  12.9 us
  transfers between devices with their start and end apart: 33, of which 22 were waited for; matrix products, arithmetic and copies ran while one was open for 2% of the time, Pallas kernels for 9%

profile of v6, /device:TPU:32, one launch (start us, length us, event | category | flops | bytes accessed | tf_op | source)
XLA Modules:
  0.0 189.5 jit_solution(12920156869376321707)
XLA Ops:
  0.0 0.8 reshape.106
  1.1 1.0 convolution_convert_fusion
  2.8 13.0 %all-to-all-start = ((bf16[32,2,1280]{2,1,0:T(2,128)(2,1)}), bf16[32,2,1280]{2,1,0:T(2,128)(2,1)S(1)}, u32[]{:S(2)}, u32[]{:S(2)}) async-start(bf16[32,2,1280]{2,1,0:T(2,128)(2,1)} %reshape.107), calls=%async_computation | async-start | bytes 327680 | tf_op jit(solution)/shard_map/all_to_all | solution.py:313
  16.7 1.8 collective-permute-start
  18.5 2.7 %collective-permute-start.1 = (bf16[16,512]{1,0:T(8,128)(2,1)S(1)}, bf16[16,512]{1,0:T(8,128)(2,1)S(1)}, u32[]{:S(2)}, u32[]{:S(2)}) collective-permute-start(bf16[16,512]{1,0:T(8,128)(2,1)S(1)} %get-tuple-element.51), channel_id=1, source_target_pairs={{0,16},{8,24},{16,0},{24,8},{1,17},{9,25},{17,1},{25,9},{2,18},{10... | collective-permute-start | bytes 49160 | tf_op jit(solution)/shard_map/ppermute | solution.py:335
  21.4 1.2 convert_reduce_fusion.1
  23.4 5.3 %all-to-all-done = bf16[32,2,1280]{2,1,0:T(2,128)(2,1)S(1)} async-done(((bf16[32,2,1280]{2,1,0:T(2,128)(2,1)}), bf16[32,2,1280]{2,1,0:T(2,128)(2,1)S(1)}, u32[]{:S(2)}, u32[]{:S(2)}) %all-to-all-start) | async-done | bytes 163872 | tf_op jit(solution)/shard_map/all_to_all | solution.py:313
  28.9 0.9 copy-done.9
  29.8 0.9 copy-done.10
  31.4 0.9 shard_map.128
  32.3 2.7 %collective-permute-start.3 = (bf16[16,1024]{1,0:T(8,128)(2,1)S(1)}, bf16[16,1024]{1,0:T(8,128)(2,1)S(1)}, u32[]{:S(2)}, u32[]{:S(2)}) collective-permute-start(bf16[16,1024]{1,0:T(8,128)(2,1)S(1)} %get-tuple-element.53.near_ref), channel_id=1, source_target_pairs={{0,128},{128,0},{1,129},{129,1},{2,130},{130,2},{3,131},{131,3},{4... | collective-permute-start | bytes 98312 | tf_op jit(solution)/shard_map/ppermute | solution.py:45
  35.0 5.2 %collective-permute-done.3.far_ref = bf16[16,1024]{1,0:T(8,128)(2,1)S(1)} collective-permute-done((bf16[16,1024]{1,0:T(8,128)(2,1)S(1)}, bf16[16,1024]{1,0:T(8,128)(2,1)S(1)}, u32[]{:S(2)}, u32[]{:S(2)}) %collective-permute-start.3) | collective-permute-done | bytes 32800 | tf_op jit(solution)/shard_map/ppermute | solution.py:45
  40.3 17.8 %all_to_all.30 = bf16[16,32,1024]{2,1,0:T(8,128)(2,1)S(1)} all-to-all(bf16[16,32,1024]{2,1,0:T(8,128)(2,1)S(1)} %shard_map.129), channel_id=1, replica_groups=mesh['z_hi'=2,'y'=4,'x'=4,'z_lo'=4,'core'=2] {'y','x'}, dimensions={0} | all-to-all | bytes 2097152 | tf_op jit(solution)/shard_map/all_to_all | solution.py:54
  58.4 1.1 shard_map.130
  59.6 1.5 collective-permute-done.4.got_ref
  62.5 1.7 collective-permute-start.6
  64.2 1.0 collective-permute-start.7
  65.2 3.6 %collective-permute-start.10 = (bf16[32,1024]{1,0:T(8,128)(2,1)S(1)}, bf16[32,1024]{1,0:T(8,128)(2,1)S(1)}, u32[]{:S(2)}, u32[]{:S(2)}) collective-permute-start(bf16[32,1024]{1,0:T(8,128)(2,1)S(1)} %get-tuple-element.66.tok_ref), channel_id=1, source_target_pairs={{0,128},{128,0},{1,129},{129,1},{2,130},{130,2},{3,131},{131,3},{4... | collective-permute-start | bytes 196616 | tf_op jit(solution)/shard_map/ppermute | solution.py:45
  69.0 3.2 %collective-permute-done.7 = bf16[64,512]{1,0:T(8,128)(2,1)S(1)} collective-permute-done((bf16[64,512]{1,0:T(8,128)(2,1)S(1)}, bf16[64,512]{1,0:T(8,128)(2,1)S(1)}, u32[]{:S(2)}, u32[]{:S(2)}) %collective-permute-start.7) | collective-permute-done | bytes 65568 | tf_op jit(solution)/shard_map/ppermute | solution.py:157
  72.3 1.9 %collective-permute-start.9 = (bf16[64,512]{1,0:T(8,128)(2,1)S(1)}, bf16[64,512]{1,0:T(8,128)(2,1)S(1)}, u32[]{:S(2)}, u32[]{:S(2)}) collective-permute-start(bf16[64,512]{1,0:T(8,128)(2,1)S(1)} %add_convert_fusion.1), channel_id=1, source_target_pairs={{0,128},{1,0},{2,160},{3,32},{4,192},{5,64},{6,224},{7,96},{8,136}... | collective-permute-start | bytes 196616 | tf_op jit(solution)/shard_map/ppermute | solution.py:360
  74.2 1.5 collective-permute-done.10.tok_ref
  75.7 3.1 %collective-permute-done.9.attn_ref = bf16[64,512]{1,0:T(8,128)(2,1)S(1)} collective-permute-done((bf16[64,512]{1,0:T(8,128)(2,1)S(1)}, bf16[64,512]{1,0:T(8,128)(2,1)S(1)}, u32[]{:S(2)}, u32[]{:S(2)}) %collective-permute-start.9) | collective-permute-done | bytes 65568 | tf_op jit(solution)/shard_map/ppermute | solution.py:360
  79.0 1.0 copy-done.5
  80.0 4.3 %all-to-all-start.3 = ((bf16[16,64,512]{2,1,0:T(8,128)(2,1)}), bf16[16,64,512]{2,1,0:T(8,128)(2,1)}, u32[]{:S(2)}, u32[]{:S(2)}) async-start(bf16[16,64,512]{2,1,0:T(8,128)(2,1)} %copy-done.5), calls=%async_computation.3 | async-start | bytes 2097152 | tf_op jit(solution)/shard_map/all_to_all | solution.py:272
  84.3 5.2 %collective-permute-start.8 = (bf16[64,512]{1,0:T(8,128)(2,1)S(1)}, bf16[64,512]{1,0:T(8,128)(2,1)S(1)}, u32[]{:S(2)}, u32[]{:S(2)}) collective-permute-start(bf16[64,512]{1,0:T(8,128)(2,1)S(1)} %add_convert_fusion.1), channel_id=1, source_target_pairs={{0,0},{1,128},{2,32},{3,160},{4,64},{5,192},{6,96},{7,224},{8,8},{... | collective-permute-start | bytes 196616 | tf_op jit(solution)/shard_map/ppermute | solution.py:361
  89.5 5.0 %collective-permute-done.8.attn_ref = bf16[64,512]{1,0:T(8,128)(2,1)S(1)} collective-permute-done((bf16[64,512]{1,0:T(8,128)(2,1)S(1)}, bf16[64,512]{1,0:T(8,128)(2,1)S(1)}, u32[]{:S(2)}, u32[]{:S(2)}) %collective-permute-start.8) | collective-permute-done | bytes 65568 | tf_op jit(solution)/shard_map/ppermute | solution.py:361
  94.6 1.0 copy-done.4
  95.6 4.3 %all-to-all-done.3 = bf16[16,64,512]{2,1,0:T(8,128)(2,1)} async-done(((bf16[16,64,512]{2,1,0:T(8,128)(2,1)}), bf16[16,64,512]{2,1,0:T(8,128)(2,1)}, u32[]{:S(2)}, u32[]{:S(2)}) %all-to-all-start.3) | async-done | bytes 1048608 | tf_op jit(solution)/shard_map/all_to_all | solution.py:272
  99.8 4.3 %all-to-all-start.2 = ((bf16[16,64,512]{2,1,0:T(8,128)(2,1)}), bf16[16,64,512]{2,1,0:T(8,128)(2,1)}, u32[]{:S(2)}, u32[]{:S(2)}) async-start(bf16[16,64,512]{2,1,0:T(8,128)(2,1)} %copy-done.4), calls=%async_computation.2 | async-start | bytes 2097152 | tf_op jit(solution)/shard_map/all_to_all | solution.py:272
  104.2 2.7 %shard_map.134 = (bf16[256,2048]{1,0:T(8,128)(2,1)S(1)}, bf16[256,896]{1,0:T(8,128)(2,1)S(1)}) custom-call(bf16[4,4,64,512]{3,2,1,0:T(8,128)(2,1)} %bitcast.17.rows_ref, bf16[1,2048]{1,0:T(2,128)(2,1)S(1)} %reshape.116.gain_ref, bf16[832,2048]{1,0:T(8,128)(2,1)S(1)} %bitcast.33), custom_call_target="tpu_custom_call" | custom-call | flops 1 | bytes 1 | tf_op jit(solution)/shard_map/pallas_call | solution.py:63
  106.9 1.6 shard_map.135
  108.6 1.8 collective-permute-done.11.got_ref
  111.1 0.8 collective-permute-start.16
  112.0 4.8 %collective-permute-start.17 = (bf16[32,1792]{1,0:T(8,128)(2,1)}, bf16[32,1792]{1,0:T(8,128)(2,1)}, u32[]{:S(2)}, u32[]{:S(2)}) collective-permute-start(bf16[32,1792]{1,0:T(8,128)(2,1)} %get-tuple-element.82), channel_id=1, source_target_pairs={{0,4},{2,6},{4,0},{6,2},{1,5},{3,7},{5,1},{7,3},{8,12},{10,14},{12... | collective-permute-start | bytes 344072 | tf_op jit(solution)/shard_map/ppermute | solution.py:157
  116.8 5.2 %all-to-all-done.2 = bf16[16,64,512]{2,1,0:T(8,128)(2,1)} async-done(((bf16[16,64,512]{2,1,0:T(8,128)(2,1)}), bf16[16,64,512]{2,1,0:T(8,128)(2,1)}, u32[]{:S(2)}, u32[]{:S(2)}) %all-to-all-start.2) | async-done | bytes 1048608 | tf_op jit(solution)/shard_map/all_to_all | solution.py:272
  122.0 2.7 %shard_map.137 = (bf16[256,2048]{1,0:T(8,128)(2,1)S(1)}, bf16[256,896]{1,0:T(8,128)(2,1)S(1)}) custom-call(bf16[4,4,64,512]{3,2,1,0:T(8,128)(2,1)} %bitcast.12.rows_ref, bf16[1,2048]{1,0:T(2,128)(2,1)S(1)} %reshape.116.gain_ref, bf16[832,2048]{1,0:T(8,128)(2,1)S(1)} %bitcast.34, f32[8,128]{1,0:T(8,128)S(1)} %get-tuple-element.71.refs_0_), custom_call_target="tpu_custom_call" | custom-call | flops 1 | bytes 1 | tf_op jit(solution)/shard_map/pallas_call | solution.py:63
  124.7 1.3 shard_map.138
  126.6 1.4 shard_map.140.own_ref
  128.0 2.5 %collective-permute-start.21 = (bf16[32,832]{1,0:T(8,128)(2,1)S(1)}, bf16[32,832]{1,0:T(8,128)(2,1)S(1)}, u32[]{:S(2)}, u32[]{:S(2)}) collective-permute-start(bf16[32,832]{1,0:T(8,128)(2,1)S(1)} %shard_map.140.own_ref), channel_id=1, source_target_pairs={{0,6},{2,4},{4,2},{6,0},{1,7},{3,5},{5,3},{7,1},{8,14},{10,12},{12... | collective-permute-start | bytes 159752 | tf_op jit(solution)/shard_map/ppermute | solution.py:157
  130.6 1.5 collective-permute-start.19
  132.9 2.1 %collective-permute-done.21.three_ref = bf16[32,832]{1,0:T(8,128)(2,1)S(1)} collective-permute-done((bf16[32,832]{1,0:T(8,128)(2,1)S(1)}, bf16[32,832]{1,0:T(8,128)(2,1)S(1)}, u32[]{:S(2)}, u32[]{:S(2)}) %collective-permute-start.21) | collective-permute-done | bytes 53280 | tf_op jit(solution)/shard_map/ppermute | solution.py:157
  135.0 1.0 collective-permute-done.20.two_ref
  136.7 1.3 collective-permute-start.13
  138.0 1.3 collective-permute-start.14
  139.3 1.0 collective-permute-start.15
  140.3 1.3 shard_map.142
  141.6 1.0 copy-done.7
  142.6 6.4 %all-to-all-start.5 = ((bf16[16,16,2048]{2,1,0:T(8,128)(2,1)}), bf16[16,16,2048]{2,1,0:T(8,128)(2,1)}, u32[]{:S(2)}, u32[]{:S(2)}) async-start(bf16[16,16,2048]{2,1,0:T(8,128)(2,1)} %bitcast.38), calls=%async_computation.5 | async-start | bytes 2097152 | tf_op jit(solution)/shard_map/all_to_all | solution.py:272
  149.0 2.2 %collective-permute-done.15.three_ref = bf16[32,1792]{1,0:T(8,128)(2,1)} collective-permute-done((bf16[32,1792]{1,0:T(8,128)(2,1)}, bf16[32,1792]{1,0:T(8,128)(2,1)}, u32[]{:S(2)}, u32[]{:S(2)}) %collective-permute-start.15) | collective-permute-done | bytes 114720 | tf_op jit(solution)/shard_map/ppermute | solution.py:157
  151.2 1.2 shard_map.143.own_ref
  152.4 1.3 collective-permute-start.25
  153.7 1.3 collective-permute-start.24
  155.0 1.0 collective-permute-start.23
  156.0 2.2 %collective-permute-done.25.three_ref = bf16[32,832]{1,0:T(8,128)(2,1)S(1)} collective-permute-done((bf16[32,832]{1,0:T(8,128)(2,1)S(1)}, bf16[32,832]{1,0:T(8,128)(2,1)S(1)}, u32[]{:S(2)}, u32[]{:S(2)}) %collective-permute-start.25) | collective-permute-done | bytes 53280 | tf_op jit(solution)/shard_map/ppermute | solution.py:157
  158.2 0.8 collective-permute-done.24.two_ref
  159.6 1.5 collective-permute-done.26.other_ref
  161.0 1.7 shard_map.145
  162.8 1.0 copy-done.8
  163.7 3.0 %all-to-all-done.5.parts_ref = bf16[16,16,2048]{2,1,0:T(8,128)(2,1)} async-done(((bf16[16,16,2048]{2,1,0:T(8,128)(2,1)}), bf16[16,16,2048]{2,1,0:T(8,128)(2,1)}, u32[]{:S(2)}, u32[]{:S(2)}) %all-to-all-start.5) | async-done | bytes 1048608 | tf_op jit(solution)/shard_map/all_to_all | solution.py:272
  166.7 4.2 %all-to-all-start.4 = ((bf16[16,16,2048]{2,1,0:T(8,128)(2,1)}), bf16[16,16,2048]{2,1,0:T(8,128)(2,1)S(1)}, u32[]{:S(2)}, u32[]{:S(2)}) async-start(bf16[16,16,2048]{2,1,0:T(8,128)(2,1)} %bitcast.39), calls=%async_computation.4 | async-start | bytes 2097152 | tf_op jit(solution)/shard_map/all_to_all | solution.py:272
  170.9 1.4 shard_map.147
  172.3 6.0 %collective-permute-start.27 = (bf16[16,2048]{1,0:T(8,128)(2,1)S(1)}, bf16[16,2048]{1,0:T(8,128)(2,1)S(1)}, u32[]{:S(2)}, u32[]{:S(2)}) collective-permute-start(bf16[16,2048]{1,0:T(8,128)(2,1)S(1)} %shard_map.147), channel_id=1, source_target_pairs={{0,128},{128,0},{1,129},{129,1},{2,130},{130,2},{3,131},{131,3},{4... | collective-permute-start | bytes 196616 | tf_op jit(solution)/shard_map/ppermute | solution.py:45
  178.3 0.9 convert_bitcast_fusion
  179.2 9.5 %all-to-all-done.4.parts_ref = bf16[16,16,2048]{2,1,0:T(8,128)(2,1)S(1)} async-done(((bf16[16,16,2048]{2,1,0:T(8,128)(2,1)}), bf16[16,16,2048]{2,1,0:T(8,128)(2,1)S(1)}, u32[]{:S(2)}, u32[]{:S(2)}) %all-to-all-start.4) | async-done | bytes 1048608 | tf_op jit(solution)/shard_map/all_to_all | solution.py:272
  (73 shorter events, 10.2 us)
Async XLA Ops:
  0.0 58.4 %copy-start.6 = (bf16[1024,512]{1,0:T(8,128)(2,1)S(1)}, bf16[1024,512]{1,0:T(8,128)(2,1)}, u32[]{:S(2)}) copy-start(bf16[1024,512]{1,0:T(8,128)(2,1)} %weight_ref.3) | copy-start | bytes 3145732
  2.8 26.0 %all-to-all-start = ((bf16[32,2,1280]{2,1,0:T(2,128)(2,1)}), bf16[32,2,1280]{2,1,0:T(2,128)(2,1)S(1)}, u32[]{:S(2)}, u32[]{:S(2)}) async-start(bf16[32,2,1280]{2,1,0:T(2,128)(2,1)} %reshape.107), calls=%async_computation | async-start | bytes 327680 | tf_op jit(solution)/shard_map/all_to_all | solution.py:313
  15.8 0.8 copy-start.11
  16.7 12.2 %collective-permute-start = (bf16[16,512]{1,0:T(8,128)(2,1)S(1)}, bf16[16,512]{1,0:T(8,128)(2,1)S(1)}, u32[]{:S(2)}, u32[]{:S(2)}) collective-permute-start(bf16[16,512]{1,0:T(8,128)(2,1)S(1)} %get-tuple-element.50), channel_id=1, source_target_pairs={{0,8},{8,0},{16,24},{24,16},{1,9},{9,1},{17,25},{25,17},{2,10},{10... | collective-permute-start | bytes 49160 | tf_op jit(solution)/shard_map/ppermute | solution.py:335
  18.5 10.4 %collective-permute-start.1 = (bf16[16,512]{1,0:T(8,128)(2,1)S(1)}, bf16[16,512]{1,0:T(8,128)(2,1)S(1)}, u32[]{:S(2)}, u32[]{:S(2)}) collective-permute-start(bf16[16,512]{1,0:T(8,128)(2,1)S(1)} %get-tuple-element.51), channel_id=1, source_target_pairs={{0,16},{8,24},{16,0},{24,8},{1,17},{9,25},{17,1},{25,9},{2,18},{10... | collective-permute-start | bytes 49160 | tf_op jit(solution)/shard_map/ppermute | solution.py:335
  21.1 7.7 %collective-permute-start.2 = (bf16[16,512]{1,0:T(8,128)(2,1)S(1)}, bf16[16,512]{1,0:T(8,128)(2,1)S(1)}, u32[]{:S(2)}, u32[]{:S(2)}) collective-permute-start(bf16[16,512]{1,0:T(8,128)(2,1)S(1)} %get-tuple-element.52), channel_id=1, source_target_pairs={{0,24},{8,16},{16,8},{24,0},{1,25},{9,17},{17,9},{25,1},{2,26},{10... | collective-permute-start | bytes 49160 | tf_op jit(solution)/shard_map/ppermute | solution.py:335
  28.9 0.9 copy-start.9
  29.8 0.9 copy-start.10
  30.7 0.7 copy-start.12
  32.3 7.9 %collective-permute-start.3 = (bf16[16,1024]{1,0:T(8,128)(2,1)S(1)}, bf16[16,1024]{1,0:T(8,128)(2,1)S(1)}, u32[]{:S(2)}, u32[]{:S(2)}) collective-permute-start(bf16[16,1024]{1,0:T(8,128)(2,1)S(1)} %get-tuple-element.53.near_ref), channel_id=1, source_target_pairs={{0,128},{128,0},{1,129},{129,1},{2,130},{130,2},{3,131},{131,3},{4... | collective-permute-start | bytes 98312 | tf_op jit(solution)/shard_map/ppermute | solution.py:45
  59.5 1.6 collective-permute-start.4
  61.7 7.1 %collective-permute-start.5 = (bf16[64,512]{1,0:T(8,128)(2,1)S(1)}, bf16[64,512]{1,0:T(8,128)(2,1)S(1)}, u32[]{:S(2)}, u32[]{:S(2)}) collective-permute-start(bf16[64,512]{1,0:T(8,128)(2,1)S(1)} %get-tuple-element.63), channel_id=1, source_target_pairs={{0,2},{2,0},{4,6},{6,4},{1,3},{3,1},{5,7},{7,5},{8,10},{10,8},{12,... | collective-permute-start | bytes 196616 | tf_op jit(solution)/shard_map/ppermute | solution.py:157
  62.5 6.5 %collective-permute-start.6 = (bf16[64,512]{1,0:T(8,128)(2,1)S(1)}, bf16[64,512]{1,0:T(8,128)(2,1)S(1)}, u32[]{:S(2)}, u32[]{:S(2)}) collective-permute-start(bf16[64,512]{1,0:T(8,128)(2,1)S(1)} %get-tuple-element.64), channel_id=1, source_target_pairs={{0,4},{2,6},{4,0},{6,2},{1,5},{3,7},{5,1},{7,3},{8,12},{10,14},{12... | collective-permute-start | bytes 196616 | tf_op jit(solution)/shard_map/ppermute | solution.py:157
  64.2 8.1 %collective-permute-start.7 = (bf16[64,512]{1,0:T(8,128)(2,1)S(1)}, bf16[64,512]{1,0:T(8,128)(2,1)S(1)}, u32[]{:S(2)}, u32[]{:S(2)}) collective-permute-start(bf16[64,512]{1,0:T(8,128)(2,1)S(1)} %get-tuple-element.65), channel_id=1, source_target_pairs={{0,6},{2,4},{4,2},{6,0},{1,7},{3,5},{5,3},{7,1},{8,14},{10,12},{12... | collective-permute-start | bytes 196616 | tf_op jit(solution)/shard_map/ppermute | solution.py:157
  65.2 10.6 %collective-permute-start.10 = (bf16[32,1024]{1,0:T(8,128)(2,1)S(1)}, bf16[32,1024]{1,0:T(8,128)(2,1)S(1)}, u32[]{:S(2)}, u32[]{:S(2)}) collective-permute-start(bf16[32,1024]{1,0:T(8,128)(2,1)S(1)} %get-tuple-element.66.tok_ref), channel_id=1, source_target_pairs={{0,128},{128,0},{1,129},{129,1},{2,130},{130,2},{3,131},{131,3},{4... | collective-permute-start | bytes 196616 | tf_op jit(solution)/shard_map/ppermute | solution.py:45
  72.2 32.0 %copy-start.13 = (bf16[2048]{0:T(1024)(128)(2,1)S(1)}, bf16[2048]{0:T(1024)(128)(2,1)}, u32[]{:S(2)}) copy-start(bf16[2048]{0:T(1024)(128)(2,1)} %param.22) | copy-start | bytes 12292
  72.2 32.0 %copy-start = (bf16[2048,832]{0,1:T(8,128)(2,1)S(1)}, bf16[2048,832]{0,1:T(8,128)(2,1)}, u32[]{:S(2)}) copy-start(bf16[2048,832]{0,1:T(8,128)(2,1)} %param.23) | copy-start | bytes 10223620
  72.3 6.6 %collective-permute-start.9 = (bf16[64,512]{1,0:T(8,128)(2,1)S(1)}, bf16[64,512]{1,0:T(8,128)(2,1)S(1)}, u32[]{:S(2)}, u32[]{:S(2)}) collective-permute-start(bf16[64,512]{1,0:T(8,128)(2,1)S(1)} %add_convert_fusion.1), channel_id=1, source_target_pairs={{0,128},{1,0},{2,160},{3,32},{4,192},{5,64},{6,224},{7,96},{8,136}... | collective-permute-start | bytes 196616 | tf_op jit(solution)/shard_map/ppermute | solution.py:360
  79.0 1.0 copy-start.5
  80.0 19.9 %all-to-all-start.3 = ((bf16[16,64,512]{2,1,0:T(8,128)(2,1)}), bf16[16,64,512]{2,1,0:T(8,128)(2,1)}, u32[]{:S(2)}, u32[]{:S(2)}) async-start(bf16[16,64,512]{2,1,0:T(8,128)(2,1)} %copy-done.5), calls=%async_computation.3 | async-start | bytes 2097152 | tf_op jit(solution)/shard_map/all_to_all | solution.py:272
  84.3 10.2 %collective-permute-start.8 = (bf16[64,512]{1,0:T(8,128)(2,1)S(1)}, bf16[64,512]{1,0:T(8,128)(2,1)S(1)}, u32[]{:S(2)}, u32[]{:S(2)}) collective-permute-start(bf16[64,512]{1,0:T(8,128)(2,1)S(1)} %add_convert_fusion.1), channel_id=1, source_target_pairs={{0,0},{1,128},{2,32},{3,160},{4,64},{5,192},{6,96},{7,224},{8,8},{... | collective-permute-start | bytes 196616 | tf_op jit(solution)/shard_map/ppermute | solution.py:361
  94.6 1.0 copy-start.4
  99.8 22.1 %all-to-all-start.2 = ((bf16[16,64,512]{2,1,0:T(8,128)(2,1)}), bf16[16,64,512]{2,1,0:T(8,128)(2,1)}, u32[]{:S(2)}, u32[]{:S(2)}) async-start(bf16[16,64,512]{2,1,0:T(8,128)(2,1)} %copy-done.4), calls=%async_computation.2 | async-start | bytes 2097152 | tf_op jit(solution)/shard_map/all_to_all | solution.py:272
  104.2 2.7 %copy-start.1 = (bf16[2048,832]{0,1:T(8,128)(2,1)S(1)}, bf16[2048,832]{0,1:T(8,128)(2,1)}, u32[]{:S(2)}) copy-start(bf16[2048,832]{0,1:T(8,128)(2,1)} %param.24) | copy-start | bytes 10223620
  108.6 1.8 collective-permute-start.11
  111.1 15.0 %collective-permute-start.16 = (bf16[32,1792]{1,0:T(8,128)(2,1)}, bf16[32,1792]{1,0:T(8,128)(2,1)}, u32[]{:S(2)}, u32[]{:S(2)}) collective-permute-start(bf16[32,1792]{1,0:T(8,128)(2,1)} %get-tuple-element.81), channel_id=1, source_target_pairs={{0,2},{2,0},{4,6},{6,4},{1,3},{3,1},{5,7},{7,5},{8,10},{10,8},{12,... | collective-permute-start | bytes 344072 | tf_op jit(solution)/shard_map/ppermute | solution.py:157
  112.0 14.1 %collective-permute-start.17 = (bf16[32,1792]{1,0:T(8,128)(2,1)}, bf16[32,1792]{1,0:T(8,128)(2,1)}, u32[]{:S(2)}, u32[]{:S(2)}) collective-permute-start(bf16[32,1792]{1,0:T(8,128)(2,1)} %get-tuple-element.82), channel_id=1, source_target_pairs={{0,4},{2,6},{4,0},{6,2},{1,5},{3,7},{5,1},{7,3},{8,12},{10,14},{12... | collective-permute-start | bytes 344072 | tf_op jit(solution)/shard_map/ppermute | solution.py:157
  116.8 9.9 %collective-permute-start.18 = (bf16[32,1792]{1,0:T(8,128)(2,1)}, bf16[32,1792]{1,0:T(8,128)(2,1)}, u32[]{:S(2)}, u32[]{:S(2)}) collective-permute-start(bf16[32,1792]{1,0:T(8,128)(2,1)} %get-tuple-element.83), channel_id=1, source_target_pairs={{0,6},{2,4},{4,2},{6,0},{1,7},{3,5},{5,3},{7,1},{8,14},{10,12},{12... | collective-permute-start | bytes 344072 | tf_op jit(solution)/shard_map/ppermute | solution.py:157
  122.0 2.7 %copy-start.2 = (bf16[2048,832]{0,1:T(8,128)(2,1)S(1)}, bf16[2048,832]{0,1:T(8,128)(2,1)}, u32[]{:S(2)}) copy-start(bf16[2048,832]{0,1:T(8,128)(2,1)} %param.24) | copy-start | bytes 10223620
  126.0 6.1 %collective-permute-start.12 = (bf16[128,1792]{1,0:T(8,128)(2,1)S(1)}, bf16[128,1792]{1,0:T(8,128)(2,1)S(1)}, u32[]{:S(2)}, u32[]{:S(2)}) collective-permute-start(bf16[128,1792]{1,0:T(8,128)(2,1)S(1)} %get-tuple-element.75), channel_id=1, source_target_pairs={{0,1},{1,0},{2,3},{3,2},{4,5},{5,4},{6,7},{7,6},{8,9},{9,8},{10,11... | collective-permute-start | bytes 1376264 | tf_op jit(solution)/shard_map/ppermute | solution.py:45
  126.6 13.7 %copy-start.3 = (bf16[832,2048]{1,0:T(8,128)(2,1)S(1)}, bf16[832,2048]{1,0:T(8,128)(2,1)}, u32[]{:S(2)}) copy-start(bf16[832,2048]{1,0:T(8,128)(2,1)} %weight_ref.5) | copy-start | bytes 10223620
  128.0 7.0 %collective-permute-start.21 = (bf16[32,832]{1,0:T(8,128)(2,1)S(1)}, bf16[32,832]{1,0:T(8,128)(2,1)S(1)}, u32[]{:S(2)}, u32[]{:S(2)}) collective-permute-start(bf16[32,832]{1,0:T(8,128)(2,1)S(1)} %shard_map.140.own_ref), channel_id=1, source_target_pairs={{0,6},{2,4},{4,2},{6,0},{1,7},{3,5},{5,3},{7,1},{8,14},{10,12},{12... | collective-permute-start | bytes 159752 | tf_op jit(solution)/shard_map/ppermute | solution.py:157
  130.6 5.5 %collective-permute-start.20 = (bf16[32,832]{1,0:T(8,128)(2,1)S(1)}, bf16[32,832]{1,0:T(8,128)(2,1)S(1)}, u32[]{:S(2)}, u32[]{:S(2)}) collective-permute-start(bf16[32,832]{1,0:T(8,128)(2,1)S(1)} %shard_map.140.own_ref), channel_id=1, source_target_pairs={{0,4},{2,6},{4,0},{6,2},{1,5},{3,7},{5,1},{7,3},{8,12},{10,14},{12... | collective-permute-start | bytes 159752 | tf_op jit(solution)/shard_map/ppermute | solution.py:157
  130.6 6.0 %collective-permute-start.19 = (bf16[32,832]{1,0:T(8,128)(2,1)S(1)}, bf16[32,832]{1,0:T(8,128)(2,1)S(1)}, u32[]{:S(2)}, u32[]{:S(2)}) collective-permute-start(bf16[32,832]{1,0:T(8,128)(2,1)S(1)} %shard_map.140.own_ref), channel_id=1, source_target_pairs={{0,2},{2,0},{4,6},{6,4},{1,3},{3,1},{5,7},{7,5},{8,10},{10,8},{12,... | collective-permute-start | bytes 159752 | tf_op jit(solution)/shard_map/ppermute | solution.py:157
  136.6 3.7 %collective-permute-start.22 = (bf16[128,832]{1,0:T(8,128)(2,1)S(1)}, bf16[128,832]{1,0:T(8,128)(2,1)S(1)}, u32[]{:S(2)}, u32[]{:S(2)}) collective-permute-start(bf16[128,832]{1,0:T(8,128)(2,1)S(1)} %shard_map.141.own_ref), channel_id=1, source_target_pairs={{0,1},{1,0},{2,3},{3,2},{4,5},{5,4},{6,7},{7,6},{8,9},{9,8},{10,11... | collective-permute-start | bytes 638984 | tf_op jit(solution)/shard_map/ppermute | solution.py:45
  136.7 12.2 %collective-permute-start.13 = (bf16[32,1792]{1,0:T(8,128)(2,1)}, bf16[32,1792]{1,0:T(8,128)(2,1)}, u32[]{:S(2)}, u32[]{:S(2)}) collective-permute-start(bf16[32,1792]{1,0:T(8,128)(2,1)} %get-tuple-element.77), channel_id=1, source_target_pairs={{0,2},{2,0},{4,6},{6,4},{1,3},{3,1},{5,7},{7,5},{8,10},{10,8},{12,... | collective-permute-start | bytes 344072 | tf_op jit(solution)/shard_map/ppermute | solution.py:157
  138.0 11.0 %collective-permute-start.14 = (bf16[32,1792]{1,0:T(8,128)(2,1)}, bf16[32,1792]{1,0:T(8,128)(2,1)}, u32[]{:S(2)}, u32[]{:S(2)}) collective-permute-start(bf16[32,1792]{1,0:T(8,128)(2,1)} %get-tuple-element.78), channel_id=1, source_target_pairs={{0,4},{2,6},{4,0},{6,2},{1,5},{3,7},{5,1},{7,3},{8,12},{10,14},{12... | collective-permute-start | bytes 344072 | tf_op jit(solution)/shard_map/ppermute | solution.py:157
  139.3 11.9 %collective-permute-start.15 = (bf16[32,1792]{1,0:T(8,128)(2,1)}, bf16[32,1792]{1,0:T(8,128)(2,1)}, u32[]{:S(2)}, u32[]{:S(2)}) collective-permute-start(bf16[32,1792]{1,0:T(8,128)(2,1)} %get-tuple-element.79), channel_id=1, source_target_pairs={{0,6},{2,4},{4,2},{6,0},{1,7},{3,5},{5,3},{7,1},{8,14},{10,12},{12... | collective-permute-start | bytes 344072 | tf_op jit(solution)/shard_map/ppermute | solution.py:157
  141.6 1.0 copy-start.7
  142.6 24.1 %all-to-all-start.5 = ((bf16[16,16,2048]{2,1,0:T(8,128)(2,1)}), bf16[16,16,2048]{2,1,0:T(8,128)(2,1)}, u32[]{:S(2)}, u32[]{:S(2)}) async-start(bf16[16,16,2048]{2,1,0:T(8,128)(2,1)} %bitcast.38), calls=%async_computation.5 | async-start | bytes 2097152 | tf_op jit(solution)/shard_map/all_to_all | solution.py:272
  152.4 5.8 %collective-permute-start.25 = (bf16[32,832]{1,0:T(8,128)(2,1)S(1)}, bf16[32,832]{1,0:T(8,128)(2,1)S(1)}, u32[]{:S(2)}, u32[]{:S(2)}) collective-permute-start(bf16[32,832]{1,0:T(8,128)(2,1)S(1)} %shard_map.143.own_ref), channel_id=1, source_target_pairs={{0,6},{2,4},{4,2},{6,0},{1,7},{3,5},{5,3},{7,1},{8,14},{10,12},{12... | collective-permute-start | bytes 159752 | tf_op jit(solution)/shard_map/ppermute | solution.py:157
  153.7 5.4 %collective-permute-start.24 = (bf16[32,832]{1,0:T(8,128)(2,1)S(1)}, bf16[32,832]{1,0:T(8,128)(2,1)S(1)}, u32[]{:S(2)}, u32[]{:S(2)}) collective-permute-start(bf16[32,832]{1,0:T(8,128)(2,1)S(1)} %shard_map.143.own_ref), channel_id=1, source_target_pairs={{0,4},{2,6},{4,0},{6,2},{1,5},{3,7},{5,1},{7,3},{8,12},{10,14},{12... | collective-permute-start | bytes 159752 | tf_op jit(solution)/shard_map/ppermute | solution.py:157
  155.0 4.2 %collective-permute-start.23 = (bf16[32,832]{1,0:T(8,128)(2,1)S(1)}, bf16[32,832]{1,0:T(8,128)(2,1)S(1)}, u32[]{:S(2)}, u32[]{:S(2)}) collective-permute-start(bf16[32,832]{1,0:T(8,128)(2,1)S(1)} %shard_map.143.own_ref), channel_id=1, source_target_pairs={{0,2},{2,0},{4,6},{6,4},{1,3},{3,1},{5,7},{7,5},{8,10},{10,8},{12,... | collective-permute-start | bytes 159752 | tf_op jit(solution)/shard_map/ppermute | solution.py:157
  159.2 1.8 collective-permute-start.26
  162.8 1.0 copy-start.8
  166.7 22.0 %all-to-all-start.4 = ((bf16[16,16,2048]{2,1,0:T(8,128)(2,1)}), bf16[16,16,2048]{2,1,0:T(8,128)(2,1)S(1)}, u32[]{:S(2)}, u32[]{:S(2)}) async-start(bf16[16,16,2048]{2,1,0:T(8,128)(2,1)} %bitcast.39), calls=%async_computation.4 | async-start | bytes 2097152 | tf_op jit(solution)/shard_map/all_to_all | solution.py:272
  172.3 16.6 %collective-permute-start.27 = (bf16[16,2048]{1,0:T(8,128)(2,1)S(1)}, bf16[16,2048]{1,0:T(8,128)(2,1)S(1)}, u32[]{:S(2)}, u32[]{:S(2)}) collective-permute-start(bf16[16,2048]{1,0:T(8,128)(2,1)S(1)} %shard_map.147), channel_id=1, source_target_pairs={{0,128},{128,0},{1,129},{129,1},{2,130},{130,2},{3,131},{131,3},{4... | collective-permute-start | bytes 196616 | tf_op jit(solution)/shard_map/ppermute | solution.py:45
